TPU v7x, 32 devices: a whole 2x2x4 slice. The times are simulated.
32 devices in a mesh: replica: 4 (over y, core), shard: 8 (over z, x).
Axes of the slice: x: 2, y: 2, z: 4, core: 2. Of those that a mesh axis runs over, the one named last changes fastest.
Arguments:
- layer_input: bfloat16 [8192, 2048], P(('replica', 'shard')), may hold values from -6 to 6
- out_cotangent: bfloat16 [8192, 2048], P(('replica', 'shard')), may hold values from -6 to 6
- seq_lengths: int32 [4, 8, 2], P('replica'), may hold values from 1 to 192, 256 in all within a row
- seq_order: int32 [4, 16], P('replica'), may hold values from 0 to 15, each once within a row
- w_query: bfloat16 [2048, 2048], P('shard'), may hold values from -0.125 to 0.125
- w_key: bfloat16 [2048, 2048], P('shard'), may hold values from -0.125 to 0.125
- w_value: bfloat16 [2048, 2048], P('shard'), may hold values from -0.125 to 0.125
- w_beta: bfloat16 [2048, 16], P('shard'), may hold values from -0.125 to 0.125
- w_outgate: bfloat16 [2048, 2048], P('shard'), may hold values from -0.125 to 0.125
- w_output: bfloat16 [2048, 2048], P('shard'), may hold values from -0.125 to 0.125
- conv_query: bfloat16 [4, 2048], P(None, 'shard'), may hold values from -3 to 3
- conv_key: bfloat16 [4, 2048], P(None, 'shard'), may hold values from -3 to 3
- conv_value: bfloat16 [4, 2048], P(None, 'shard'), may hold values from -3 to 3
- attn_gain: bfloat16 [2048], P('shard'), may hold values from 0.5 to 1.5
- head_gain: bfloat16 [128], P('shard'), may hold values from 0.5 to 1.5
- mlp_gain: bfloat16 [2048], P('shard'), may hold values from 0.5 to 1.5
- w_gate: bfloat16 [2048, 5632], P('shard'), may hold values from -0.125 to 0.125
- w_up: bfloat16 [2048, 5632], P('shard'), may hold values from -0.125 to 0.125
- w_down: bfloat16 [5632, 2048], P('shard'), may hold values from -0.078125 to 0.078125
Outputs:
- layer_output: bfloat16 [8192, 2048], P(('replica', 'shard'))
- input_grad: bfloat16 [8192, 2048], P(('replica', 'shard'))
- g_query: float32 [2048, 2048], P('shard')
- g_key: float32 [2048, 2048], P('shard')
- g_value: float32 [2048, 2048], P('shard')
- g_beta: float32 [2048, 16], P('shard')
- g_outgate: float32 [2048, 2048], P('shard')
- g_output: float32 [2048, 2048], P('shard')
- g_conv_query: float32 [4, 2048], P(None, 'shard')
- g_conv_key: float32 [4, 2048], P(None, 'shard')
- g_conv_value: float32 [4, 2048], P(None, 'shard')
- g_attn_gain: float32 [2048], P('shard')
- g_head_gain: float32 [128], P('shard')
- g_mlp_gain: float32 [2048], P('shard')
- g_gate: float32 [2048, 5632], P('shard')
- g_up: float32 [2048, 5632], P('shard')
- g_down: float32 [5632, 2048], P('shard')
Inputs may be any that keep to these rules, and one draw needn't show every extreme that they name: `seq_lengths`: entry [g, d, k] is the length of slot d * 2 + k of group g; the 2 lengths of each [g, d] add up to 256, and the largest of them is at most 192. `seq_order`: row g lists, for the runs of group g's stream in order, the slot of each run's sequence; every slot once.
All inputs are finite; a program needn't handle non-finite values.
Results may differ from a plain program's by a relative error of at most 0.025.
Values may be sent and summed in bfloat16 or wider, within the bound.
A program may use at most 512 MiB of HBM per device.

v0:
```python
import jax
import jax.numpy as jnp
from jax import lax
from jax.sharding import PartitionSpec as P

H = 16
HD = 128
SPAN = 64
SEQ_DEV = 2


norm_eps = 1e-06
head_eps = 1e-05
unit_eps = 1e-06


def rms_scale(values, scales, epsilon):
    return values * lax.rsqrt(jnp.mean(values * values, axis=-1, keepdims=True) + epsilon) * scales


def plain_norm(values, scales):
    return rms_scale(values, scales, norm_eps)


def unit_rows(values):
    return values * lax.rsqrt(jnp.sum(values * values, axis=-1, keepdims=True) + unit_eps)


def causal_conv(signal, filters, positions):
    tap_count = filters.shape[0]
    row_count = signal.shape[0]
    padded = jnp.pad(signal, ((tap_count - 1, 0), (0, 0)))
    summed = signal * filters[0]
    for offset in range(1, tap_count):
        shifted = padded[tap_count - 1 - offset : tap_count - 1 - offset + row_count]
        summed = (
            summed
            + jnp.where(positions[:, None] >= offset, shifted, jnp.zeros_like(shifted))
            * filters[offset]
        )
    return summed


def span_step(carried, pieces):
    queries, key_rows, value_rows, strength, restart = pieces
    carried = jnp.where(restart, jnp.zeros_like(carried), carried)
    highest = lax.Precision.HIGHEST
    span_len = key_rows.shape[1]
    row_ids = lax.broadcasted_iota(jnp.int32, (span_len, span_len), 0)
    col_ids = lax.broadcasted_iota(jnp.int32, (span_len, span_len), 1)
    identity = jnp.eye(span_len, dtype=jnp.float32)
    key_inner = jnp.einsum("hid,hjd->hij", key_rows, key_rows, precision=highest)
    strict_low = jnp.where(row_ids > col_ids, -strength[:, :, None] * key_inner, 0.0)
    inverse = identity + strict_low
    powered = strict_low
    for doubling in range(span_len.bit_length() - 2):
        powered = jnp.einsum("hij,hjk->hik", powered, powered, precision=highest)
        inverse = jnp.einsum("hij,hjk->hik", inverse, identity + powered, precision=highest)
    mixed_keys = jnp.einsum(
        "hij,hjd->hid", inverse, strength[:, :, None] * key_rows, precision=highest
    )
    mixed_values = jnp.einsum(
        "hij,hjd->hid", inverse, strength[:, :, None] * value_rows, precision=highest
    )
    fresh_rows = mixed_values - jnp.einsum("hid,hde->hie", mixed_keys, carried, precision=highest)
    scores = jnp.where(
        row_ids >= col_ids, jnp.einsum("hid,hjd->hij", queries, key_rows, precision=highest), 0.0
    )
    head_scale = queries.shape[-1] ** (-0.5)
    outputs = (
        jnp.einsum("hid,hde->hie", queries, carried, precision=highest)
        + jnp.einsum("hij,hje->hie", scores, fresh_rows, precision=highest)
    ) * head_scale
    carried = carried + jnp.einsum("hid,hie->hde", key_rows, fresh_rows, precision=highest)
    return (carried, outputs)


def mixer(
    query_in, key_in, value_in, logit_in, query_taps, key_taps, value_taps, positions, restarts
):
    row_count = query_in.shape[0]
    blocks = row_count // SPAN

    def prepare(signal, filters):
        return jax.nn.silu(causal_conv(signal, filters, positions)).reshape(row_count, H, HD)

    def to_blocks(heads_in):
        return heads_in.reshape(blocks, SPAN, H, HD).transpose(0, 2, 1, 3)

    queries = unit_rows(prepare(query_in, query_taps))
    key_rows = unit_rows(prepare(key_in, key_taps))
    value_rows = prepare(value_in, value_taps)
    strength = jax.nn.sigmoid(logit_in).reshape(blocks, SPAN, H).transpose(0, 2, 1)
    initial = jnp.zeros((H, HD, HD), jnp.float32)
    carried_end, outputs = lax.scan(
        jax.checkpoint(span_step),
        initial,
        (to_blocks(queries), to_blocks(key_rows), to_blocks(value_rows), strength, restarts),
    )
    return outputs.transpose(0, 2, 1, 3).reshape(row_count, H * HD)


def gated_norm(mixed_rows, head_scale, gate_pre):
    row_count = mixed_rows.shape[0]
    head_normed = rms_scale(mixed_rows.reshape(row_count, H, HD), head_scale, head_eps).reshape(
        row_count, H * HD
    )
    return head_normed * jax.nn.silu(gate_pre)


def swiglu(gate_lin, up_lin):
    return jax.nn.silu(gate_lin) * up_lin


def project(left_side, right_side):
    return jnp.dot(left_side, right_side, preferred_element_type=jnp.float32)


def times_t(left_side, right_side):
    return lax.dot_general(
        left_side, right_side, (((1,), (1,)), ((), ())), preferred_element_type=jnp.float32
    )


def contract_rows(left_side, right_side):
    return lax.dot_general(
        left_side, right_side, (((0,), (0,)), ((), ())), preferred_element_type=jnp.float32
    )


def body(
    layer_input,
    out_cotangent,
    seq_lengths,
    seq_order,
    w_query,
    w_key,
    w_value,
    w_beta,
    w_outgate,
    w_output,
    conv_query,
    conv_key,
    conv_value,
    attn_gain,
    head_gain,
    mlp_gain,
    w_gate,
    w_up,
    w_down,
):
    shards = lax.axis_size("shard")
    shard_pos = lax.axis_index("shard")
    tok_dev = layer_input.shape[0]
    feat_width = layer_input.shape[1]
    ffn_width = w_gate.shape[1]
    lengths_grid = seq_lengths[0]
    order_row = seq_order[0]
    seq_total = order_row.shape[0]
    slot_rows = tok_dev // shards + SEQ_DEV
    packed_rows = (tok_dev // SPAN + SEQ_DEV - 1) * SPAN
    lengths_flat = lengths_grid.reshape(seq_total)
    slot_match = order_row[:, None] == lax.broadcasted_iota(jnp.int32, (seq_total, seq_total), 1)
    stream_len = jnp.sum(jnp.where(slot_match, lengths_flat[None, :], 0), axis=1)
    starts = jnp.cumsum(stream_len) - stream_len
    slot_start = jnp.sum(jnp.where(slot_match, starts[:, None], 0), axis=0)
    key_slots = lax.iota(jnp.int32, shards * slot_rows)
    stream_here = lax.iota(jnp.int32, tok_dev) * shards + shard_pos
    run_index = jnp.sum((starts[None, :] <= stream_here[:, None]).astype(jnp.int32), axis=1) - 1
    run_match = run_index[:, None] == lax.iota(jnp.int32, seq_total)[None, :]
    slot_here = jnp.sum(jnp.where(run_match, order_row[None, :], 0), axis=1)
    target = slot_here // SEQ_DEV
    target_hot = (target[:, None] == lax.iota(jnp.int32, shards)[None, :]).astype(jnp.int32)
    send_rank = jnp.sum(jnp.cumsum(target_hot, axis=0) * target_hot, axis=1) - 1
    send_key = target * slot_rows + send_rank
    send_match = send_key[None, :] == key_slots[:, None]
    send_row = jnp.sum(jnp.where(send_match, lax.iota(jnp.int32, tok_dev)[None, :], 0), axis=1)
    send_live = jnp.any(send_match, axis=1)
    my_length = lax.dynamic_slice_in_dim(lengths_grid, shard_pos, 1, 0)[0]
    my_start = lax.dynamic_slice_in_dim(slot_start, shard_pos * SEQ_DEV, SEQ_DEV)
    block_count = (my_length + SPAN - 1) // SPAN
    block_first = jnp.cumsum(block_count) - block_count
    row_ids = lax.iota(jnp.int32, packed_rows)
    seq_index = (
        jnp.sum((block_first[None, :] <= (row_ids // SPAN)[:, None]).astype(jnp.int32), axis=1) - 1
    )
    seq_hot = seq_index[:, None] == lax.iota(jnp.int32, SEQ_DEV)[None, :]

    def pick_seq(per_seq):
        return jnp.sum(jnp.where(seq_hot, per_seq[None, :], 0), axis=1)

    offset_in = row_ids - pick_seq(block_first) * SPAN
    filled = offset_in < pick_seq(my_length)
    positions = jnp.where(filled, offset_in, 0)
    own_start = pick_seq(my_start)
    stream_at = own_start + offset_in
    anchor = stream_at % shards

    def count_upto(bound):
        return (bound - anchor[:, None] + shards - 1) // shards

    earlier = my_start[None, :] < own_start[:, None]
    before = jnp.sum(
        jnp.where(
            earlier, count_upto((my_start + my_length)[None, :]) - count_upto(my_start[None, :]), 0
        ),
        axis=1,
    )
    recv_rank = before + count_upto(stream_at[:, None])[:, 0] - count_upto(own_start[:, None])[:, 0]
    recv_key = jnp.where(filled, anchor * slot_rows + recv_rank, 0)
    back_match = (recv_key[None, :] == key_slots[:, None]) & filled[None, :]
    back_row = jnp.sum(jnp.where(back_match, row_ids[None, :], 0), axis=1)
    back_live = jnp.any(back_match, axis=1)
    restarts = jnp.any(
        block_first[None, :] == lax.iota(jnp.int32, packed_rows // SPAN)[:, None], axis=1
    )

    def outbound(rows_in):
        picked = jnp.where(send_live[:, None], rows_in[send_row], jnp.zeros((), rows_in.dtype))
        return picked.reshape(shards, slot_rows, rows_in.shape[-1])

    def arrange(received):
        flat = received.reshape(shards * slot_rows, received.shape[-1])
        return jnp.where(filled[:, None], flat[recv_key], jnp.zeros((), received.dtype))

    def homeward(rows_in):
        picked = jnp.where(back_live[:, None], rows_in[back_row], jnp.zeros((), rows_in.dtype))
        return picked.reshape(shards, slot_rows, rows_in.shape[-1])

    def collect(received):
        return received.reshape(shards * slot_rows, received.shape[-1])[send_key]

    gathered = (
        lax.all_gather(w_query, "shard", axis=0, tiled=True),
        lax.all_gather(w_key, "shard", axis=0, tiled=True),
        lax.all_gather(w_value, "shard", axis=0, tiled=True),
        lax.all_gather(w_beta, "shard", axis=0, tiled=True),
        lax.all_gather(w_outgate, "shard", axis=0, tiled=True),
        lax.all_gather(w_output, "shard", axis=0, tiled=True),
        lax.all_gather(attn_gain, "shard", axis=0, tiled=True),
        lax.all_gather(head_gain, "shard", axis=0, tiled=True),
        lax.all_gather(conv_query, "shard", axis=1, tiled=True),
        lax.all_gather(conv_key, "shard", axis=1, tiled=True),
        lax.all_gather(conv_value, "shard", axis=1, tiled=True),
    )
    (
        full_query,
        full_key,
        full_value,
        full_beta,
        full_outgate,
        full_output,
        full_attn_gain,
        full_head_gain,
        taps_query,
        taps_key,
        taps_value,
    ) = gathered
    source = layer_input.astype(jnp.float32)
    normed_f, attn_norm_back = jax.vjp(plain_norm, source, full_attn_gain.astype(jnp.float32))
    normed = normed_f.astype(jnp.bfloat16)
    gate_pre = project(normed, full_outgate)
    normed_dst = arrange(
        lax.all_to_all(outbound(normed), "shard", split_axis=0, concat_axis=0, tiled=True)
    )
    query_dst = project(normed_dst, full_query).astype(jnp.bfloat16)
    key_dst = project(normed_dst, full_key).astype(jnp.bfloat16)
    value_dst = project(normed_dst, full_value).astype(jnp.bfloat16)
    logit_dst = project(normed_dst, full_beta).astype(jnp.bfloat16)

    def local_mixer(query_in, key_in, value_in, logit_in, query_taps, key_taps, value_taps):
        return mixer(
            query_in,
            key_in,
            value_in,
            logit_in,
            query_taps,
            key_taps,
            value_taps,
            positions,
            restarts,
        )

    mixed_f, mixer_back = jax.vjp(
        local_mixer,
        query_dst.astype(jnp.float32),
        key_dst.astype(jnp.float32),
        value_dst.astype(jnp.float32),
        logit_dst.astype(jnp.float32),
        taps_query.astype(jnp.float32),
        taps_key.astype(jnp.float32),
        taps_value.astype(jnp.float32),
    )
    mixed_src = collect(
        lax.all_to_all(
            homeward(mixed_f.astype(jnp.bfloat16)), "shard", split_axis=0, concat_axis=0, tiled=True
        )
    )
    zed_f, gated_back = jax.vjp(
        gated_norm, mixed_src.astype(jnp.float32), full_head_gain.astype(jnp.float32), gate_pre
    )
    zed_rows = zed_f.astype(jnp.bfloat16)
    hidden = source + project(zed_rows, full_output)
    full_gate, full_up, full_down, full_mlp_gain = (
        lax.all_gather(w_gate, "shard", axis=0, tiled=True),
        lax.all_gather(w_up, "shard", axis=0, tiled=True),
        lax.all_gather(w_down, "shard", axis=0, tiled=True),
        lax.all_gather(mlp_gain, "shard", axis=0, tiled=True),
    )
    mlp_f, mlp_norm_back = jax.vjp(plain_norm, hidden, full_mlp_gain.astype(jnp.float32))
    mlp_in = mlp_f.astype(jnp.bfloat16)
    gate_lin = project(mlp_in, full_gate)
    up_lin = project(mlp_in, full_up)
    product_f, swiglu_back = jax.vjp(swiglu, gate_lin, up_lin)
    product = product_f.astype(jnp.bfloat16)
    layer_output = (hidden + project(product, full_down)).astype(jnp.bfloat16)
    d_product = times_t(out_cotangent, full_down)
    d_gate_f, d_up_f = swiglu_back(d_product)
    d_gate = d_gate_f.astype(jnp.bfloat16)
    d_up = d_up_f.astype(jnp.bfloat16)
    d_mlp_in = times_t(d_gate, full_gate) + times_t(d_up, full_up)
    d_hidden_norm, g_mlp_part = mlp_norm_back(d_mlp_in)
    d_hidden = out_cotangent.astype(jnp.float32) + d_hidden_norm
    d_attn = d_hidden.astype(jnp.bfloat16)
    d_zed = times_t(d_attn, full_output)
    d_mixed_f, g_head_part, d_gate_pre_f = gated_back(d_zed)
    d_gate_pre = d_gate_pre_f.astype(jnp.bfloat16)
    d_mixed_dst = arrange(
        lax.all_to_all(
            outbound(d_mixed_f.astype(jnp.bfloat16)),
            "shard",
            split_axis=0,
            concat_axis=0,
            tiled=True,
        )
    )
    d_query_f, d_key_f, d_value_f, d_logit_f, g_taps_query, g_taps_key, g_taps_value = mixer_back(
        d_mixed_dst.astype(jnp.float32)
    )
    d_query = d_query_f.astype(jnp.bfloat16)
    d_key = d_key_f.astype(jnp.bfloat16)
    d_value = d_value_f.astype(jnp.bfloat16)
    d_logit = d_logit_f.astype(jnp.bfloat16)
    d_dest = (
        times_t(d_query, full_query)
        + times_t(d_key, full_key)
        + times_t(d_value, full_value)
        + times_t(d_logit, full_beta)
    )
    d_normed = collect(
        lax.all_to_all(homeward(d_dest), "shard", split_axis=0, concat_axis=0, tiled=True)
    )
    proj_grads = (d_query, d_key, d_value, d_logit)
    d_normed = d_normed + times_t(d_gate_pre, full_outgate)
    d_source_norm, g_attn_part = attn_norm_back(d_normed)
    input_grad = (d_hidden + d_source_norm).astype(jnp.bfloat16)
    qkv_right = jnp.concatenate([proj_grads[0], proj_grads[1], proj_grads[2]], axis=1)
    attn_grads = lax.psum_scatter(
        contract_rows(normed_dst, qkv_right).astype(jnp.bfloat16),
        "shard",
        scatter_dimension=0,
        tiled=True,
    ).astype(jnp.float32)
    gate_out_grads = lax.psum_scatter(
        jnp.concatenate(
            [contract_rows(normed, d_gate_pre), contract_rows(zed_rows, d_attn)], axis=1
        ).astype(jnp.bfloat16),
        "shard",
        scatter_dimension=0,
        tiled=True,
    ).astype(jnp.float32)
    d_gate_up = jnp.concatenate([d_gate, d_up], axis=1)
    gate_up_grads = lax.psum_scatter(
        contract_rows(mlp_in, d_gate_up).astype(jnp.bfloat16),
        "shard",
        scatter_dimension=0,
        tiled=True,
    ).astype(jnp.float32)
    down_grads = lax.psum_scatter(
        contract_rows(product, out_cotangent).astype(jnp.bfloat16),
        "shard",
        scatter_dimension=0,
        tiled=True,
    )
    beta_full = lax.dot_general(
        normed_dst, proj_grads[3], (((0,), (0,)), ((), ())), preferred_element_type=jnp.float32
    )
    small_sums = (
        lax.psum_scatter(
            beta_full.astype(jnp.bfloat16), "shard", scatter_dimension=0, tiled=True
        ).astype(jnp.float32),
        lax.psum_scatter(
            g_attn_part.astype(jnp.bfloat16), "shard", scatter_dimension=0, tiled=True
        ).astype(jnp.float32),
        lax.psum_scatter(
            g_head_part.astype(jnp.bfloat16), "shard", scatter_dimension=0, tiled=True
        ).astype(jnp.float32),
        lax.psum_scatter(
            g_mlp_part.astype(jnp.bfloat16), "shard", scatter_dimension=0, tiled=True
        ).astype(jnp.float32),
        lax.psum_scatter(
            g_taps_query.astype(jnp.bfloat16), "shard", scatter_dimension=1, tiled=True
        ).astype(jnp.float32),
        lax.psum_scatter(
            g_taps_key.astype(jnp.bfloat16), "shard", scatter_dimension=1, tiled=True
        ).astype(jnp.float32),
        lax.psum_scatter(
            g_taps_value.astype(jnp.bfloat16), "shard", scatter_dimension=1, tiled=True
        ).astype(jnp.float32),
    )
    summed = (
        lax.psum(attn_grads[:, :feat_width].astype(jnp.bfloat16), "replica").astype(jnp.float32),
        lax.psum(attn_grads[:, feat_width : 2 * feat_width].astype(jnp.bfloat16), "replica").astype(
            jnp.float32
        ),
        lax.psum(attn_grads[:, 2 * feat_width :].astype(jnp.bfloat16), "replica").astype(
            jnp.float32
        ),
        lax.psum(small_sums[0].astype(jnp.bfloat16), "replica").astype(jnp.float32),
        lax.psum(gate_out_grads[:, :feat_width].astype(jnp.bfloat16), "replica").astype(
            jnp.float32
        ),
        lax.psum(gate_out_grads[:, feat_width:].astype(jnp.bfloat16), "replica").astype(
            jnp.float32
        ),
        lax.psum(small_sums[4].astype(jnp.bfloat16), "replica").astype(jnp.float32),
        lax.psum(small_sums[5].astype(jnp.bfloat16), "replica").astype(jnp.float32),
        lax.psum(small_sums[6].astype(jnp.bfloat16), "replica").astype(jnp.float32),
        lax.psum(small_sums[1].astype(jnp.bfloat16), "replica").astype(jnp.float32),
        lax.psum(small_sums[2].astype(jnp.bfloat16), "replica").astype(jnp.float32),
        lax.psum(small_sums[3].astype(jnp.bfloat16), "replica").astype(jnp.float32),
        lax.psum(gate_up_grads[:, :ffn_width].astype(jnp.bfloat16), "replica").astype(jnp.float32),
        lax.psum(gate_up_grads[:, ffn_width:].astype(jnp.bfloat16), "replica").astype(jnp.float32),
        lax.psum(down_grads, "replica").astype(jnp.float32),
    )
    return (
        layer_output,
        input_grad,
        summed[0],
        summed[1],
        summed[2],
        summed[3],
        summed[4],
        summed[5],
        summed[6],
        summed[7],
        summed[8],
        summed[9],
        summed[10],
        summed[11],
        summed[12],
        summed[13],
        summed[14],
    )


def solution(mesh):
    in_specs = (
        P(("replica", "shard"), None),
        P(("replica", "shard"), None),
        P("replica", None, None),
        P("replica", None),
        P("shard", None),
        P("shard", None),
        P("shard", None),
        P("shard", None),
        P("shard", None),
        P("shard", None),
        P(None, "shard"),
        P(None, "shard"),
        P(None, "shard"),
        P("shard"),
        P("shard"),
        P("shard"),
        P("shard", None),
        P("shard", None),
        P("shard", None),
    )
    out_specs = (
        P(("replica", "shard"), None),
        P(("replica", "shard"), None),
        P("shard", None),
        P("shard", None),
        P("shard", None),
        P("shard", None),
        P("shard", None),
        P("shard", None),
        P(None, "shard"),
        P(None, "shard"),
        P(None, "shard"),
        P("shard"),
        P("shard"),
        P("shard"),
        P("shard", None),
        P("shard", None),
        P("shard", None),
    )
    return jax.shard_map(body, mesh=mesh, in_specs=in_specs, out_specs=out_specs, check_vma=False)
```

profile of v0, /device:TPU:0, one launch (start us, length us, event | category | flops | bytes accessed | tf_op | source)
XLA Modules:
  0.0 5098.0 jit_solution(10749298914543289635)
XLA Ops:
  13.6 22.4 all-gather
  49.5 68.6 %all_gather.50 = bf16[4,2048]{1,0:T(4,128)(2,1)S(1)} all-gather(bf16[4,256]{1,0:T(4,128)(2,1)S(1)} %copy-done.143), channel_id=1, replica_groups=mesh['replica'=4,'shard'=8] {'shard'}, dimensions={1}, use_global_device_ids=true | all-gather | bytes 18432 | tf_op jit(solution)/shard_map/all_gather | solution.py:244
  118.1 26.2 all_gather.52
  144.3 30.7 all_gather.48
  176.3 26.9 all_gather.47
  221.5 61.6 %all-gather.13.cloned.1.call-done = bf16[2048,2048]{1,0:T(8,128)(2,1)} async-done(((bf16[256,2048]{1,0:T(8,128)(2,1)}), bf16[2048,2048]{1,0:T(8,128)(2,1)}) %all-gather.13.cloned.1.call-update) | async-done | bytes 8388624 | tf_op jit(solution)/shard_map/all_gather | solution.py:236
  300.7 107.7 %all-gather.11.cloned.1.call-done = bf16[2048,2048]{1,0:T(8,128)(2,1)} async-done(((bf16[256,2048]{1,0:T(8,128)(2,1)}), bf16[2048,2048]{1,0:T(8,128)(2,1)}) %all-gather.11.cloned.1.call-update) | async-done | bytes 8388624 | tf_op jit(solution)/shard_map/all_gather | solution.py:235
  430.6 128.1 %while.42 = (s32[]{:T(128)}, f32[16,128,128]{2,1,0:T(8,128)S(1)}, bf16[5,16,64,128]{3,2,1,0:T(8,128)(2,1)}, f32[5,16,128,128]{3,2,1,0:T(8,128)}, pred[5]{0:T(512...) while((s32[]{:T(128)}, f32[16,128,128]{2,1,0:T(8,128)S(1)}, ...), condition=%wide.region_22.23_spmd.clone.clone, body=%wide.region_21.22_spmd.clone.clone.sunk | while | flops 1613964288 | bytes 23205524 | solution.py:95
  570.6 43.2 all-reduce.24
  613.8 39.6 all-gather.1
  687.1 432.3 %all-gather.21.cloned.1.call-done = bf16[2048,5632]{1,0:T(8,128)(2,1)} async-done(((bf16[256,5632]{1,0:T(8,128)(2,1)}), bf16[2048,5632]{1,0:T(8,128)(2,1)}) %all-gather.21.cloned.1.call-update) | async-done | bytes 23068688 | tf_op jit(solution)/shard_map/all_gather | solution.py:305
  1132.1 430.0 %all-gather.23.cloned.1.call-done = bf16[2048,5632]{1,0:T(8,128)(2,1)} async-done(((bf16[256,5632]{1,0:T(8,128)(2,1)}), bf16[2048,5632]{1,0:T(8,128)(2,1)}) %all-gather.23.cloned.1.call-update) | async-done | bytes 23068688 | tf_op jit(solution)/shard_map/all_gather | solution.py:306
  1575.0 429.8 %all-gather.25.cloned.1.call-done = bf16[5632,2048]{1,0:T(8,128)(2,1)} async-done(((bf16[704,2048]{1,0:T(8,128)(2,1)}), bf16[5632,2048]{1,0:T(8,128)(2,1)}) %all-gather.25.cloned.1.call-update) | async-done | bytes 23068688 | tf_op jit(solution)/shard_map/all_gather | solution.py:307
  2093.9 21.0 convolution_convert_fusion
  2115.1 43.4 all-to-all-done.2
  2172.0 391.3 %while.41 = (s32[]{:T(128)}, f32[16,128,128]{2,1,0:T(8,128)S(1)}, f32[5,16,64,128]{3,1,2,0:T(8,128)}, f32[5,16,64,128]{3,1,2,0:T(8,128)}, f32[5,16,64,128]{3,2,1...) while((s32[]{:T(128)}, f32[16,128,128]{2,1,0:T(8,128)S(1)}, ...), condition=%wide.region_32.33_spmd.clone, body=%wide.region_28.32_spmd.clone.sunk | while | flops 4335944704 | bytes 114103048 | solution.py:95
  2670.7 1087.6 %all-reduce.35.cloned.1.call-done = bf16[2048,11264]{1,0:T(8,128)(2,1)} async-done(((bf16[2048,11264]{1,0:T(8,128)(2,1)}), bf16[2048,11264]{1,0:T(8,128)(2,1)}) %all-reduce.35.cloned.1.call-update) | async-done | bytes 46137360
  3765.1 400.5 %reduce-scatter.14.cloned.1.call-done = bf16[256,6144]{1,0:T(8,128)(2,1)} async-done(((bf16[2048,6144]{1,0:T(8,128)(2,1)}), bf16[256,6144]{1,0:T(8,128)(2,1)}) %reduce-scatter.14.cloned.1.call-update) | async-done | bytes 3145744 | tf_op jit(solution)/shard_map/reduce_scatter | solution.py:358
  4169.3 373.2 %reduce-scatter.20.cloned.1.call-done = bf16[704,2048]{1,0:T(8,128)(2,1)} async-done(((bf16[5632,2048]{1,0:T(8,128)(2,1)}), bf16[704,2048]{1,0:T(8,128)(2,1)}) %reduce-scatter.20.cloned.1.call-update) | async-done | bytes 2883600 | tf_op jit(solution)/shard_map/reduce_scatter | solution.py:379
  4575.9 63.0 %reduce-scatter.26.cloned.1.call-done = bf16[256,4]{1,0:T(8,128)(2,1)} async-done(((bf16[2048,4]{1,0:T(8,128)(2,1)}), bf16[256,4]{1,0:T(8,128)(2,1)}) %reduce-scatter.26.cloned.1.call-update) | async-done | bytes 2064
  4639.8 63.1 %reduce-scatter.24.cloned.1.call-done = bf16[256,4]{1,0:T(8,128)(2,1)} async-done(((bf16[2048,4]{1,0:T(8,128)(2,1)}), bf16[256,4]{1,0:T(8,128)(2,1)}) %reduce-scatter.24.cloned.1.call-update) | async-done | bytes 2064
  4703.8 63.6 %reduce-scatter.22.cloned.1.call-done = bf16[256,4]{1,0:T(8,128)(2,1)} async-done(((bf16[2048,4]{1,0:T(8,128)(2,1)}), bf16[256,4]{1,0:T(8,128)(2,1)}) %reduce-scatter.22.cloned.1.call-update) | async-done | bytes 2064
  4802.0 21.2 reduce-scatter.16.cloned.1.call-done
  4840.6 230.8 %all-reduce.37.cloned.1.call-done = (bf16[256,2048]{0,1:T(8,128)(2,1)}, bf16[256,2048]{0,1:T(8,128)(2,1)}, bf16[256,2048]{1,0:T(8,128)(2,1)}, bf16[256,2048]{1,0...) async-done(((bf16[256,2048]{0,1:T(8,128)(2,1)}, bf16[256,2048]{0,1:T(8,128)(2,1)}, ...) | async-done | bytes 13893648 | tf_op jit(solution)/shard_map/psum | solution.py:420
  (1193 shorter events, 979.7 us)
Async XLA Ops:
  7.2 206.0 %all-gather.15.cloned.1.call-start = ((), (), s32[]{:S(2)}) async-start(), calls=%async_computation.13 | async-start | bytes 9437184 | tf_op jit(solution)/shard_map/all_gather | solution.py:234
  7.9 275.3 %all-gather.13.cloned.1.call-start = ((), (), s32[]{:S(2)}) async-start(), calls=%async_computation.12 | async-start | bytes 9437184 | tf_op jit(solution)/shard_map/all_gather | solution.py:236
  8.7 399.8 %all-gather.11.cloned.1.call-start = ((), (), s32[]{:S(2)}) async-start(), calls=%async_computation.11 | async-start | bytes 9437184 | tf_op jit(solution)/shard_map/all_gather | solution.py:235
  9.4 648.3 %all-gather.17.cloned.1.call-start = ((), (), s32[]{:S(2)}) async-start(), calls=%async_computation.14 | async-start | bytes 9437184 | tf_op jit(solution)/shard_map/all_gather | solution.py:238
  10.0 668.2 %all-gather.19.cloned.1.call-start = ((), (), s32[]{:S(2)}) async-start(), calls=%async_computation.15 | async-start | bytes 9437184 | tf_op jit(solution)/shard_map/all_gather | solution.py:239
  10.6 1108.9 %all-gather.21.cloned.1.call-start = ((), (), s32[]{:S(2)}) async-start(), calls=%async_computation.16 | async-start | bytes 25952256 | tf_op jit(solution)/shard_map/all_gather | solution.py:305
  11.2 1550.9 %all-gather.23.cloned.1.call-start = ((), (), s32[]{:S(2)}) async-start(), calls=%async_computation.17 | async-start | bytes 25952256 | tf_op jit(solution)/shard_map/all_gather | solution.py:306
  42.9 163.1 %all-to-all-start = ((bf16[8,34,2048]{2,1,0:T(8,128)(2,1)}), bf16[8,34,2048]{2,1,0:T(8,128)(2,1)}, u32[]{:S(2)}, u32[]{:S(2)}) async-start(bf16[8,34,2048]{2,1,0:T(8,128)(2,1)} %broadcast_select_fusion.4), calls=%async_computation | async-start | bytes 2621440 | tf_op jit(solution)/shard_map/all_to_all | solution.py:264
  47.4 1957.4 %all-gather.25.cloned.1.call-start = ((), (), s32[]{:S(2)}) async-start(), calls=%async_computation.18 | async-start | bytes 25952256 | tf_op jit(solution)/shard_map/all_gather | solution.py:307
  48.9 157.2 %copy-start.111 = (s32[320]{0:T(512)}, s32[320]{0:T(512)S(1)}, u32[]{:S(2)}) copy-start(s32[320]{0:T(512)S(1)} %get-tuple-element.960) | copy-start | bytes 3844
  49.0 234.1 %copy-start.134 = (pred[320]{0:T(512)(128)(4,1)}, pred[320]{0:T(512)(128)(4,1)S(1)}, u32[]{:S(2)}) copy-start(pred[320]{0:T(512)(128)(4,1)S(1)} %get-tuple-element.906) | copy-start | bytes 964
  49.5 161.1 %copy-start.113 = (s32[1024]{0:T(1024)}, s32[1024]{0:T(1024)S(1)}, u32[]{:S(2)}) copy-start(s32[1024]{0:T(1024)S(1)} %pad_clamp_fusion.2) | copy-start | bytes 12292
  565.5 88.1 %all-to-all-start.1 = ((bf16[8,34,2048]{2,1,0:T(8,128)(2,1)}), bf16[8,34,2048]{2,1,0:T(8,128)(2,1)S(1)}, u32[]{:S(2)}, u32[]{:S(2)}) async-start(bf16[8,34,2048]{2,1,0:T(8,128)(2,1)} %broadcast_select_fusion.5), calls=%async_computation.1 | async-start | bytes 2621440 | tf_op jit(solution)/shard_map/all_to_all | solution.py:295
  569.1 2098.6 %reduce-scatter.18.cloned.1.call-start = ((), (), s32[]{:S(2)}) async-start(), calls=%async_computation.21 | async-start | bytes 18874368 | tf_op jit(solution)/shard_map/reduce_scatter | solution.py:364
  2089.2 69.3 %all-to-all-start.2 = ((bf16[8,34,2048]{2,1,0:T(8,128)(2,1)}), bf16[8,34,2048]{2,1,0:T(8,128)(2,1)}, u32[]{:S(2)}, u32[]{:S(2)}) async-start(bf16[8,34,2048]{2,1,0:T(8,128)(2,1)} %broadcast_select_fusion.3), calls=%async_computation.2 | async-start | bytes 2621440 | tf_op jit(solution)/shard_map/all_to_all | solution.py:329
  2093.9 1664.5 %all-reduce.35.cloned.1.call-start = ((), (), s32[]{:S(2)}) async-start(), calls=%async_computation.26 | async-start | bytes 92274688
  2115.0 2050.6 %reduce-scatter.14.cloned.1.call-start = ((), (), s32[]{:S(2)}) async-start(), calls=%async_computation.19 | async-start | bytes 28311552 | tf_op jit(solution)/shard_map/reduce_scatter | solution.py:358
  2634.1 1908.4 %reduce-scatter.20.cloned.1.call-start = ((), (), s32[]{:S(2)}) async-start(), calls=%async_computation.22 | async-start | bytes 25952256 | tf_op jit(solution)/shard_map/reduce_scatter | solution.py:379
  2648.5 1990.4 %reduce-scatter.26.cloned.1.call-start = ((), (), s32[]{:S(2)}) async-start(), calls=%async_computation.25 | async-start | bytes 589824
  2650.6 2052.4 %reduce-scatter.24.cloned.1.call-start = ((), (), s32[]{:S(2)}) async-start(), calls=%async_computation.24 | async-start | bytes 589824
  2651.7 2115.8 %reduce-scatter.22.cloned.1.call-start = ((), (), s32[]{:S(2)}) async-start(), calls=%async_computation.23 | async-start | bytes 589824
  2652.9 2170.3 %reduce-scatter.16.cloned.1.call-start = ((), (), s32[]{:S(2)}) async-start(), calls=%async_computation.20 | async-start | bytes 73728 | tf_op jit(solution)/shard_map/reduce_scatter | solution.py:389
  2654.0 2417.4 %all-reduce.37.cloned.1.call-start = ((), (), s32[]{:S(2)}) async-start(), calls=%async_computation.27 | async-start | bytes 27787264 | tf_op jit(solution)/shard_map/psum | solution.py:420
  4558.1 210.3 %all-to-all-start.3 = ((f32[8,34,2048]{2,1,0:T(8,128)}), f32[8,34,2048]{2,1,0:T(8,128)}, u32[]{:S(2)}, u32[]{:S(2)}) async-start(f32[8,34,2048]{2,1,0:T(8,128)} %broadcast_select_fusion.1), calls=%async_computation.3 | async-start | bytes 5242880 | tf_op jit(solution)/shard_map/all_to_all | solution.py:351
  (230 other events, 3550.9 us)
Sparse Core Ops, SparseCore 0:
  10.1 146.2 all-gather.14
  158.5 124.5 all-gather.12
  285.3 123.0 all-gather.10
  410.4 123.0 all-gather.16
  535.5 142.5 all-gather.18
  679.6 439.8 all-gather.20
  1121.0 441.0 all-gather.22
  1563.6 441.0 all-gather.24
  2081.3 311.9 reduce-scatter.17
  2398.1 1360.2 all-reduce.34
  3762.8 402.8 reduce-scatter.13
  4169.8 372.6 reduce-scatter.19
  4546.2 92.5 reduce-scatter.25
  4642.1 60.8 reduce-scatter.23
  4706.5 60.9 reduce-scatter.21
  4770.5 52.7 reduce-scatter.15
  4828.0 243.3 all-reduce.36
where the time goes:
time: 5110 us; the launch traced here: 5100 us
  waiting for transfers between devices  3820 us (75%)
  matrix products  635 us (12%)
  blocking collectives  288 us (6%)
  local copies, waits for them, and re-layouts  184 us (4%)
  other arithmetic  118 us (2%)
    unnamed x21, waiting for transfers between devices  1280 us
    all_gather x1, waiting for transfers between devices, body(): lax.all_gather(w_gate, 'shard', axis=0, tiled=True)  432 us
    all_gather x1, waiting for transfers between devices, body(): lax.all_gather(w_up, 'shard', axis=0, tiled=True)  430 us
    all_gather x1, waiting for transfers between devices, body(): lax.all_gather(w_down, 'shard', axis=0, tiled=True)  430 us
    reduce_scatter x1, waiting for transfers between devices, body(): lax.psum_scatter(contract_rows(normed_dst, qkv_right).astype(jnp.bfloat16...  401 us
    reduce_scatter x1, waiting for transfers between devices, body(): lax.psum_scatter(contract_rows(product, out_cotangent).astype(jnp.bfloat1...  373 us
    psum x1, waiting for transfers between devices, body(): lax.psum(gate_out_grads[:, :feat_width].astype(jnp.bfloat16), 'replica')  231 us
    all_gather x1, waiting for transfers between devices, body(): lax.all_gather(w_key, 'shard', axis=0, tiled=True)  108 us
  transfers between devices with their start and end apart: 21, of which 15 were waited for; matrix products, arithmetic and copies ran while one was open for 16% of the time, Pallas kernels for 0%

commit v1 on v0

v1 whole, which is shorter than its diff:
```python
import functools

import jax
import jax.numpy as jnp
from jax import lax
from jax.experimental import pallas as pl
from jax.experimental.pallas import tpu as pltpu
from jax.sharding import PartitionSpec as P

MESH = pl.DeviceIdType.MESH


def grid_of(axis):
    count = lax.axis_size(axis)
    if axis == "replica":
        across = 2 if count % 2 == 0 else 1
        return count // across, across
    depth = 4 if count % 4 == 0 else count
    return depth, count // depth


def line_neighbours(z, x, Z, X):
    return ((z + 1) * X + x, (z - 1) * X + x, z * X + x + 1, z * X + x - 1), (
        z < Z - 1,
        z > 0,
        x < X - 1,
        x > 0,
    )


def greet(axis, targets, exists):
    barrier = pltpu.get_barrier_semaphore()
    count = jnp.int32(0)
    for target, there in zip(targets, exists):

        @pl.when(there)
        def _(target=target):
            pl.semaphore_signal(
                barrier, inc=1, device_id={axis: target}, device_id_type=MESH
            )

        count = count + jnp.where(there, 1, 0)
    pl.semaphore_wait(barrier, count)


def gather_kernel(axis, Z, X, NC, x_ref, out_ref, own_sem, send_sem, recv_sem):
    me = lax.axis_index(axis)
    z, x = lax.div(me, X), lax.rem(me, X)
    rows = x_ref.shape[0] // NC
    targets, exists = line_neighbours(z, x, Z, X)
    own = pltpu.make_async_copy(x_ref, out_ref.at[me], own_sem)
    own.start()
    greet(axis, targets, exists)

    def copy(way, origin, c):
        part = pl.ds(c * rows, rows)
        return pltpu.make_async_remote_copy(
            src_ref=out_ref.at[origin, part],
            dst_ref=out_ref.at[origin, part],
            send_sem=send_sem.at[way, origin, c],
            recv_sem=recv_sem.at[origin, c],
            device_id={axis: targets[way]},
            device_id_type=MESH,
        )

    for c in range(NC):
        for way in range(4):

            @pl.when(exists[way])
            def _(way=way, c=c):
                part = pl.ds(c * rows, rows)
                pltpu.make_async_remote_copy(
                    src_ref=x_ref.at[part],
                    dst_ref=out_ref.at[me, part],
                    send_sem=send_sem.at[way, me, c],
                    recv_sem=recv_sem.at[me, c],
                    device_id={axis: targets[way]},
                    device_id_type=MESH,
                ).start()

    for d in range(1, Z):
        for c in range(NC):
            for way, here in ((0, z - d >= 0), (1, z + d < Z)):

                @pl.when(here)
                def _(way=way, c=c, d=d):
                    origin = (z - d if way == 0 else z + d) * X + x
                    copy(way, origin, c).wait_recv()
                    for onward in (way, 2, 3):

                        @pl.when(exists[onward])
                        def _(onward=onward):
                            copy(onward, origin, c).start()

    for e in range(1, X):
        for dz in range(Z):
            level = lax.rem(z + dz, Z)
            for c in range(NC):
                for way, here in ((2, x - e >= 0), (3, x + e < X)):

                    @pl.when(here)
                    def _(way=way, c=c, e=e, level=level):
                        origin = level * X + (x - e if way == 2 else x + e)
                        copy(way, origin, c).wait_recv()

                        @pl.when(exists[way])
                        def _():
                            copy(way, origin, c).start()

    own.wait()
    for c in range(NC):
        for zz in range(Z):
            for way, here in ((0, zz <= z), (1, zz >= z)):

                @pl.when(exists[way] & here)
                def _(way=way, zz=zz, c=c):
                    copy(way, zz * X + x, c).wait_send()

            for xx in range(X):
                for way, here in ((2, xx <= x), (3, xx >= x)):

                    @pl.when(exists[way] & here)
                    def _(way=way, zz=zz, xx=xx, c=c):
                        copy(way, zz * X + xx, c).wait_send()


def gather_rows(block, axis, ident, chunks=4):
    Z, X = grid_of(axis)
    shards = Z * X
    rows, width = block.shape
    return pl.pallas_call(
        functools.partial(gather_kernel, axis, Z, X, chunks),
        out_shape=jax.ShapeDtypeStruct((shards, rows, width), block.dtype),
        in_specs=[pl.BlockSpec(memory_space=pl.ANY)],
        out_specs=pl.BlockSpec(memory_space=pl.ANY),
        scratch_shapes=[
            pltpu.SemaphoreType.DMA,
            pltpu.SemaphoreType.DMA((4, shards, chunks)),
            pltpu.SemaphoreType.DMA((shards, chunks)),
        ],
        compiler_params=pltpu.CompilerParams(
            collective_id=ident, has_side_effects=True
        ),
    )(block)


def scatter_kernel(axis, Z, X, NC, p_ref, out_ref, mine, from_x, from_z, load_sem, xs_sem, xr_sem, zs_sem, zr_sem):
    me = lax.axis_index(axis)
    z, x = lax.div(me, X), lax.rem(me, X)
    rows = p_ref.shape[1] // NC
    step = 16
    targets, exists = line_neighbours(z, x, Z, X)

    def load(slot):
        return pltpu.make_async_copy(p_ref.at[slot], mine.at[slot], load_sem.at[slot])

    for slot in range(Z * X):
        load(slot).start()
    greet(axis, targets, exists)

    def x_copy(up, zz, xx, c):
        part = pl.ds(c * rows, rows)
        spot = xx if up else jnp.where(xx == x - 1, X, xx)
        spot = zz * (X + 1) + spot
        return pltpu.make_async_remote_copy(
            src_ref=mine.at[zz * X + xx, part],
            dst_ref=from_x.at[spot, part],
            send_sem=xs_sem.at[zz * X + xx, c],
            recv_sem=xr_sem.at[spot, c],
            device_id={axis: targets[2 if up else 3]},
            device_id_type=MESH,
        )

    def z_copy(up, zz, c):
        part = pl.ds(c * rows, rows)
        spot = zz if up else jnp.where(zz == z - 1, Z, zz)
        return pltpu.make_async_remote_copy(
            src_ref=mine.at[zz * X + x, part],
            dst_ref=from_z.at[spot, part],
            send_sem=zs_sem.at[zz, c],
            recv_sem=zr_sem.at[spot, c],
            device_id={axis: targets[0 if up else 1]},
            device_id_type=MESH,
        )

    def wait_in(buffer, sem, spot, c):
        part = pl.ds(c * rows, rows)
        pltpu.make_async_copy(buffer.at[spot, part], buffer.at[spot, part], sem.at[spot, c]).wait()

    def add_in(slot, buffer, spot, c):
        def body(i, carry):
            part = pl.ds(pl.multiple_of(c * rows + i * step, step), step)
            mine[slot, part] = (
                mine[slot, part].astype(jnp.float32) + buffer[spot, part].astype(jnp.float32)
            ).astype(mine.dtype)
            return carry

        lax.fori_loop(0, rows // step, body, 0)

    def x_line(zz):
        for k in range(X - 1):
            for up, xx, here in ((True, X - 1 - k, X - 1 - k > x), (False, k, k < x)):

                @pl.when(here)
                def _(up=up, xx=xx):
                    load(zz * X + xx).wait()
                    for c in range(NC):

                        @pl.when(exists[3 if up else 2])
                        def _(c=c):
                            spot = zz * (X + 1) + xx
                            wait_in(from_x, xr_sem, spot, c)
                            add_in(zz * X + xx, from_x, spot, c)

                        x_copy(up, zz, xx, c).start()

    def x_join(zz, c):
        if X == 1:
            return
        slot = zz * X + x

        @pl.when(x > 0)
        def _():
            wait_in(from_x, xr_sem, zz * (X + 1) + x, c)
            add_in(slot, from_x, zz * (X + 1) + x, c)

        @pl.when(x < X - 1)
        def _():
            wait_in(from_x, xr_sem, zz * (X + 1) + X, c)
            add_in(slot, from_x, zz * (X + 1) + X, c)

    def in_order(visit):
        for k in range(Z - 1):
            for up, zz, here in ((True, Z - 1 - k, Z - 1 - k > z), (False, k, k < z)):

                @pl.when(here)
                def _(up=up, zz=zz):
                    visit(up, zz)

    in_order(lambda up, zz: x_line(zz))
    x_line(z)

    for k in range(Z - 1):
        for up, zz, here in ((True, Z - 1 - k, Z - 1 - k > z), (False, k, k < z)):

            @pl.when(here)
            def _(up=up, zz=zz):
                load(zz * X + x).wait()

        for c in range(NC):
            for up, zz, here in ((True, Z - 1 - k, Z - 1 - k > z), (False, k, k < z)):

                @pl.when(here)
                def _(up=up, zz=zz, c=c):
                    x_join(zz, c)

                    @pl.when(exists[1 if up else 0])
                    def _():
                        wait_in(from_z, zr_sem, zz, c)
                        add_in(zz * X + x, from_z, zz, c)

                    z_copy(up, zz, c).start()

    load(me).wait()
    for c in range(NC):
        x_join(z, c)

        @pl.when(z > 0)
        def _(c=c):
            wait_in(from_z, zr_sem, z, c)

        @pl.when(z < Z - 1)
        def _(c=c):
            wait_in(from_z, zr_sem, Z, c)

        def body(i, carry, c=c):
            part = pl.ds(pl.multiple_of(c * rows + i * step, step), step)
            total = mine[me, part].astype(jnp.float32)
            below = from_z[z, part].astype(jnp.float32)
            above = from_z[Z, part].astype(jnp.float32)
            total = total + jnp.where(z > 0, below, 0.0)
            total = total + jnp.where(z < Z - 1, above, 0.0)
            out_ref[part] = total.astype(out_ref.dtype)
            return carry

        lax.fori_loop(0, rows // step, body, 0)

    for zz in range(Z):
        for c in range(NC):
            for xx in range(X):

                @pl.when(xx != x)
                def _(zz=zz, xx=xx, c=c):
                    x_copy(True, zz, xx, c).wait_send()

            @pl.when(zz != z)
            def _(zz=zz, c=c):
                z_copy(True, zz, c).wait_send()


def scatter_rows(partial, axis, ident, chunks=4, dtype=jnp.float32):
    Z, X = grid_of(axis)
    shards = Z * X
    rows, width = partial.shape[0] // shards, partial.shape[1]
    kind = partial.dtype
    return pl.pallas_call(
        functools.partial(scatter_kernel, axis, Z, X, chunks),
        out_shape=jax.ShapeDtypeStruct((rows, width), dtype),
        in_specs=[pl.BlockSpec(memory_space=pl.ANY)],
        out_specs=pl.BlockSpec(memory_space=pltpu.VMEM),
        scratch_shapes=[
            pltpu.VMEM((shards, rows, width), kind),
            pltpu.VMEM((Z * (X + 1), rows, width), kind),
            pltpu.VMEM((Z + 1, rows, width), kind),
            pltpu.SemaphoreType.DMA((shards,)),
            pltpu.SemaphoreType.DMA((shards, chunks)),
            pltpu.SemaphoreType.DMA((Z * (X + 1), chunks)),
            pltpu.SemaphoreType.DMA((Z, chunks)),
            pltpu.SemaphoreType.DMA((Z + 1, chunks)),
        ],
        compiler_params=pltpu.CompilerParams(
            collective_id=ident, has_side_effects=True, vmem_limit_bytes=60 * 1024 * 1024
        ),
    )(partial.reshape(shards, rows, width))


HD = 128


def dot_nn(a, b):
    return lax.dot_general(
        a.astype(jnp.bfloat16), b.astype(jnp.bfloat16), (((1,), (0,)), ((), ())),
        preferred_element_type=jnp.float32,
    )


def dot_nt(a, b):
    return lax.dot_general(
        a.astype(jnp.bfloat16), b.astype(jnp.bfloat16), (((1,), (1,)), ((), ())),
        preferred_element_type=jnp.float32,
    )


def dot_tn(a, b):
    return lax.dot_general(
        a.astype(jnp.bfloat16), b.astype(jnp.bfloat16), (((0,), (0,)), ((), ())),
        preferred_element_type=jnp.float32,
    )


def split2(a):
    high = a.astype(jnp.bfloat16)
    return high, (a - high.astype(jnp.float32)).astype(jnp.bfloat16)


def fine(dot, a, b):
    a_high, a_low = split2(a)
    b_high, b_low = split2(b)
    return dot(a_high, b_high) + (dot(a_high, b_low) + dot(a_low, b_high))


def time_of(shape, dim, lanes):
    index = lax.broadcasted_iota(jnp.int32, shape, dim)
    return lax.rem(index, 8) * lanes + lax.div(index, 8)


def lower_inverse(a, lanes):
    size = a.shape[0]
    row_t = time_of((size, size), 0, lanes)
    col_t = time_of((size, size), 1, lanes)
    eye = jnp.where(row_t == col_t, 1.0, 0.0)

    def same(width):
        return lax.div(row_t, width) == lax.div(col_t, width)

    first = jnp.where(same(8), a, 0.0)
    second = fine(dot_nn, first, first)
    inverse = eye + first + second + fine(dot_nn, first, second)
    inverse = inverse + fine(dot_nn, inverse, fine(dot_nn, second, second))
    width = 16
    while width <= size:
        joint = jnp.where(same(width) & jnp.logical_not(same(width // 2)), a, 0.0)
        inverse = inverse + fine(dot_nn, fine(dot_nn, inverse, joint), inverse)
        width *= 2
    return inverse


def delta_forward(lanes, heads, group, q_ref, k_ref, v_ref, b_ref, low_ref, c_ref, m_ref,
                  o_ref, s_ref, t_ref, mk_ref, mv_ref, u_ref, state):
    size = lanes * 8
    scale = HD ** (-0.5)

    @pl.when(pl.program_id(0) == 0)
    def _():
        state[...] = jnp.zeros_like(state)

    row_t = time_of((size, size), 0, lanes)
    col_t = time_of((size, size), 1, lanes)
    ready = {}
    for g in range(group):
        rows = pl.ds(g * 8, 8)
        low = low_ref[g]
        strict = jnp.where(row_t == col_t, 0.0, low)
        for h in range(heads):
            cols = pl.ds(h * HD, HD)

            def take(ref):
                return ref[:, rows, cols].reshape(size, HD)

            k, q, v, beta = take(k_ref), take(q_ref), take(v_ref), take(b_ref)
            kb = beta * k
            a = -strict * fine(dot_nt, kb, k)
            inverse = lower_inverse(a, lanes)
            mk = fine(dot_nn, inverse, kb)
            mv = fine(dot_nn, inverse, beta * v)
            scores = low * dot_nt(q, k)
            t_ref[g, h] = inverse
            mk_ref[g, h] = mk.astype(mk_ref.dtype)
            mv_ref[g, h] = mv.astype(mv_ref.dtype)
            ready[g, h] = (q, k, mk, mv, scores)
    for g in range(group):
        rows = pl.ds(g * 8, 8)
        carry = c_ref[:, rows].reshape(size, HD)
        keep = m_ref[:, rows].reshape(size, HD)
        for h in range(heads):
            q, k, mk, mv, scores = ready[g, h]
            held = state[h]
            s_ref[g, h] = held
            u = mv - carry * dot_nn(mk, held)
            u_ref[g, h] = u.astype(u_ref.dtype)
            state[h] = (carry[0:1] * keep[0:1]) * held + dot_tn(k, keep * u)
            out = (carry * dot_nn(q, held) + dot_nn(scores, u)) * scale
            o_ref[:, rows, pl.ds(h * HD, HD)] = out.reshape(lanes, 8, HD).astype(o_ref.dtype)


def delta_backward(lanes, heads, group, q_ref, k_ref, v_ref, b_ref, low_ref, c_ref, m_ref, do_ref,
                   s_ref, t_ref, mk_ref, mv_ref, u_ref,
                   dq_ref, dk_ref, dv_ref, db_ref, state):
    size = lanes * 8
    scale = HD ** (-0.5)

    @pl.when(pl.program_id(0) == 0)
    def _():
        state[...] = jnp.zeros_like(state)

    row_t = time_of((size, size), 0, lanes)
    col_t = time_of((size, size), 1, lanes)
    ready = {}
    for g in range(group):
        rows = pl.ds(g * 8, 8)
        low = low_ref[g]
        carry = c_ref[:, rows].reshape(size, HD)
        for h in range(heads):
            cols = pl.ds(h * HD, HD)

            def take(ref):
                return ref[:, rows, cols].reshape(size, HD)

            k, q = take(k_ref), take(q_ref)
            do = take(do_ref).astype(jnp.float32) * scale
            held = s_ref[g, h]
            u = u_ref[g, h]
            scores = low * dot_nt(q, k)
            du = dot_tn(scores, do)
            ds = low * dot_nt(do, u)
            cdo = carry * do
            dq = dot_nt(cdo, held) + dot_nn(ds, k)
            dk = dot_tn(ds, q)
            gain = dot_tn(q, cdo)
            dq_ref[:, rows, cols] = dq.reshape(lanes, 8, HD)
            ready[g, h] = (k, du, dk, gain)
    after = {}
    for g in reversed(range(group)):
        rows = pl.ds(g * 8, 8)
        carry = c_ref[:, rows].reshape(size, HD)
        keep = m_ref[:, rows].reshape(size, HD)
        for h in range(heads):
            k, du, dk, gain = ready[g, h]
            later = state[h]
            du = du + keep * dot_nn(k, later)
            state[h] = (carry[0:1] * keep[0:1]) * later + gain - dot_tn(carry * mk_ref[g, h].astype(jnp.float32), du)
            after[g, h] = (du, later)
    for g in range(group):
        rows = pl.ds(g * 8, 8)
        low = low_ref[g]
        strict = jnp.where(row_t == col_t, 0.0, low)
        carry = c_ref[:, rows].reshape(size, HD)
        keep = m_ref[:, rows].reshape(size, HD)
        for h in range(heads):
            cols = pl.ds(h * HD, HD)

            def take(ref):
                return ref[:, rows, cols].reshape(size, HD)

            k, du, dk, gain = ready[g, h]
            v, beta = take(v_ref), take(b_ref)
            du, later = after[g, h]
            u = u_ref[g, h].astype(jnp.float32)
            inverse = t_ref[g, h]
            dk = dk + dot_nt(keep * u, later)
            dmk = -carry * dot_nt(du, s_ref[g, h])
            xx = dot_tn(inverse, dmk)
            yy = dot_tn(inverse, du)
            da = strict * (dot_nt(xx, mk_ref[g, h]) + dot_nt(yy, mv_ref[g, h]))
            dkb = xx - dot_nn(da, k)
            dk = dk - dot_tn(da, beta * k) + beta * dkb
            dk_ref[:, rows, cols] = dk.reshape(lanes, 8, HD)
            dv_ref[:, rows, cols] = (beta * yy).reshape(lanes, 8, HD)
            db = jnp.sum(dkb * k + yy * v, axis=1, keepdims=True)
            db_ref[:, rows, cols] = jnp.broadcast_to(db, (size, HD)).reshape(lanes, 8, HD)


def block_specs(lanes, heads, group, flip):
    size = lanes * 8
    wide = heads * HD
    at = (lambda i: flip - 1 - i) if flip else (lambda i: i)
    token = pl.BlockSpec((lanes, 8 * group, wide), lambda i: (0, at(i), 0))
    flag = pl.BlockSpec((lanes, 8 * group, HD), lambda i: (0, at(i), 0))
    square = pl.BlockSpec((group, size, size), lambda i: (at(i), 0, 0))
    held = pl.BlockSpec((group, heads, HD, HD), lambda i: (at(i), 0, 0, 0))
    tri = pl.BlockSpec((group, heads, size, size), lambda i: (at(i), 0, 0, 0))
    rows = pl.BlockSpec((group, heads, size, HD), lambda i: (at(i), 0, 0, 0))
    return token, flag, square, held, tri, rows


def mixer_forward(q, k, v, beta, low, carry, keep, group=4):
    lanes, tokens, wide = q.shape
    heads, blocks, size = wide // HD, tokens // 8, lanes * 8
    token, flag, square, held, tri, rows = block_specs(lanes, heads, group, 0)
    row_shape = jax.ShapeDtypeStruct((blocks, heads, size, HD), jnp.bfloat16)
    return pl.pallas_call(
        functools.partial(delta_forward, lanes, heads, group),
        grid=(blocks // group,),
        in_specs=[token, token, token, token, square, flag, flag],
        out_specs=[token, held, tri, rows, rows, rows],
        out_shape=[
            jax.ShapeDtypeStruct((lanes, tokens, wide), jnp.float32),
            jax.ShapeDtypeStruct((blocks, heads, HD, HD), jnp.float32),
            jax.ShapeDtypeStruct((blocks, heads, size, size), jnp.float32),
            row_shape, row_shape, row_shape,
        ],
        scratch_shapes=[pltpu.VMEM((heads, HD, HD), jnp.float32)],
        compiler_params=pltpu.CompilerParams(vmem_limit_bytes=48 * 1024 * 1024),
    )(q, k, v, beta, low, carry, keep)


def mixer_backward(q, k, v, beta, low, carry, keep, d_out, saved, group=4):
    lanes, tokens, wide = q.shape
    heads, blocks, size = wide // HD, tokens // 8, lanes * 8
    token, flag, square, held, tri, rows = block_specs(lanes, heads, group, blocks // group)
    shape = jax.ShapeDtypeStruct((lanes, tokens, wide), jnp.float32)
    return pl.pallas_call(
        functools.partial(delta_backward, lanes, heads, group),
        grid=(blocks // group,),
        in_specs=[token, token, token, token, square, flag, flag, token, held, tri, rows, rows, rows],
        out_specs=[token] * 4,
        out_shape=[shape] * 4,
        scratch_shapes=[pltpu.VMEM((heads, HD, HD), jnp.float32)],
        compiler_params=pltpu.CompilerParams(vmem_limit_bytes=48 * 1024 * 1024),
    )(q, k, v, beta, low, carry, keep, d_out, *saved)


def segment_masks(lengths_grid, order_row, lanes, tokens):
    slots = order_row.shape[0]
    flat = lengths_grid.reshape(slots)
    match = order_row[:, None] == lax.broadcasted_iota(jnp.int32, (slots, slots), 1)
    run_len = jnp.sum(jnp.where(match, flat[None, :], 0), axis=1)
    upto = lax.broadcasted_iota(jnp.int32, (slots, slots), 0) >= lax.broadcasted_iota(jnp.int32, (slots, slots), 1)
    ends = jnp.sum(jnp.where(upto, run_len[None, :], 0), axis=1)
    starts = ends - run_len
    size = lanes * 8
    blocks = tokens // 8
    lane = lax.broadcasted_iota(jnp.int32, (lanes, tokens), 0)
    step = lax.broadcasted_iota(jnp.int32, (lanes, tokens), 1)
    place = step * lanes + lane
    inside = (starts[:, None, None] <= place[None]) & (place[None] < ends[:, None, None])
    start_at = jnp.sum(jnp.where(inside, starts[:, None, None], 0), axis=0)
    end_at = jnp.sum(jnp.where(inside, ends[:, None, None], 0), axis=0)
    block = step // 8
    carry = (start_at < block * size).astype(jnp.float32)
    keep = (end_at >= (block + 1) * size).astype(jnp.float32)

    def blocked(values):
        return values.reshape(lanes, blocks, 8).transpose(1, 0, 2).reshape(blocks, size)

    start_b, place_b = blocked(start_at), blocked(place)
    low = (start_b[:, :, None] == start_b[:, None, :]) & (place_b[:, :, None] >= place_b[:, None, :])
    offset = place - start_at
    wide = (lanes, tokens, HD)
    return (
        low.astype(jnp.float32),
        jnp.broadcast_to(carry[:, :, None], wide),
        jnp.broadcast_to(keep[:, :, None], wide),
        offset,
    )


def back_in_stream(values, hops):
    lanes, tokens, wide = values.shape
    moved = jnp.pad(values[lanes - hops :, : tokens - 1], ((0, 0), (1, 0), (0, 0)))
    return jnp.concatenate([moved, values[: lanes - hops]], axis=0)


def ahead_in_stream(values, hops):
    moved = jnp.pad(values[:hops, 1:], ((0, 0), (0, 1), (0, 0)))
    return jnp.concatenate([values[hops:], moved], axis=0)


def conv_sums(signal, taps, offset):
    total = signal * taps[0]
    for hop in range(1, taps.shape[0]):
        moved = jnp.where((offset >= hop)[:, :, None], back_in_stream(signal, hop), 0.0)
        total = total + moved * taps[hop]
    return total


def conv_back(err, signal, taps, offset):
    d_signal = err * taps[0]
    d_taps = [jnp.sum(err * signal, axis=(0, 1))]
    for hop in range(1, taps.shape[0]):
        live = jnp.where((offset >= hop)[:, :, None], err, 0.0)
        d_taps.append(jnp.sum(live * back_in_stream(signal, hop), axis=(0, 1)))
        d_signal = d_signal + ahead_in_stream(live, hop) * taps[hop]
    return d_signal, jnp.stack(d_taps)


def unit_heads(pre):
    lanes, tokens, wide = pre.shape
    split = pre.reshape(lanes, tokens, wide // HD, HD)
    inverse = lax.rsqrt(jnp.sum(split * split, axis=-1, keepdims=True) + 1e-6)
    return (split * inverse).reshape(pre.shape)


def unit_back(pre, grad):
    lanes, tokens, wide = pre.shape
    split = pre.reshape(lanes, tokens, wide // HD, HD)
    g = grad.reshape(split.shape)
    inverse = lax.rsqrt(jnp.sum(split * split, axis=-1, keepdims=True) + 1e-6)
    inner = jnp.sum(split * g, axis=-1, keepdims=True)
    return (inverse * g - split * (inverse * inverse * inverse) * inner).reshape(pre.shape)


def silu_slope(total):
    s = jax.nn.sigmoid(total)
    return s * (1.0 + total * (1.0 - s))


def prepare(q0, k0, v0, logits, taps, offset):
    sums = [conv_sums(signal, tap, offset) for signal, tap in zip((q0, k0, v0), taps)]
    pre = [jax.nn.silu(t) for t in sums]
    lanes, tokens, heads = logits.shape
    strength = jax.nn.sigmoid(logits)
    beta = jnp.broadcast_to(strength[..., None], (lanes, tokens, heads, HD)).reshape(lanes, tokens, heads * HD)
    return unit_heads(pre[0]), unit_heads(pre[1]), pre[2], beta


def unprepare(q0, k0, v0, logits, taps, offset, dq, dk, dv, db):
    signals = (q0, k0, v0)
    sums = [conv_sums(signal, tap, offset) for signal, tap in zip(signals, taps)]
    pre = [jax.nn.silu(t) for t in sums]
    grads = (unit_back(pre[0], dq), unit_back(pre[1], dk), dv)
    errs = [g * silu_slope(t) for g, t in zip(grads, sums)]
    backs = [conv_back(e, signal, tap, offset) for e, signal, tap in zip(errs, signals, taps)]
    lanes, tokens, heads = logits.shape
    strength = jax.nn.sigmoid(logits)
    d_strength = db.reshape(lanes, tokens, heads, HD)[..., 0]
    d_logits = d_strength * strength * (1.0 - strength)
    return [b[0] for b in backs], d_logits, [b[1] for b in backs]


def project(left_side, right_side):
    return jnp.dot(left_side, right_side, preferred_element_type=jnp.float32)


def times_t(left_side, right_side):
    return lax.dot_general(
        left_side, right_side, (((1,), (1,)), ((), ())), preferred_element_type=jnp.float32
    )


def contract_rows(left_side, right_side):
    return lax.dot_general(
        left_side, right_side, (((0,), (0,)), ((), ())), preferred_element_type=jnp.float32
    )


def rms(values, gain, eps):
    return values * lax.rsqrt(jnp.mean(values * values, axis=-1, keepdims=True) + eps) * gain


def rms_back(values, gain, eps, grad):
    r = lax.rsqrt(jnp.mean(values * values, axis=-1, keepdims=True) + eps)
    inner = jnp.mean(values * gain * grad, axis=-1, keepdims=True)
    return r * gain * grad - values * (r * r * r) * inner, grad * values * r


def heads_of(values):
    return values.reshape(values.shape[0], -1, HD)


def deal(stacked):
    return lax.all_to_all(stacked, "shard", split_axis=0, concat_axis=0, tiled=True)


def body(
    layer_input,
    out_cotangent,
    seq_lengths,
    seq_order,
    w_query,
    w_key,
    w_value,
    w_beta,
    w_outgate,
    w_output,
    conv_query,
    conv_key,
    conv_value,
    attn_gain,
    head_gain,
    mlp_gain,
    w_gate,
    w_up,
    w_down,
):
    bf16, f32 = jnp.bfloat16, jnp.float32
    shards, replicas = lax.axis_size("shard"), lax.axis_size("replica")
    rows, width = layer_input.shape
    tokens = shards * rows
    own = w_output.shape[0]
    heads = own // HD
    hidden_own = w_down.shape[0]
    ffn = w_gate.shape[1]

    def by_columns(weight):
        return weight.reshape(weight.shape[0], shards, -1).transpose(1, 0, 2)

    attn_weights = jnp.concatenate(
        [by_columns(w) for w in (w_query, w_key, w_value, w_outgate)]
        + [jnp.pad(by_columns(w_beta), ((0, 0), (0, 0), (0, HD - heads)))],
        axis=2,
    )
    attn_weights = deal(attn_weights).reshape(width, -1)
    mlp_weights = deal(jnp.concatenate([by_columns(w_gate), by_columns(w_up)], axis=2))
    mlp_weights = mlp_weights.reshape(width, -1)
    gains = lax.all_gather(jnp.stack([attn_gain, mlp_gain]), "shard", axis=1, tiled=True).astype(f32)
    full_attn_gain, full_mlp_gain = gains[0], gains[1]
    full_head_gain = lax.all_gather(head_gain, "shard", axis=0, tiled=True).astype(f32)
    low, carry, keep, offset = segment_masks(seq_lengths[0], seq_order[0], shards, rows)

    source = layer_input.astype(f32)
    all_source = gather_rows(layer_input, "shard", 0).reshape(tokens, width)
    normed = rms(all_source.astype(f32), full_attn_gain, 1e-6).astype(bf16)
    projected = project(normed, attn_weights)

    def stream(values):
        return values.astype(bf16).astype(f32).reshape(shards, rows, -1)

    query0 = stream(projected[:, :own])
    key0 = stream(projected[:, own : 2 * own])
    value0 = stream(projected[:, 2 * own : 3 * own])
    gate = projected[:, 3 * own : 4 * own]
    logits = stream(projected[:, 4 * own : 4 * own + heads])
    taps = [t.astype(f32) for t in (conv_query, conv_key, conv_value)]
    q, k, v, beta = prepare(query0, key0, value0, logits, taps, offset)
    mixed, *saved = mixer_forward(q, k, v, beta, low, carry, keep)
    mixed = mixed.astype(bf16).astype(f32).reshape(tokens, heads, HD)
    gate_heads = heads_of(gate)
    head_normed = rms(mixed, full_head_gain, 1e-5)
    zed = (head_normed * jax.nn.silu(gate_heads)).astype(bf16).reshape(tokens, own)
    hidden = source + scatter_rows(project(zed, w_output).astype(bf16), "shard", 1)

    mlp_in = gather_rows(rms(hidden, full_mlp_gain, 1e-6).astype(bf16), "shard", 2)
    mlp_in = mlp_in.reshape(tokens, width)
    lin = project(mlp_in, mlp_weights)
    gate_lin, up_lin = lin[:, :hidden_own], lin[:, hidden_own:]
    s = jax.nn.sigmoid(gate_lin)
    product = (gate_lin * s * up_lin).astype(bf16)
    layer_output = hidden + scatter_rows(project(product, w_down).astype(bf16), "shard", 3)

    dy = gather_rows(out_cotangent, "shard", 4).reshape(tokens, width)
    d_product = times_t(dy, w_down)
    d_gate = (d_product * up_lin * s * (1.0 + gate_lin * (1.0 - s))).astype(bf16)
    d_up = (d_product * gate_lin * s).astype(bf16)
    d_lin = jnp.concatenate([d_gate, d_up], axis=1)
    d_mlp_in = scatter_rows(times_t(d_lin, mlp_weights).astype(bf16), "shard", 5)
    d_hidden_norm, g_mlp_rows = rms_back(hidden, full_mlp_gain, 1e-6, d_mlp_in)
    d_hidden = out_cotangent.astype(f32) + d_hidden_norm
    g_down = contract_rows(product, dy)
    g_lin = contract_rows(mlp_in, d_lin)

    d_attn = gather_rows(d_hidden.astype(bf16), "shard", 6).reshape(tokens, width)
    g_output = contract_rows(zed, d_attn)
    d_zed = heads_of(times_t(d_attn, w_output))
    d_mixed, g_head_rows = rms_back(mixed, full_head_gain, 1e-5, d_zed * jax.nn.silu(gate_heads))
    d_gate_pre = (d_zed * head_normed * silu_slope(gate_heads)).astype(bf16).reshape(tokens, own)
    d_mixed = d_mixed.astype(bf16).astype(f32).reshape(shards, rows, own)
    d_all = mixer_backward(q, k, v, beta, low, carry, keep, d_mixed, saved)
    signals, d_logits, g_taps = unprepare(query0, key0, value0, logits, taps, offset, *d_all)
    d_logits = jnp.pad(d_logits.reshape(tokens, heads), ((0, 0), (0, HD - heads)))
    d_proj = jnp.concatenate(
        [d.reshape(tokens, own).astype(bf16) for d in signals] + [d_gate_pre, d_logits.astype(bf16)],
        axis=1,
    )
    d_normed = scatter_rows(times_t(d_proj, attn_weights).astype(bf16), "shard", 7)
    d_source, g_attn_rows = rms_back(source, full_attn_gain, 1e-6, d_normed)
    input_grad = (d_hidden + d_source).astype(bf16)
    g_proj = contract_rows(normed, d_proj)

    part = width // shards // replicas
    split_grads = jnp.concatenate([g_proj, g_lin], axis=1).astype(bf16)
    wide = split_grads.shape[1]
    split_grads = split_grads.reshape(shards, replicas, part, wide).transpose(1, 0, 2, 3)
    split_grads = scatter_rows(split_grads.reshape(-1, wide), "replica", 8, 4, bf16)
    split_grads = deal(split_grads.reshape(shards, part, wide)).reshape(-1, wide)
    split_grads = gather_rows(split_grads, "replica", 9, 4).reshape(replicas, shards, part, wide)

    def assemble(first, count):
        taken = split_grads[..., first : first + count].transpose(0, 2, 1, 3)
        return taken.reshape(replicas * part, shards * count).astype(f32)

    lone = jnp.concatenate([g_output, g_down], axis=0).astype(bf16)
    fill = -lone.shape[0] % (replicas * 16)
    lone = jnp.pad(lone, ((0, fill), (0, 0)))
    lone = gather_rows(scatter_rows(lone, "replica", 10, 1, bf16), "replica", 11, 1)
    lone = lone.reshape(-1, width).astype(f32)

    def small(values):
        total = lax.psum(values.astype(f32), ("replica", "shard"))
        count = total.shape[0] // shards
        return lax.dynamic_slice_in_dim(total, lax.axis_index("shard") * count, count)

    g_taps = lax.psum(jnp.stack(g_taps), "replica")
    return (
        layer_output.astype(bf16),
        input_grad,
        assemble(0, own),
        assemble(own, own),
        assemble(2 * own, own),
        assemble(4 * own, heads),
        assemble(3 * own, own),
        lone[:own],
        g_taps[0],
        g_taps[1],
        g_taps[2],
        small(jnp.sum(g_attn_rows, axis=0)),
        small(jnp.sum(g_head_rows, axis=(0, 1))),
        small(jnp.sum(g_mlp_rows, axis=0)),
        assemble(4 * own + HD, hidden_own),
        assemble(4 * own + HD + hidden_own, hidden_own),
        lone[own : own + hidden_own],
    )


def solution(mesh):
    tokens = P(("replica", "shard"), None)
    whole, columns, vector = P("shard", None), P(None, "shard"), P("shard")
    in_specs = (tokens, tokens, P("replica", None, None), P("replica", None)) + (whole,) * 6
    in_specs += (columns,) * 3 + (vector,) * 3 + (whole,) * 3
    out_specs = (tokens, tokens) + (whole,) * 6 + (columns,) * 3 + (vector,) * 3 + (whole,) * 3
    return jax.shard_map(body, mesh=mesh, in_specs=in_specs, out_specs=out_specs, check_vma=False)
```

time: 5110 us -> 1990 us (0.39)
  waiting for transfers between devices: 3820 us -> 0.01 us
  Pallas kernels: 0 us -> 1130 us
  matrix products: 635 us -> 149 us
  local copies, waits for them, and re-layouts: 184 us -> 393 us
  blocking collectives: 288 us -> 107 us
  other arithmetic: 118 us -> 182 us
    all_gather x8 -> x0, waiting for transfers between devices: 1470 us -> none  [the longest x1 432 us: body(): lax.all_gather(w_gate, 'shard', axis=0, tiled=True)]
    unnamed x21 -> x0, waiting for transfers between devices: 1280 us -> none
    pallas_call x0 -> x14, Pallas kernels: none -> 1130 us  [the longest x6 504 us: gather_rows(): pl.pallas_call(functools.partial(gather_kernel, axis, Z, X, chunks), out_...]
    reduce_scatter x4 -> x0, waiting for transfers between devices: 795 us -> none  [the longest x1 401 us: body(): lax.psum_scatter(contract_rows(normed_dst, qkv_right).astype(jnp.bfloat16...]
    dot_general x346 -> x0, matrix products: 424 us -> none  [the longest x100 105 us: span_step(): jnp.einsum('hij,hjk->hik', inverse, identity + powered, precision=highest)]
    psum x1 -> x0, waiting for transfers between devices: 231 us -> none  [body(): lax.psum(gate_out_grads[:, :feat_width].astype(jnp.bfloat16), 'replica')]
    all_gather x6 -> x1, blocking collectives: 215 us -> 17.1 us  [body(): lax.all_gather(jnp.stack([attn_gain, mlp_gain]), 'shard', axis=1, tiled=T...]
    slice x7 -> x51, local copies, waits for them, and re-layouts: 14.4 us -> 76.6 us  [the longest x18 37.3 us: back_in_stream(): return jnp.concatenate([moved, values[:lanes - hops]], axis=0)]
  transfers between devices with their start and end apart: 21 -> 3, of which waited for: 15 -> 0; matrix products, arithmetic and copies ran while one was open for 16% -> 20% of each run, Pallas kernels for 0% -> 33%
where the time goes in v1:
time: 1990 us; the launch traced here: 1980 us
  Pallas kernels  1130 us (57%)
  local copies, waits for them, and re-layouts  393 us (20%)
  other arithmetic  182 us (9%)
  matrix products  149 us (7%)
  blocking collectives  107 us (5%)
    pallas_call x6, Pallas kernels, gather_rows(): pl.pallas_call(functools.partial(gather_kernel, axis, Z, X, chunks), out_...  504 us
    pallas_call x6, Pallas kernels, scatter_rows(): pl.pallas_call(functools.partial(scatter_kernel, axis, Z, X, chunks), out...  476 us
    pallas_call x1, Pallas kernels, mixer_forward(): pl.pallas_call(functools.partial(delta_forward, lanes, heads, group), gri...  109 us
    unnamed x339, local copies, waits for them, and re-layouts  67.1 us
    dot_general x4, matrix products, times_t(): lax.dot_general(left_side, right_side, (((1,), (1,)), ((), ())), preferre...  58 us
    dot_general x4, matrix products, project(): return jnp.dot(left_side, right_side, preferred_element_type=jnp.float32)  50.1 us
    psum x1, blocking collectives, small(): total = lax.psum(values.astype(f32), ('replica', 'shard'))  44.6 us
    dot_general x4, matrix products, contract_rows(): lax.dot_general(left_side, right_side, (((0,), (0,)), ((), ())), preferre...  40.8 us
  transfers between devices with their start and end apart: 3, of which 0 were waited for; matrix products, arithmetic and copies ran while one was open for 20% of the time, Pallas kernels for 33%

profile of v1, /device:TPU:0, one launch (start us, length us, event | category | flops | bytes accessed | tf_op | source)
XLA Modules:
  0.0 1981.2 jit_solution(12031216811588128970)
XLA Ops:
  25.5 163.5 %shard_map.314 = bf16[8,256,2048]{2,1,0:T(8,128)(2,1)} custom-call(bf16[256,2048]{1,0:T(8,128)(2,1)} %x_ref.2), custom_call_target="tpu_custom_call" | custom-call | tf_op jit(solution)/shard_map/pallas_call | solution.py:131
  191.1 34.4 %all-reduce.20 = bf16[128]{0:T(256)(128)(2,1)S(1)} all-reduce(bf16[128]{0:T(256)(128)(2,1)S(1)} %dynamic-update-slice), channel_id=1, replica_groups=mesh['replica'=4,'shard'=8] {'shard'}, use_global_device_ids=true, to_apply=%add.20 | all-reduce | flops 128 | bytes 512
  234.6 90.0 %shard_map.319 = bf16[8,256,2048]{2,1,0:T(8,128)(2,1)} custom-call(bf16[256,2048]{1,0:T(8,128)(2,1)} %x_ref.3), custom_call_target="tpu_custom_call" | custom-call | tf_op jit(solution)/shard_map/pallas_call | solution.py:131
  329.7 17.1 all_gather.6
  396.5 16.4 fusion.78
  470.1 17.4 multiply_reduce_fusion.21
  563.6 17.5 multiply_reduce_fusion.22
  630.7 109.1 %shard_map.315 = (f32[8,256,256]{2,1,0:T(8,128)}, f32[32,2,128,128]{3,2,1,0:T(8,128)}, f32[32,2,64,64]{3,2,1,0:T(8,128)}, bf16[32,2,64,128]{3,2,1,0:T(8,128)(2,1...) custom-call(f32[8,256,256]{2,1,0:T(8,128)} %get-tuple-element.82.q_ref, ...), custom_call_target="tpu_custom_call" | custom-call | tf_op jit(solution)/shard_map/pallas_call | solution.py:531
  776.5 96.1 %shard_map.316 = f32[256,2048]{1,0:T(8,128)} custom-call(bf16[8,256,2048]{2,1,0:T(8,128)(2,1)} %bitcast.239), custom_call_target="tpu_custom_call" | custom-call | tf_op jit(solution)/shard_map/pallas_call | solution.py:306
  877.6 78.7 %shard_map.317 = bf16[8,256,2048]{2,1,0:T(8,128)(2,1)} custom-call(bf16[256,2048]{1,0:T(8,128)(2,1)} %multiply_convert_fusion.5.x_ref), custom_call_target="tpu_custom_call" | custom-call | tf_op jit(solution)/shard_map/pallas_call | solution.py:131
  1000.6 19.0 fusion.79
  1019.6 16.5 multiply_convert_fusion.2
  1052.7 17.9 convolution_convert_fusion.1
  1070.6 88.4 %shard_map.320 = f32[256,2048]{1,0:T(8,128)} custom-call(bf16[8,256,2048]{2,1,0:T(8,128)(2,1)} %bitcast.284), custom_call_target="tpu_custom_call" | custom-call | tf_op jit(solution)/shard_map/pallas_call | solution.py:306
  1161.7 89.2 %shard_map.318 = f32[256,2048]{1,0:T(8,128)} custom-call(bf16[8,256,2048]{2,1,0:T(8,128)(2,1)} %bitcast.282), custom_call_target="tpu_custom_call" | custom-call | tf_op jit(solution)/shard_map/pallas_call | solution.py:306
  1255.9 59.4 %shard_map.321 = bf16[8,256,2048]{2,1,0:T(8,128)(2,1)} custom-call(bf16[256,2048]{1,0:T(8,128)(2,1)} %get-tuple-element.72.x_ref), custom_call_target="tpu_custom_call" | custom-call | tf_op jit(solution)/shard_map/pallas_call | solution.py:131
  1334.7 40.4 %shard_map.322 = (f32[8,256,256]{2,1,0:T(8,128)}, f32[8,256,256]{2,1,0:T(8,128)}, f32[8,256,256]{2,1,0:T(8,128)}, f32[8,256,256]{2,1,0:T(8,128)}) custom-call(f32[8,256,256]{2,1,0:T(8,128)} %get-tuple-element.82.q_ref, f32[8,256,256]{2,1,0:T(8,128)} %get-tuple-element.78.k_ref, f32[8,256,256]{2,1,0:T(8,128)} %get-tuple-element.76.v_ref, ...), custom_call_target="tpu_custom_call" | custom-call | tf_op jit(solution)/shard_map/pallas_call | solution.py:552
  1443.6 27.7 %shard_map.326.x_ref = bf16[240,2048]{1,0:T(8,128)(2,1)} custom-call(bf16[4,240,2048]{2,1,0:T(8,128)(2,1)} %bitcast.273), custom_call_target="tpu_custom_call" | custom-call | tf_op jit(solution)/shard_map/pallas_call | solution.py:306
  1471.4 31.1 %shard_map.327 = bf16[4,240,2048]{2,1,0:T(8,128)(2,1)} custom-call(bf16[240,2048]{1,0:T(8,128)(2,1)} %shard_map.326.x_ref), custom_call_target="tpu_custom_call" | custom-call | tf_op jit(solution)/shard_map/pallas_call | solution.py:131
  1514.2 17.4 fusion.6
  1571.7 65.0 %shard_map.324 = bf16[512,2560]{1,0:T(8,128)(2,1)} custom-call(bf16[4,512,2560]{2,1,0:T(8,128)(2,1)} %bitcast.243), custom_call_target="tpu_custom_call" | custom-call | tf_op jit(solution)/shard_map/pallas_call | solution.py:306
  1662.3 109.9 %shard_map.323 = f32[256,2048]{1,0:T(8,128)} custom-call(bf16[8,256,2048]{2,1,0:T(8,128)(2,1)} %bitcast.283), custom_call_target="tpu_custom_call" | custom-call | tf_op jit(solution)/shard_map/pallas_call | solution.py:306
  1774.6 44.6 %all-reduce.21 = (f32[2048]{0:T(1024)S(1)}, f32[128]{0:T(128)S(1)}, f32[2048]{0:T(1024)S(1)}) all-reduce(f32[2048]{0:T(1024)S(1)} %get-tuple-element.41, f32[128]{0:T(128)S(1)} %copy-done.137, f32[2048]{0:T(1024)S(1)} %copy-done.101), channel_id=1, replica_groups=mesh['replica'=4,'shard'=8] {'replica','shard'}, use_global_device_ids=true, to_apply=%region_29.30 | all-reduce | flops 4224 | bytes 33792 | tf_op jit(solution)/shard_map/psum | solution.py:829
  1836.3 81.3 %shard_map.325 = bf16[4,512,2560]{2,1,0:T(8,128)(2,1)} custom-call(bf16[512,2560]{1,0:T(8,128)(2,1)} %bitcast.83.x_ref), custom_call_target="tpu_custom_call" | custom-call | tf_op jit(solution)/shard_map/pallas_call | solution.py:131
  (564 shorter events, 630.1 us)
Async XLA Ops:
  0.7 1018.9 %copy-start = (bf16[704,2048]{1,0:T(8,128)(2,1)S(1)}, bf16[704,2048]{1,0:T(8,128)(2,1)}, u32[]{:S(2)}) copy-start(bf16[704,2048]{1,0:T(8,128)(2,1)} %param.37) | copy-start | bytes 8650756
  17.5 367.5 %all-to-all-start = ((bf16[8,256,1152]{1,2,0:T(8,128)(2,1)}), bf16[8,256,1152]{1,2,0:T(8,128)(2,1)}, u32[]{:S(2)}, u32[]{:S(2)}) async-start(bf16[8,256,1152]{1,2,0:T(8,128)(2,1)} %pad_dynamic-update-slice_fusion.1), calls=%async_computation | async-start | bytes 9437184 | tf_op jit(solution)/shard_map/all_to_all | solution.py:702
  25.4 164.1 %copy-start.142 = (u32[32]{0:T(128)S(1)}, u32[32]{0:T(128)}, u32[]{:S(2)}) copy-start(u32[32]{0:T(128)} %constant.122) | copy-start | bytes 388
  25.5 165.4 %copy-start.141 = (bf16[16]{0:T(256)(128)(2,1)S(1)}, bf16[16]{0:T(256)(128)(2,1)}, u32[]{:S(2)}) copy-start(bf16[16]{0:T(256)(128)(2,1)} %param.33) | copy-start | bytes 100
  225.5 142.4 %copy-start.135 = (f32[128]{0:T(128)}, f32[128]{0:T(128)S(1)}, u32[]{:S(2)}) copy-start(f32[128]{0:T(128)S(1)} %convert_element_type.280) | copy-start | bytes 1540
  368.4 243.9 %copy-start.102 = (f32[1,256]{1,0:T(1,128)}, f32[1,256]{1,0:T(1,128)S(1)}, u32[]{:S(2)}) copy-start(f32[1,256]{1,0:T(1,128)S(1)} %get-tuple-element.142) | copy-start | bytes 3076
  368.4 243.9 %copy-start.104 = (f32[1,256]{1,0:T(1,128)}, f32[1,256]{1,0:T(1,128)S(1)}, u32[]{:S(2)}) copy-start(f32[1,256]{1,0:T(1,128)S(1)} %get-tuple-element.143) | copy-start | bytes 3076
  368.5 243.9 %copy-start.106 = (f32[1,256]{1,0:T(1,128)}, f32[1,256]{1,0:T(1,128)S(1)}, u32[]{:S(2)}) copy-start(f32[1,256]{1,0:T(1,128)S(1)} %get-tuple-element.144) | copy-start | bytes 3076
  368.5 243.9 %copy-start.108 = (f32[1,256]{1,0:T(1,128)}, f32[1,256]{1,0:T(1,128)S(1)}, u32[]{:S(2)}) copy-start(f32[1,256]{1,0:T(1,128)S(1)} %get-tuple-element.145) | copy-start | bytes 3076
  368.5 251.7 %copy-start.110 = (f32[1,256]{1,0:T(1,128)}, f32[1,256]{1,0:T(1,128)S(1)}, u32[]{:S(2)}) copy-start(f32[1,256]{1,0:T(1,128)S(1)} %get-tuple-element.146) | copy-start | bytes 3076
  368.5 251.7 %copy-start.112 = (f32[1,256]{1,0:T(1,128)}, f32[1,256]{1,0:T(1,128)S(1)}, u32[]{:S(2)}) copy-start(f32[1,256]{1,0:T(1,128)S(1)} %get-tuple-element.147) | copy-start | bytes 3076
  368.5 251.7 %copy-start.114 = (f32[1,256]{1,0:T(1,128)}, f32[1,256]{1,0:T(1,128)S(1)}, u32[]{:S(2)}) copy-start(f32[1,256]{1,0:T(1,128)S(1)} %get-tuple-element.148) | copy-start | bytes 3076
  368.5 251.7 %copy-start.116 = (f32[1,256]{1,0:T(1,128)}, f32[1,256]{1,0:T(1,128)S(1)}, u32[]{:S(2)}) copy-start(f32[1,256]{1,0:T(1,128)S(1)} %get-tuple-element.149) | copy-start | bytes 3076
  369.1 255.0 %copy-start.119 = (f32[1,256]{1,0:T(1,128)}, f32[1,256]{1,0:T(1,128)S(1)}, u32[]{:S(2)}) copy-start(f32[1,256]{1,0:T(1,128)S(1)} %get-tuple-element.138) | copy-start | bytes 3076
  369.1 255.0 %copy-start.121 = (f32[1,256]{1,0:T(1,128)}, f32[1,256]{1,0:T(1,128)S(1)}, u32[]{:S(2)}) copy-start(f32[1,256]{1,0:T(1,128)S(1)} %get-tuple-element.139) | copy-start | bytes 3076
  369.1 255.0 %copy-start.123 = (f32[1,256]{1,0:T(1,128)}, f32[1,256]{1,0:T(1,128)S(1)}, u32[]{:S(2)}) copy-start(f32[1,256]{1,0:T(1,128)S(1)} %get-tuple-element.140) | copy-start | bytes 3076
  369.1 254.9 %copy-start.94 = (pred[8,256]{1,0:T(8,128)(4,1)}, pred[8,256]{1,0:T(8,128)(4,1)S(1)}, u32[]{:S(2)}) copy-start(pred[8,256]{1,0:T(8,128)(4,1)S(1)} %get-tuple-element.124) | copy-start | bytes 6148
  369.2 254.9 %copy-start.96 = (pred[8,256]{1,0:T(8,128)(4,1)}, pred[8,256]{1,0:T(8,128)(4,1)S(1)}, u32[]{:S(2)}) copy-start(pred[8,256]{1,0:T(8,128)(4,1)S(1)} %get-tuple-element.125) | copy-start | bytes 6148
  369.2 254.9 %copy-start.98 = (pred[8,256]{1,0:T(8,128)(4,1)}, pred[8,256]{1,0:T(8,128)(4,1)S(1)}, u32[]{:S(2)}) copy-start(pred[8,256]{1,0:T(8,128)(4,1)S(1)} %get-tuple-element.126) | copy-start | bytes 6148
  385.0 607.4 %all-to-all-start.1 = ((bf16[8,256,1408]{1,2,0:T(8,128)(2,1)}), bf16[8,256,1408]{1,2,0:T(8,128)(2,1)}, u32[]{:S(2)}, u32[]{:S(2)}) async-start(bf16[8,256,1408]{1,2,0:T(8,128)(2,1)} %pad_maximum_fusion), calls=%async_computation.1 | async-start | bytes 11534336 | tf_op jit(solution)/shard_map/all_to_all | solution.py:702
  629.4 110.4 %copy-start.4 = (f32[8,256,128]{2,1,0:T(8,128)}, f32[8,256,128]{2,1,0:T(8,128)S(1)}, u32[]{:S(2)}) copy-start(f32[8,256,128]{2,1,0:T(8,128)S(1)} %broadcast_in_dim.246.c_ref) | copy-start | bytes 3145732
  1636.7 199.5 %all-to-all-start.2 = ((bf16[8,64,2560]{2,1,0:T(8,128)(2,1)}), bf16[8,64,2560]{2,1,0:T(8,128)(2,1)}, u32[]{:S(2)}, u32[]{:S(2)}) async-start(bf16[8,64,2560]{2,1,0:T(8,128)(2,1)} %bitcast.280), calls=%async_computation.2 | async-start | bytes 5242880 | tf_op jit(solution)/shard_map/all_to_all | solution.py:702
  1662.3 109.9 %copy-start.93 = (f32[1,2048]{1,0:T(1,128)S(1)}, f32[1,2048]{1,0:T(1,128)}, u32[]{:S(2)}) copy-start(f32[1,2048]{1,0:T(1,128)} %copy-done.92) | copy-start | bytes 24580
  1662.3 109.9 %copy-start.118 = (f32[256]{0:T(256)S(1)}, f32[256]{0:T(256)}, u32[]{:S(2)}) copy-start(f32[256]{0:T(256)} %get-tuple-element.151) | copy-start | bytes 3076
  (134 other events, 1658.6 us)

commit v2 on v1

v2 whole, which is shorter than its diff:
```python
import functools

import jax
import jax.numpy as jnp
from jax import lax
from jax.experimental import pallas as pl
from jax.experimental.pallas import tpu as pltpu
from jax.sharding import PartitionSpec as P

MESH = pl.DeviceIdType.MESH
ANY = pl.BlockSpec(memory_space=pl.ANY)
VMEM = pl.BlockSpec(memory_space=pltpu.VMEM)
DMA = pltpu.SemaphoreType.DMA
UP, DOWN, RIGHT, LEFT = range(4)


def grid_of(axis):
    count = lax.axis_size(axis)
    if axis == "replica":
        across = 2 if count % 2 == 0 else 1
        return count // across, across
    depth = 4 if count % 4 == 0 else count
    return depth, count // depth


class Lines:
    def __init__(self, axis):
        self.axis = axis
        self.Z, self.X = grid_of(axis)
        self.count = self.Z * self.X
        self.me = lax.axis_index(axis)
        self.z, self.x = lax.div(self.me, self.X), lax.rem(self.me, self.X)
        z, x, X = self.z, self.x, self.X
        self.targets = ((z + 1) * X + x, (z - 1) * X + x, z * X + x + 1, z * X + x - 1)
        self.exists = (z < self.Z - 1, z > 0, x < X - 1, x > 0)

    def to(self, way):
        return {self.axis: self.targets[way]}

    def other(self, k):
        return lax.rem(self.me + k, self.count)


def greet(lines, everyone):
    barrier = pltpu.get_barrier_semaphore()
    count = jnp.int32(0)
    for line in lines:
        if line.axis in everyone:
            for k in range(1, line.count):
                pl.semaphore_signal(
                    barrier, inc=1, device_id={line.axis: line.other(k)}, device_id_type=MESH
                )
            count = count + (line.count - 1)
            continue
        for way in range(4):

            @pl.when(line.exists[way])
            def _(line=line, way=way):
                pl.semaphore_signal(barrier, inc=1, device_id=line.to(way), device_id_type=MESH)

            count = count + jnp.where(line.exists[way], 1, 0)
    pl.semaphore_wait(barrier, count)


def remote(src, dst, send_sem, recv_sem, device):
    return pltpu.make_async_remote_copy(
        src_ref=src,
        dst_ref=dst,
        send_sem=send_sem,
        recv_sem=recv_sem,
        device_id=device,
        device_id_type=MESH,
    )


def in_place(view, sem):
    return pltpu.make_async_copy(view, view, sem)


def gather_sems(axis, chunks):
    Z, X = grid_of(axis)
    return [DMA((4, Z * X, chunks)), DMA((Z * X, chunks))]


def gather_steps(line, chunks, view, source, ready, sems, start, pace):
    send_sem, recv_sem = sems
    Z, X, z, x, me = line.Z, line.X, line.z, line.x, line.me
    exists = line.exists

    def copy(way, origin, c, src=None):
        spot = view(origin, c)
        return remote(
            spot if src is None else src,
            spot,
            send_sem.at[way, origin, c],
            recv_sem.at[origin, c],
            line.to(way),
        )

    def first(c):
        ready(c)
        for way in range(4):

            @pl.when(exists[way])
            def _(way=way):
                copy(way, me, c, source(c)).start()

    def hop(d, c):
        for way, here in ((UP, z - d >= 0), (DOWN, z + d < Z)):

            @pl.when(here)
            def _(way=way):
                origin = (z - d if way == UP else z + d) * X + x
                copy(way, origin, c).wait_recv()
                for onward in (way, RIGHT, LEFT):

                    @pl.when(exists[onward])
                    def _(onward=onward):
                        copy(onward, origin, c).start()

    def across(e, level, c):
        for way, here in ((RIGHT, x - e >= 0), (LEFT, x + e < X)):

            @pl.when(here)
            def _(way=way):
                origin = level * X + (x - e if way == RIGHT else x + e)
                copy(way, origin, c).wait_recv()
                if X > 2:

                    @pl.when(exists[way])
                    def _():
                        copy(way, origin, c).start()

    def finish():
        for c in range(chunks):
            for zz in range(Z):
                for way, here in ((UP, zz <= z), (DOWN, zz >= z)):

                    @pl.when(exists[way] & here)
                    def _(way=way, zz=zz, c=c):
                        copy(way, zz * X + x, c).wait_send()

                for xx in range(X):
                    for way, here in ((RIGHT, xx <= x), (LEFT, xx >= x)):

                        @pl.when(exists[way] & here)
                        def _(way=way, zz=zz, xx=xx, c=c):
                            copy(way, zz * X + xx, c).wait_send()

    steps = []
    for c in range(chunks):
        steps.append((start + pace * c / chunks, functools.partial(first, c)))
    for d in range(1, Z):
        for c in range(chunks):
            steps.append((start + pace * (d + (c + 1) / chunks), functools.partial(hop, d, c)))
    for e in range(1, X):
        for dz in range(Z):
            level = lax.rem(z + dz, Z)
            for c in range(chunks):
                when = start + pace * (Z + e + (dz * chunks + c) / (Z * chunks))
                steps.append((when, functools.partial(across, e, level, c)))
    steps.append((start + pace * (Z + X + 1), finish))
    return steps


def scatter_slots(axis):
    Z, X = grid_of(axis)
    if X <= 2:
        return Z, Z
    return Z * X, Z * (X + 1)


def scatter_scratch(axis, chunks, rows, width, kind):
    Z, X = grid_of(axis)
    held, across = scatter_slots(axis)
    return [
        pltpu.VMEM((held, chunks, rows, width), kind),
        pltpu.VMEM((across, chunks, rows, width), kind),
        pltpu.VMEM((Z + 1, chunks, rows, width), kind),
        DMA((held,)),
        DMA((Z * X, chunks)),
        DMA((across, chunks)),
        DMA((Z, chunks)),
        DMA((Z + 1, chunks)),
    ]


STEP = 16


def scatter_steps(line, chunks, block, piece, scratch, store, done, start, pace):
    mine, from_x, from_z, load_sem, xs_sem, xr_sem, zs_sem, zr_sem = scratch
    Z, X, z, x = line.Z, line.X, line.z, line.x
    exists = line.exists
    rows = mine.shape[2]

    def spot(zz, xx):
        return zz if X <= 2 else zz * X + xx

    def load(zz, xx):
        at = spot(zz, xx)
        return pltpu.make_async_copy(block(zz * X + xx), mine.at[at], load_sem.at[at])

    def x_landing(zz, xx, right, receiver):
        if X <= 2:
            return zz
        return zz * (X + 1) + (xx if right else jnp.where(xx == receiver, X, xx))

    def x_copy(right, zz, xx, c):
        landing = x_landing(zz, xx, right, x + 1 if right else x - 1)
        src = piece(zz * X + xx, c) if X <= 2 else mine.at[spot(zz, xx), c]
        return remote(
            src,
            from_x.at[landing, c],
            xs_sem.at[zz * X + xx, c],
            xr_sem.at[landing, c],
            line.to(RIGHT if right else LEFT),
        )

    def z_copy(up, zz, c):
        landing = zz if up else jnp.where(zz == z - 1, Z, zz)
        return remote(
            mine.at[spot(zz, x), c],
            from_z.at[landing, c],
            zs_sem.at[zz, c],
            zr_sem.at[landing, c],
            line.to(UP if up else DOWN),
        )

    def wait_in(buffer, sem, at, c):
        in_place(buffer.at[at, c], sem.at[at, c]).wait()

    def add_in(at, buffer, landing, c):
        def body(i, carry):
            part = pl.ds(pl.multiple_of(i * STEP, STEP), STEP)
            mine[at, c, part] = (
                mine[at, c, part].astype(jnp.float32) + buffer[landing, c, part].astype(jnp.float32)
            ).astype(mine.dtype)
            return carry

        lax.fori_loop(0, rows // STEP, body, 0)

    def x_line(zz):
        for k in range(X - 1):
            for right, xx, here in ((True, X - 1 - k, X - 1 - k > x), (False, k, k < x)):

                @pl.when(here)
                def _(right=right, xx=xx):
                    if X > 2:
                        load(zz, xx).wait()
                    for c in range(chunks):
                        if X > 2:

                            @pl.when(exists[LEFT if right else RIGHT])
                            def _(c=c):
                                landing = x_landing(zz, xx, right, jnp.int32(-1))
                                wait_in(from_x, xr_sem, landing, c)
                                add_in(spot(zz, xx), from_x, landing, c)

                        x_copy(right, zz, xx, c).start()

    def x_join(zz, c):
        at = spot(zz, x)
        if X == 2:
            wait_in(from_x, xr_sem, zz, c)
            add_in(at, from_x, zz, c)
        elif X > 2:
            for right in (True, False):

                @pl.when(exists[LEFT if right else RIGHT])
                def _(right=right):
                    landing = zz * (X + 1) + (x if right else X)
                    wait_in(from_x, xr_sem, landing, c)
                    add_in(at, from_x, landing, c)

    def ways(k):
        return ((True, Z - 1 - k, Z - 1 - k > z), (False, k, k < z))

    def begin():
        for zz in range(Z):
            for xx in range(X):
                if X > 2:
                    load(zz, xx).start()
            if X <= 2:
                load(zz, x).start()
        for k in range(Z - 1):
            for up, zz, here in ways(k):

                @pl.when(here)
                def _(zz=zz):
                    x_line(zz)

        x_line(z)

    def pass_on(k, c):
        for up, zz, here in ways(k):

            @pl.when(here)
            def _(up=up, zz=zz):
                if c == 0:
                    load(zz, x).wait()
                x_join(zz, c)

                @pl.when(exists[DOWN if up else UP])
                def _():
                    wait_in(from_z, zr_sem, zz, c)
                    add_in(spot(zz, x), from_z, zz, c)

                z_copy(up, zz, c).start()

    def settle(c):
        if c == 0:
            load(z, x).wait()
        x_join(z, c)

        @pl.when(exists[DOWN])
        def _():
            wait_in(from_z, zr_sem, z, c)

        @pl.when(exists[UP])
        def _():
            wait_in(from_z, zr_sem, Z, c)

        def body(i, carry):
            part = pl.ds(pl.multiple_of(i * STEP, STEP), STEP)
            total = mine[spot(z, x), c, part].astype(jnp.float32)
            below = from_z[z, c, part].astype(jnp.float32)
            above = from_z[Z, c, part].astype(jnp.float32)
            total = total + jnp.where(z > 0, below, 0.0)
            total = total + jnp.where(z < Z - 1, above, 0.0)
            store(c, part, total)
            return carry

        lax.fori_loop(0, rows // STEP, body, 0)
        done(c)

    def finish():
        for zz in range(Z):
            for c in range(chunks):
                for xx in range(X):

                    @pl.when(xx != x)
                    def _(zz=zz, xx=xx, c=c):
                        x_copy(True, zz, xx, c).wait_send()

                @pl.when(zz != z)
                def _(zz=zz, c=c):
                    z_copy(True, zz, c).wait_send()

    steps = [(start, begin)]
    for k in range(Z - 1):
        for c in range(chunks):
            steps.append(
                (start + pace * (1 + k + (c + 1) / chunks), functools.partial(pass_on, k, c))
            )
    for c in range(chunks):
        steps.append((start + pace * (Z + (c + 1) / chunks), functools.partial(settle, c)))
    steps.append((start + pace * (Z + 2), finish))
    return steps


class Gather:
    def __init__(self, axis, block, chunks, start=0.0, pace=21.0):
        self.axis, self.chunks, self.start, self.pace = axis, chunks, start, pace
        self.inputs = [block]
        self.everyone = ()
        count = lax.axis_size(axis)
        self.outputs = [(ANY, jax.ShapeDtypeStruct((count,) + block.shape, block.dtype))]
        self.scratch = [DMA] + gather_sems(axis, chunks)

    def steps(self, lines, ins, outs, scratch):
        line, (x_ref,), (out_ref,) = lines[self.axis], ins, outs
        own_sem, *sems = scratch
        rows = x_ref.shape[0] // self.chunks
        own = pltpu.make_async_copy(x_ref, out_ref.at[line.me], own_sem)

        def part(c):
            return pl.ds(c * rows, rows)

        steps = gather_steps(
            line,
            self.chunks,
            lambda origin, c: out_ref.at[origin, part(c)],
            lambda c: x_ref.at[part(c)],
            lambda c: None,
            sems,
            self.start,
            self.pace,
        )
        return [(self.start, own.start)] + steps + [(steps[-1][0], own.wait)]


class Scatter:
    def __init__(self, axis, terms, chunks, start=0.0, pace=21.0):
        self.axis, self.chunks, self.start, self.pace = axis, chunks, start, pace
        count = lax.axis_size(axis)
        rows, width = terms.shape[0] // count // chunks, terms.shape[1]
        self.inputs = [terms.reshape(count, chunks, rows, width)]
        self.everyone = ()
        self.outputs = [(VMEM, jax.ShapeDtypeStruct((chunks * rows, width), jnp.float32))]
        self.scratch = scatter_scratch(axis, chunks, rows, width, terms.dtype)

    def steps(self, lines, ins, outs, scratch):
        (p_ref,), (out_ref,) = ins, outs
        rows = p_ref.shape[2]

        def store(c, part, total):
            out_ref[pl.ds(pl.multiple_of(c * rows + part.start, STEP), STEP)] = total

        return scatter_steps(
            lines[self.axis],
            self.chunks,
            lambda slot: p_ref.at[slot],
            lambda slot, c: p_ref.at[slot, c],
            scratch,
            store,
            lambda c: None,
            self.start,
            self.pace,
        )


class Spread:
    def __init__(self, weights, window, first, start=0.0, pace=6.0):
        self.inputs = list(weights)
        self.window, self.first, self.start, self.pace = window, first, start, pace
        self.everyone = ("shard",)
        shards, replicas = lax.axis_size("shard"), lax.axis_size("replica")
        self.part = weights[0].shape[0] // replicas
        wide = len(weights) * window
        shape = (shards, replicas, self.part, wide)
        self.outputs = [(ANY, jax.ShapeDtypeStruct(shape, weights[0].dtype))]
        self.scratch = [
            DMA((len(weights),)),
            DMA((len(weights), shards)),
            DMA((len(weights), shards)),
        ] + gather_sems("replica", shards)

    def steps(self, lines, ins, outs, scratch):
        own_sem, deal_send, deal_recv, *sems = scratch
        (out_ref,) = outs
        group, copies = lines["shard"], lines["replica"]
        rows = pl.ds(pl.multiple_of(copies.me * self.part, self.part), self.part)
        kinds = range(len(ins))

        def source(kind, target):
            return ins[kind].at[rows, pl.ds(pl.multiple_of(self.first(target), 128), self.window)]

        def landing(kind, origin):
            return out_ref.at[origin, copies.me, :, pl.ds(kind * self.window, self.window)]

        def own(kind):
            return pltpu.make_async_copy(
                source(kind, group.me), landing(kind, group.me), own_sem.at[kind]
            )

        def deal(kind, k):
            target = group.other(k)
            return remote(
                source(kind, target),
                landing(kind, group.me),
                deal_send.at[kind, k],
                deal_recv.at[kind, group.me],
                {"shard": target},
            )

        def begin():
            for k in range(1, group.count):
                for kind in kinds:
                    deal(kind, k).start()
            for kind in kinds:
                own(kind).start()

        def ready(c):
            @pl.when(c == group.me)
            def _():
                for kind in kinds:
                    own(kind).wait()

            @pl.when(c != group.me)
            def _():
                for kind in kinds:
                    in_place(landing(kind, c), deal_recv.at[kind, c]).wait()

        def finish():
            for k in range(1, group.count):
                for kind in kinds:
                    deal(kind, k).wait_send()

        steps = gather_steps(
            copies,
            group.count,
            lambda origin, c: out_ref.at[c, origin],
            lambda c: out_ref.at[c, copies.me],
            ready,
            sems,
            self.start + 2 * self.pace,
            self.pace,
        )
        return [(self.start, begin)] + steps + [(steps[-1][0], finish)]


class Collect:
    def __init__(self, terms, start=0.0, pace=6.0):
        shards, replicas = lax.axis_size("shard"), lax.axis_size("replica")
        part, wide = terms.shape[0] // shards // replicas, terms.shape[1]
        self.inputs = [terms.reshape(shards, replicas, part, wide)]
        self.start, self.pace = start, pace
        self.everyone = ("shard",)
        kind = terms.dtype
        self.outputs = [(ANY, jax.ShapeDtypeStruct((replicas, shards, part, wide), kind))]
        self.own_scratch = [
            pltpu.VMEM((shards, part, wide), kind),
            DMA,
            DMA((shards,)),
            DMA((shards,)),
        ] + gather_sems("replica", shards)
        self.scratch = self.own_scratch + scatter_scratch("replica", shards, part, wide, kind)

    def steps(self, lines, ins, outs, scratch):
        (p_ref,), (out_ref,) = ins, outs
        total_ref, own_sem, send_sem, recv_sem = scratch[:4]
        sems = scratch[4:6]
        group, copies = lines["shard"], lines["replica"]

        def own():
            return pltpu.make_async_copy(
                total_ref.at[group.me], out_ref.at[copies.me, group.me], own_sem
            )

        def deal(c):
            return remote(
                total_ref.at[c],
                out_ref.at[copies.me, group.me],
                send_sem.at[c],
                recv_sem.at[group.me],
                {"shard": jnp.int32(c)},
            )

        def store(c, part, total):
            total_ref[c, part] = total.astype(total_ref.dtype)

        def done(c):
            @pl.when(c == group.me)
            def _():
                own().start()

            @pl.when(c != group.me)
            def _():
                deal(c).start()

        def ready(c):
            @pl.when(c == group.me)
            def _():
                own().wait()

            @pl.when(c != group.me)
            def _():
                in_place(out_ref.at[copies.me, c], recv_sem.at[c]).wait()

        def finish():
            for c in range(group.count):

                @pl.when(c != group.me)
                def _(c=c):
                    deal(c).wait_send()

        summing = scatter_steps(
            copies,
            group.count,
            lambda slot: p_ref.at[:, slot],
            lambda slot, c: p_ref.at[c, slot],
            scratch[6:],
            store,
            done,
            self.start,
            self.pace,
        )
        again = self.start + self.pace * (copies.Z + 3)
        sharing = gather_steps(
            copies,
            group.count,
            lambda origin, c: out_ref.at[origin, c],
            lambda c: out_ref.at[copies.me, c],
            ready,
            sems,
            again,
            self.pace,
        )
        return summing + sharing + [(sharing[-1][0], finish)]


class Total:
    def __init__(self, terms, start=0.0, pace=6.0):
        replicas = lax.axis_size("replica")
        share, wide = terms.shape[0] // replicas, terms.shape[1]
        chunks = max(n for n in (1, 2, 3, 4) if share % (n * STEP) == 0)
        rows = share // chunks
        self.inputs = [terms.reshape(replicas, chunks, rows, wide)]
        self.start, self.pace, self.chunks = start, pace, chunks
        self.everyone = ()
        kind = terms.dtype
        self.outputs = [(ANY, jax.ShapeDtypeStruct((replicas, chunks, rows, wide), kind))]
        self.scratch = [pltpu.VMEM((chunks, rows, wide), kind), DMA((chunks,))]
        self.scratch += gather_sems("replica", chunks)
        self.scratch += scatter_scratch("replica", chunks, rows, wide, kind)

    def steps(self, lines, ins, outs, scratch):
        (p_ref,), (out_ref,) = ins, outs
        total_ref, own_sem = scratch[:2]
        copies = lines["replica"]

        def own(c):
            return pltpu.make_async_copy(
                total_ref.at[c], out_ref.at[copies.me, c], own_sem.at[c]
            )

        def store(c, part, total):
            total_ref[c, part] = total.astype(total_ref.dtype)

        def finish():
            for c in range(self.chunks):
                own(c).wait()

        summing = scatter_steps(
            copies,
            self.chunks,
            lambda slot: p_ref.at[slot],
            lambda slot, c: p_ref.at[slot, c],
            scratch[4:],
            store,
            lambda c: own(c).start(),
            self.start,
            self.pace,
        )
        sharing = gather_steps(
            copies,
            self.chunks,
            lambda origin, c: out_ref.at[origin, c],
            lambda c: total_ref.at[c],
            lambda c: None,
            scratch[2:4],
            self.start + self.pace * (copies.Z + 2),
            self.pace,
        )
        return summing + sharing + [(sharing[-1][0], finish)]


class Small:
    def __init__(self, dealt, shared, start=0.0):
        shards, replicas = lax.axis_size("shard"), lax.axis_size("replica")
        self.inputs = [dealt, shared]
        self.start = start
        self.everyone = ("shard", "replica")
        one = dealt.shape[1:]
        self.outputs = [
            (VMEM, jax.ShapeDtypeStruct(one, jnp.float32)),
            (VMEM, jax.ShapeDtypeStruct(shared.shape, jnp.float32)),
        ]
        self.scratch = [
            pltpu.VMEM((shards,) + one, jnp.float32),
            pltpu.VMEM((replicas,) + one, jnp.float32),
            pltpu.VMEM((replicas,) + shared.shape, jnp.float32),
            DMA((shards,)), DMA((shards,)),
            DMA((2, replicas)), DMA((2, replicas)), DMA((2,)),
        ]

    def steps(self, lines, ins, outs, scratch):
        dealt, shared = ins
        out_one, out_rows = outs
        got, got_one, got_rows, send, recv, send2, recv2, own = scratch
        group, copies = lines["shard"], lines["replica"]

        def deal(k):
            target = group.other(k)
            return remote(
                dealt.at[target], got.at[group.me], send.at[k], recv.at[group.me], {"shard": target}
            )

        def share(which, k):
            buffer = (got_one, got_rows)[which]
            return remote(
                buffer.at[copies.me] if which == 0 else shared,
                buffer.at[copies.me],
                send2.at[which, k],
                recv2.at[which, copies.me],
                {"replica": copies.other(k)},
            )

        def keep():
            return pltpu.make_async_copy(dealt.at[group.me], got.at[group.me], own.at[0])

        def keep_rows():
            return pltpu.make_async_copy(shared, got_rows.at[copies.me], own.at[1])

        def begin():
            keep().start()
            keep_rows().start()
            for k in range(1, group.count):
                deal(k).start()
            for k in range(1, copies.count):
                share(1, k).start()

        def middle():
            keep().wait()
            for k in range(1, group.count):
                origin = group.other(k)
                in_place(got.at[origin], recv.at[origin]).wait()
            total = got[0]
            for s in range(1, group.count):
                total = total + got[s]
            got_one[copies.me] = total
            for k in range(1, copies.count):
                share(0, k).start()

        def end():
            keep_rows().wait()
            for k in range(1, copies.count):
                origin = copies.other(k)
                in_place(got_one.at[origin], recv2.at[0, origin]).wait()
                in_place(got_rows.at[origin], recv2.at[1, origin]).wait()
            one, rows = got_one[0], got_rows[0]
            for r in range(1, copies.count):
                one, rows = one + got_one[r], rows + got_rows[r]
            out_one[...] = one
            out_rows[...] = rows
            for k in range(1, group.count):
                deal(k).wait_send()
            for k in range(1, copies.count):
                share(0, k).wait_send()
                share(1, k).wait_send()

        return [(self.start, begin), (self.start + 5.0, middle), (self.start + 10.0, end)]


def layout_of(tasks):
    inputs, outputs, scratch, spans = [], [], [], []
    for task in tasks:
        spans.append((len(inputs), len(outputs), len(scratch)))
        inputs += task.inputs
        outputs += task.outputs
        scratch += task.scratch
    return inputs, outputs, scratch, spans


def task_steps(tasks, spans, axes, ins, outs, scratch):
    lines = {axis: Lines(axis) for axis in axes}
    everyone = {axis for task in tasks for axis in task.everyone}
    steps = []
    for task, (i, o, s) in zip(tasks, spans):
        steps += task.steps(
            lines,
            ins[i : i + len(task.inputs)],
            outs[o : o + len(task.outputs)],
            scratch[s : s + len(task.scratch)],
        )
    steps.sort(key=lambda step: step[0])
    return [(-1.0, lambda: greet(list(lines.values()), everyone))] + steps


def exchange(tasks, axes, ident):
    inputs, outputs, scratch, spans = layout_of(tasks)

    def kernel(*refs):
        ins = refs[: len(inputs)]
        outs = refs[len(inputs) : len(inputs) + len(outputs)]
        rest = refs[len(inputs) + len(outputs) :]
        for _, step in task_steps(tasks, spans, axes, ins, outs, rest):
            step()

    return pl.pallas_call(
        kernel,
        in_specs=[ANY] * len(inputs),
        out_specs=[spec for spec, _ in outputs],
        out_shape=[shape for _, shape in outputs],
        scratch_shapes=scratch,
        compiler_params=pltpu.CompilerParams(
            collective_id=ident, has_side_effects=True, vmem_limit_bytes=60 * 1024 * 1024
        ),
    )(*inputs)


HD = 128
TAPS = 4
KINDS = 3


def dot_nn(a, b):
    return lax.dot_general(
        a.astype(jnp.bfloat16),
        b.astype(jnp.bfloat16),
        (((1,), (0,)), ((), ())),
        preferred_element_type=jnp.float32,
    )


def dot_nt(a, b):
    return lax.dot_general(
        a.astype(jnp.bfloat16),
        b.astype(jnp.bfloat16),
        (((1,), (1,)), ((), ())),
        preferred_element_type=jnp.float32,
    )


def dot_tn(a, b):
    return lax.dot_general(
        a.astype(jnp.bfloat16),
        b.astype(jnp.bfloat16),
        (((0,), (0,)), ((), ())),
        preferred_element_type=jnp.float32,
    )


def time_of(shape, dim, lanes):
    index = lax.broadcasted_iota(jnp.int32, shape, dim)
    return lax.rem(index, 8) * lanes + lax.div(index, 8)


def lower_inverses(lowers, lanes):
    size = lowers[0].shape[0]
    row_t = time_of((size, size), 0, lanes)
    col_t = time_of((size, size), 1, lanes)
    eye = jnp.where(row_t == col_t, 1.0, 0.0)

    def same(width):
        return lax.div(row_t, width) == lax.div(col_t, width)

    first = [jnp.where(same(8), a, 0.0) for a in lowers]
    second = [dot_nn(f, f) for f in first]
    inverse = [eye + f + s + dot_nn(f, s) for f, s in zip(first, second)]
    fourth = [dot_nn(s, s) for s in second]
    inverse = [t + dot_nn(t, f) for t, f in zip(inverse, fourth)]
    width = 16
    while width <= size:
        fresh = same(width) & jnp.logical_not(same(width // 2))
        left = [dot_nn(t, jnp.where(fresh, a, 0.0)) for t, a in zip(inverse, lowers)]
        inverse = [t + dot_nn(l, t) for t, l in zip(inverse, left)]
        width *= 2
    return inverse


def rounded(values):
    return values.astype(jnp.bfloat16).astype(jnp.float32)


def sigmoid(values):
    return 1.0 / (1.0 + jnp.exp(-values))


def unit_scale(pre):
    return lax.rsqrt(jnp.sum(pre * pre, axis=1, keepdims=True) + 1e-6)


def mean_scale(values):
    return lax.rsqrt(jnp.mean(values * values, axis=1, keepdims=True) + 1e-5)


def delta_forward(
    lanes, heads, group, proj_ref, taps_ref, gain_ref, low_ref, off_ref, rem_ref,
    zed_ref, mixed_ref, sums_ref, s_ref, t_ref, mk_ref, mv_ref, u_ref,
    state, last, unit,
):
    size = lanes * 8
    rows = group * 8
    wide = heads * HD
    scale = HD ** (-0.5)

    @pl.when(pl.program_id(0) == 0)
    def _():
        state[...] = jnp.zeros_like(state)
        last[...] = jnp.zeros_like(last)

    top = lax.broadcasted_iota(jnp.int32, (rows, HD), 0) == 0
    for kind in range(KINDS):
        for h in range(heads):
            cols = pl.ds(kind * wide + h * HD, HD)
            signal = [rounded(proj_ref[s, :, cols]) for s in range(lanes)]
            moved = {}
            for back in range(1, TAPS):
                lane = lanes - back
                edge = last[kind * heads + h, back, 0:1]
                moved[lane] = jnp.where(top, edge, pltpu.roll(signal[lane], 1, 0))
            for back in range(1, TAPS):
                last[kind * heads + h, back, 0:1] = signal[lanes - back][rows - 1 : rows]
            for s in range(lanes):
                off = off_ref[s]
                total = signal[s] * taps_ref[kind * TAPS : kind * TAPS + 1, h * HD : (h + 1) * HD]
                for hop in range(1, TAPS):
                    earlier = signal[s - hop] if s >= hop else moved[lanes + s - hop]
                    tap = taps_ref[kind * TAPS + hop : kind * TAPS + hop + 1, h * HD : (h + 1) * HD]
                    total = total + jnp.where(off >= hop, earlier, 0.0) * tap
                sums_ref[s, :, cols] = total
                pre = total * sigmoid(total)
                if kind < 2:
                    pre = pre * unit_scale(pre)
                unit[s, :, cols] = pre

    row_t = time_of((size, size), 0, lanes)
    col_t = time_of((size, size), 1, lanes)
    local_t = time_of((size, HD), 0, lanes).astype(jnp.float32)
    pairs = [(g, h) for g in range(group) for h in range(heads)]

    def span(g):
        return pl.ds(g * 8, 8)

    def flat(ref, g, first, count=HD):
        return ref[:, span(g), first : first + count].reshape(size, count)

    gates = {}
    for g in range(group):
        logits = flat(proj_ref, g, 4 * wide)
        strength = sigmoid(rounded(logits))
        for h in range(heads):
            gates[g, h] = jnp.broadcast_to(strength[:, h : h + 1], (size, HD))
    keys = {p: flat(unit, p[0], wide + p[1] * HD) for p in pairs}
    kbs = {p: gates[p] * keys[p] for p in pairs}
    lows = {g: low_ref[g].astype(jnp.float32) for g in range(group)}
    lowers = [
        -jnp.where(row_t == col_t, 0.0, lows[p[0]]) * dot_nt(kbs[p], keys[p]) for p in pairs
    ]
    inverses = dict(zip(pairs, lower_inverses(lowers, lanes)))
    mks = {p: dot_nn(inverses[p], kbs[p]) for p in pairs}
    mvs = {
        p: dot_nn(inverses[p], gates[p] * flat(unit, p[0], 2 * wide + p[1] * HD))
        for p in pairs
    }
    queries = {p: flat(unit, p[0], p[1] * HD) for p in pairs}
    scores = {p: lows[p[0]] * dot_nt(queries[p], keys[p]) for p in pairs}
    for g, h in pairs:
        t_ref[g, h] = inverses[g, h].astype(t_ref.dtype)
        mk_ref[g, h] = mks[g, h].astype(mk_ref.dtype)
        mv_ref[g, h] = mvs[g, h].astype(mv_ref.dtype)
    for g in range(group):
        carry = jnp.where(flat(off_ref, g, 0) > local_t, 1.0, 0.0)
        keep = jnp.where(flat(rem_ref, g, 0) + local_t >= size, 1.0, 0.0)
        for h in range(heads):
            p = (g, h)
            held = state[h]
            s_ref[g, h] = held.astype(s_ref.dtype)
            u = mvs[p] - carry * dot_nn(mks[p], held)
            u_ref[g, h] = u.astype(u_ref.dtype)
            state[h] = (carry[0:1] * keep[0:1]) * held + dot_tn(keys[p], keep * u)
            out = (carry * dot_nn(queries[p], held) + dot_nn(scores[p], u)) * scale
            mixed = rounded(out)
            gate = flat(proj_ref, g, 3 * wide + h * HD)
            zed = mixed * mean_scale(mixed) * gain_ref[...] * (gate * sigmoid(gate))
            mixed_ref[:, span(g), h * HD : (h + 1) * HD] = mixed.reshape(lanes, 8, HD).astype(
                mixed_ref.dtype
            )
            zed_ref[:, span(g), h * HD : (h + 1) * HD] = zed.reshape(lanes, 8, HD).astype(
                zed_ref.dtype
            )


def delta_backward(
    lanes, heads, group, proj_ref, sums_ref, mixed_ref, dzed_ref, taps_ref, gain_ref,
    low_ref, off_ref, rem_ref, s_ref, t_ref, mk_ref, mv_ref, u_ref,
    dproj_ref, gtaps_ref, ghead_ref,
    state, edge, edge_off, errs, taps_sum, head_sum,
):
    size = lanes * 8
    rows = group * 8
    wide = heads * HD
    scale = HD ** (-0.5)

    @pl.when(pl.program_id(0) == 0)
    def _():
        state[...] = jnp.zeros_like(state)
        edge[...] = jnp.zeros_like(edge)
        edge_off[...] = jnp.zeros_like(edge_off)
        taps_sum[...] = jnp.zeros_like(taps_sum)
        head_sum[...] = jnp.zeros_like(head_sum)

    row_t = time_of((size, size), 0, lanes)
    col_t = time_of((size, size), 1, lanes)
    local_t = time_of((size, HD), 0, lanes).astype(jnp.float32)
    lane_id = lax.broadcasted_iota(jnp.int32, (size, HD), 1)
    pairs = [(g, h) for g in range(group) for h in range(heads)]

    def span(g):
        return pl.ds(g * 8, 8)

    def flat(ref, g, first, count=HD):
        return ref[:, span(g), first : first + count].reshape(size, count)

    def put(ref, g, first, value):
        ref[:, span(g), first : first + HD] = value.reshape(lanes, 8, HD).astype(ref.dtype)

    gain = gain_ref[...]
    d_out, q, k, v, beta = {}, {}, {}, {}, {}
    pre, scales, slopes = {}, {}, {}
    head_total = jnp.zeros((size, HD), jnp.float32)
    strengths = {}
    carries, keeps, lows = {}, {}, {}
    for g in range(group):
        carries[g] = jnp.where(flat(off_ref, g, 0) > local_t, 1.0, 0.0)
        keeps[g] = jnp.where(flat(rem_ref, g, 0) + local_t >= size, 1.0, 0.0)
        lows[g] = low_ref[g].astype(jnp.float32)
        strengths[g] = sigmoid(rounded(flat(proj_ref, g, 4 * wide)))
    for g, h in pairs:
        p = (g, h)
        mixed = flat(mixed_ref, g, h * HD).astype(jnp.float32)
        gate = flat(proj_ref, g, 3 * wide + h * HD)
        dzed = flat(dzed_ref, g, h * HD)
        s = sigmoid(gate)
        r = mean_scale(mixed)
        through = dzed * (gate * s)
        head_total = head_total + through * mixed * r
        inner = jnp.mean(mixed * gain * through, axis=1, keepdims=True)
        d_mixed = rounded(r * gain * through - mixed * (r * r * r) * inner)
        put(dproj_ref, g, 3 * wide + h * HD, dzed * (mixed * r * gain) * (s * (1.0 + gate * (1.0 - s))))
        d_out[p] = d_mixed * scale
        for kind, store in ((0, q), (1, k), (2, v)):
            total = flat(sums_ref, g, kind * wide + h * HD)
            s = sigmoid(total)
            value = total * s
            slopes[kind, g, h] = s * (1.0 + total * (1.0 - s))
            if kind < 2:
                pre[kind, g, h] = value
                scales[kind, g, h] = unit_scale(value)
                value = value * scales[kind, g, h]
            store[p] = value
        beta[p] = jnp.broadcast_to(strengths[g][:, h : h + 1], (size, HD))
    head_sum[...] += head_total

    scores = {p: lows[p[0]] * dot_nt(q[p], k[p]) for p in pairs}
    du = {p: dot_tn(scores[p], d_out[p]) for p in pairs}
    ds = {p: lows[p[0]] * dot_nt(d_out[p], u_ref[p[0], p[1]]) for p in pairs}
    cdo = {p: carries[p[0]] * d_out[p] for p in pairs}
    dq = {p: dot_nt(cdo[p], s_ref[p[0], p[1]]) + dot_nn(ds[p], k[p]) for p in pairs}
    dk = {p: dot_tn(ds[p], q[p]) for p in pairs}
    lift = {p: dot_tn(q[p], cdo[p]) for p in pairs}
    later = {}
    for g in reversed(range(group)):
        for h in range(heads):
            p = (g, h)
            later[p] = state[h]
            du[p] = du[p] + keeps[g] * dot_nn(k[p], later[p])
            mk = carries[g] * mk_ref[g, h].astype(jnp.float32)
            state[h] = (carries[g][0:1] * keeps[g][0:1]) * later[p] + lift[p] - dot_tn(mk, du[p])
    for p in pairs:
        dk[p] = dk[p] + dot_nt(keeps[p[0]] * u_ref[p[0], p[1]].astype(jnp.float32), later[p])
    dmk = {p: -carries[p[0]] * dot_nt(du[p], s_ref[p[0], p[1]]) for p in pairs}
    xx = {p: dot_tn(t_ref[p[0], p[1]], dmk[p]) for p in pairs}
    yy = {p: dot_tn(t_ref[p[0], p[1]], du[p]) for p in pairs}
    da = {
        p: jnp.where(row_t == col_t, 0.0, lows[p[0]])
        * (dot_nt(xx[p], mk_ref[p[0], p[1]]) + dot_nt(yy[p], mv_ref[p[0], p[1]]))
        for p in pairs
    }
    dkb = {p: xx[p] - dot_nn(da[p], k[p]) for p in pairs}
    dk = {p: dk[p] - dot_tn(da[p], beta[p] * k[p]) + beta[p] * dkb[p] for p in pairs}
    for g in range(group):
        d_logits = jnp.zeros((size, HD), jnp.float32)
        for h in range(heads):
            p = (g, h)
            db = jnp.sum(dkb[p] * k[p] + yy[p] * v[p], axis=1, keepdims=True)
            d_logits = d_logits + jnp.where(lane_id == h, db * beta[p] * (1.0 - beta[p]), 0.0)
            for kind, grad in ((0, dq[p]), (1, dk[p])):
                r, raw = scales[kind, g, h], pre[kind, g, h]
                inner = jnp.sum(raw * grad, axis=1, keepdims=True)
                err = (r * grad - raw * (r * r * r) * inner) * slopes[kind, g, h]
                put(errs, g, kind * wide + h * HD, err)
            put(errs, g, 2 * wide + h * HD, beta[p] * yy[p] * slopes[2, g, h])
        put(dproj_ref, g, 4 * wide, d_logits)

    bottom = lax.broadcasted_iota(jnp.int32, (rows, HD), 0) == rows - 1
    for kind in range(KINDS):
        for h in range(heads):
            at = kind * wide + h * HD
            cols = pl.ds(at, HD)
            err = [errs[s, :, cols] for s in range(lanes)]
            taps = [
                taps_ref[kind * TAPS + hop : kind * TAPS + hop + 1, h * HD : (h + 1) * HD]
                for hop in range(TAPS)
            ]
            sums = [jnp.zeros((rows, HD), jnp.float32) for _ in range(TAPS)]
            live = {}
            for hop in range(1, TAPS):
                for s in range(lanes):
                    live[hop, s] = jnp.where(off_ref[s] >= hop, err[s], 0.0)
            for hop in range(1, TAPS):
                for s in range(hop):
                    row = jnp.where(edge_off[s, 0:1] >= hop, edge[kind * heads + h, s, 0:1], 0.0)
                    live[hop, lanes + s] = jnp.where(
                        bottom, row, pltpu.roll(live[hop, s], rows - 1, 0)
                    )
            for s in range(lanes):
                signal = rounded(proj_ref[s, :, cols])
                total = err[s] * taps[0]
                sums[0] = sums[0] + err[s] * signal
                for hop in range(1, TAPS):
                    total = total + live[hop, s + hop] * taps[hop]
                    sums[hop] = sums[hop] + live[hop, s + hop] * signal
                dproj_ref[s, :, cols] = total.astype(dproj_ref.dtype)
            for s in range(TAPS - 1):
                edge[kind * heads + h, s, 0:1] = err[s][0:1]
            for hop in range(TAPS):
                folded = sums[hop].reshape(group, 8, HD)
                taps_sum[kind * TAPS + hop, :, h * HD : (h + 1) * HD] += jnp.sum(folded, axis=0)
    for s in range(TAPS - 1):
        edge_off[s, 0:1] = off_ref[s][0:1]

    @pl.when(pl.program_id(0) == pl.num_programs(0) - 1)
    def _():
        gtaps_ref[...] = jnp.sum(taps_sum[...], axis=1)
        ghead_ref[...] = jnp.sum(head_sum[...], axis=0, keepdims=True)


def mixer_specs(lanes, heads, group, flip):
    size = lanes * 8
    at = (lambda i: flip - 1 - i) if flip else (lambda i: i)

    def token(width):
        return pl.BlockSpec((lanes, 8 * group, width), lambda i: (0, at(i), 0))

    def saved(first, second):
        return pl.BlockSpec((group, heads, first, second), lambda i: (at(i), 0, 0, 0))

    square = pl.BlockSpec((group, size, size), lambda i: (at(i), 0, 0))
    return token, saved, square


def fixed(shape):
    return pl.BlockSpec(shape, lambda i: (0,) * len(shape))


def saved_shapes(lanes, heads, blocks):
    size = lanes * 8
    kind = jnp.bfloat16
    return [
        jax.ShapeDtypeStruct((blocks, heads, HD, HD), kind),
        jax.ShapeDtypeStruct((blocks, heads, size, size), kind),
        jax.ShapeDtypeStruct((blocks, heads, size, HD), kind),
        jax.ShapeDtypeStruct((blocks, heads, size, HD), kind),
        jax.ShapeDtypeStruct((blocks, heads, size, HD), kind),
    ]


def mixer_forward(proj, taps, gain, low, off, rem, heads, group=4):
    lanes, tokens, width = proj.shape
    blocks, wide = tokens // 8, heads * HD
    size = lanes * 8
    token, saved, square = mixer_specs(lanes, heads, group, 0)
    return pl.pallas_call(
        functools.partial(delta_forward, lanes, heads, group),
        grid=(blocks // group,),
        in_specs=[token(width), fixed(taps.shape), fixed(gain.shape), square, token(HD), token(HD)],
        out_specs=[
            token(wide), token(wide), token(KINDS * wide),
            saved(HD, HD), saved(size, size), saved(size, HD), saved(size, HD), saved(size, HD),
        ],
        out_shape=[
            jax.ShapeDtypeStruct((lanes, tokens, wide), jnp.bfloat16),
            jax.ShapeDtypeStruct((lanes, tokens, wide), jnp.bfloat16),
            jax.ShapeDtypeStruct((lanes, tokens, KINDS * wide), jnp.float32),
        ] + saved_shapes(lanes, heads, blocks),
        scratch_shapes=[
            pltpu.VMEM((heads, HD, HD), jnp.float32),
            pltpu.VMEM((KINDS * heads, TAPS, 8, HD), jnp.float32),
            pltpu.VMEM((lanes, 8 * group, KINDS * wide), jnp.float32),
        ],
        compiler_params=pltpu.CompilerParams(vmem_limit_bytes=48 * 1024 * 1024),
    )(proj, taps, gain, low, off, rem)


def mixer_backward(
    proj, sums, mixed, dzed, taps, gain, low, off, rem, saves, heads, group=4
):
    lanes, tokens, width = proj.shape
    blocks, wide = tokens // 8, heads * HD
    size = lanes * 8
    token, saved, square = mixer_specs(lanes, heads, group, blocks // group)
    return pl.pallas_call(
        functools.partial(delta_backward, lanes, heads, group),
        grid=(blocks // group,),
        in_specs=[
            token(width), token(KINDS * wide), token(wide), token(wide),
            fixed(taps.shape), fixed(gain.shape), square, token(HD), token(HD),
            saved(HD, HD), saved(size, size), saved(size, HD), saved(size, HD), saved(size, HD),
        ],
        out_specs=[token(width), fixed(taps.shape), fixed(gain.shape)],
        out_shape=[
            jax.ShapeDtypeStruct((lanes, tokens, width), jnp.bfloat16),
            jax.ShapeDtypeStruct(taps.shape, jnp.float32),
            jax.ShapeDtypeStruct(gain.shape, jnp.float32),
        ],
        scratch_shapes=[
            pltpu.VMEM((heads, HD, HD), jnp.float32),
            pltpu.VMEM((KINDS * heads, TAPS, 8, HD), jnp.float32),
            pltpu.VMEM((TAPS, 8, HD), jnp.float32),
            pltpu.VMEM((lanes, 8 * group, KINDS * wide), jnp.float32),
            pltpu.VMEM((taps.shape[0], 8, wide), jnp.float32),
            pltpu.VMEM((size, HD), jnp.float32),
        ],
        compiler_params=pltpu.CompilerParams(vmem_limit_bytes=48 * 1024 * 1024),
    )(proj, sums, mixed, dzed, taps, gain, low, off, rem, *saves)


def segment_masks(lengths_grid, order_row, lanes, tokens):
    slots = order_row.shape[0]
    flat = lengths_grid.reshape(slots)
    first = lax.broadcasted_iota(jnp.int32, (slots, slots), 0)
    second = lax.broadcasted_iota(jnp.int32, (slots, slots), 1)
    run_len = jnp.sum(jnp.where(order_row[:, None] == second, flat[None, :], 0), axis=1)
    ends = jnp.sum(jnp.where(first >= second, run_len[None, :], 0), axis=1)
    starts = ends - run_len
    size = lanes * 8
    blocks = tokens // 8
    lane = lax.broadcasted_iota(jnp.int32, (lanes, tokens), 0)
    step = lax.broadcasted_iota(jnp.int32, (lanes, tokens), 1)
    place = step * lanes + lane
    inside = (starts[:, None, None] <= place[None]) & (place[None] < ends[:, None, None])
    start_at = jnp.sum(jnp.where(inside, starts[:, None, None], 0), axis=0)
    end_at = jnp.sum(jnp.where(inside, ends[:, None, None], 0), axis=0)

    def blocked(values):
        return values.reshape(lanes, blocks, 8).transpose(1, 0, 2).reshape(blocks, size)

    start_b, place_b = blocked(start_at), blocked(place)
    low = (start_b[:, :, None] == start_b[:, None, :]) & (place_b[:, :, None] >= place_b[:, None, :])

    def spread(values):
        return jnp.broadcast_to(values.astype(jnp.float32)[:, :, None], (lanes, tokens, HD))

    return low.astype(jnp.bfloat16), spread(place - start_at), spread(end_at - place)


def project(left_side, right_side):
    return jnp.dot(left_side, right_side, preferred_element_type=jnp.float32)


def times_t(left_side, right_side):
    return lax.dot_general(
        left_side, right_side, (((1,), (1,)), ((), ())), preferred_element_type=jnp.float32
    )


def contract_rows(left_side, right_side):
    return lax.dot_general(
        left_side, right_side, (((0,), (0,)), ((), ())), preferred_element_type=jnp.float32
    )


def rms(values, gain, eps):
    return values * lax.rsqrt(jnp.mean(values * values, axis=-1, keepdims=True) + eps) * gain


def rms_back(values, gain, eps, grad):
    r = lax.rsqrt(jnp.mean(values * values, axis=-1, keepdims=True) + eps)
    inner = jnp.mean(values * gain * grad, axis=-1, keepdims=True)
    return r * gain * grad - values * (r * r * r) * inner, grad * values * r


def column_windows(columns, shards):
    own = columns // shards
    tiles = columns // HD
    width = 1
    while any(min(s * own // HD, tiles - width) * HD + width * HD < (s + 1) * own for s in range(shards)):
        width += 1

    def first(s):
        if isinstance(s, int):
            return min(s * own // HD, tiles - width) * HD
        return jnp.minimum(lax.div(s * own, HD), tiles - width) * HD

    return first, width * HD


def place_windows(kinds, shards, columns, window, first, own, in_ref, *out_refs):
    for kind, out_ref in zip(range(kinds), out_refs):
        for tile in range(columns // HD):
            total = None
            for s in range(shards):
                low = max(tile * HD, s * own)
                high = min((tile + 1) * HD, (s + 1) * own)
                if low < high:
                    at = kind * window + tile * HD - first(s)
                    term = in_ref[0, s, :, at : at + HD].astype(jnp.float32)
                    total = term if total is None else total + term
            out_ref[:, tile * HD : (tile + 1) * HD] = total


def widen(collected, kinds, columns, window, first):
    replicas, shards, part, wide = collected.shape
    return pl.pallas_call(
        functools.partial(place_windows, kinds, shards, columns, window, first, columns // shards),
        grid=(replicas,),
        in_specs=[pl.BlockSpec((1, shards, part, wide), lambda i: (i, 0, 0, 0))],
        out_specs=[pl.BlockSpec((part, columns), lambda i: (i, 0))] * kinds,
        out_shape=[jax.ShapeDtypeStruct((replicas * part, columns), jnp.float32)] * kinds,
        compiler_params=pltpu.CompilerParams(vmem_limit_bytes=48 * 1024 * 1024),
    )(collected)


def body(
    layer_input,
    out_cotangent,
    seq_lengths,
    seq_order,
    w_query,
    w_key,
    w_value,
    w_beta,
    w_outgate,
    w_output,
    conv_query,
    conv_key,
    conv_value,
    attn_gain,
    head_gain,
    mlp_gain,
    w_gate,
    w_up,
    w_down,
):
    bf16, f32 = jnp.bfloat16, jnp.float32
    shards = lax.axis_size("shard")
    shard = lax.axis_index("shard")
    both, group = ("shard", "replica"), ("shard",)
    rows, width = layer_input.shape
    tokens = shards * rows
    weight_rows = w_query.shape[0]
    own = w_output.shape[0]
    heads = own // HD
    hidden_own = w_down.shape[0]
    ffn = w_gate.shape[1]
    ffn_first, ffn_window = column_windows(ffn, shards)
    col_first, col_window = column_windows(width, shards)
    shift = shard * hidden_own - ffn_first(shard)

    total_heads = w_beta.shape[1]
    head_part = jnp.pad(head_gain, (0, weight_rows - head_gain.shape[0]))
    little = jnp.concatenate([w_beta, jnp.stack([attn_gain, mlp_gain, head_part], axis=1)], axis=1)
    little = jnp.pad(little, ((0, 0), (0, HD - little.shape[1])))
    attn_weights, all_source, little = exchange(
        [
            Spread((w_query, w_key, w_value, w_outgate), col_window, col_first, -0.5, 12.0),
            Gather("shard", layer_input, 4),
            Gather("shard", little, 1, 0.0, 20.0),
        ],
        both,
        0,
    )
    mlp_weights, dy = exchange(
        [
            Spread((w_gate, w_up), ffn_window, ffn_first, -0.5, 16.0),
            Gather("shard", out_cotangent, 4),
        ],
        both,
        1,
    )
    dy = dy.reshape(tokens, width)
    mlp_weights = mlp_weights.reshape(width, 2 * ffn_window)
    full_attn_gain = little[:, :, total_heads].reshape(width).astype(f32)
    full_mlp_gain = little[:, :, total_heads + 1].reshape(width).astype(f32)
    head_row = little[:, : head_gain.shape[0], total_heads + 2].reshape(1, HD).astype(f32)
    beta = lax.dynamic_slice_in_dim(little.reshape(width, HD), shard * heads, heads, axis=1)
    attn_weights = jnp.concatenate(
        [attn_weights.reshape(width, 4 * own), jnp.pad(beta, ((0, 0), (0, HD - heads)))], axis=1
    )
    low, off, rem = segment_masks(seq_lengths[0], seq_order[0], shards, rows)

    source = layer_input.astype(f32)
    all_source = all_source.reshape(tokens, width).astype(f32)
    normed = rms(all_source, full_attn_gain, 1e-6).astype(bf16)
    projected = project(normed, attn_weights).reshape(shards, rows, -1)
    taps = jnp.concatenate([conv_query, conv_key, conv_value], axis=0).astype(f32)
    zed, mixed, sums, *saves = mixer_forward(projected, taps, head_row, low, off, rem, heads)
    zed = zed.reshape(tokens, own)
    (hidden,) = exchange([Scatter("shard", project(zed, w_output).astype(bf16), 4)], group, 2)
    hidden = source + hidden

    (mlp_in,) = exchange(
        [Gather("shard", rms(hidden, full_mlp_gain, 1e-6).astype(bf16), 4)], group, 3
    )
    mlp_in = mlp_in.reshape(tokens, width)
    w_down = lax.dynamic_update_slice(jnp.zeros((ffn_window, width), bf16), w_down, (shift, 0))
    lin = project(mlp_in, mlp_weights)
    gate_lin, up_lin = lin[:, :ffn_window], lin[:, ffn_window:]
    s = jax.nn.sigmoid(gate_lin)
    product = (gate_lin * s * up_lin).astype(bf16)
    d_product = times_t(dy, w_down)
    d_gate = (d_product * up_lin * s * (1.0 + gate_lin * (1.0 - s))).astype(bf16)
    d_up = (d_product * gate_lin * s).astype(bf16)
    d_lin = jnp.concatenate([d_gate, d_up], axis=1)
    g_down = contract_rows(product, dy).astype(bf16)
    g_lin = contract_rows(mlp_in, d_lin).astype(bf16)
    d_mlp_in, g_lin, g_down = exchange(
        [
            Scatter("shard", times_t(d_lin, mlp_weights).astype(bf16), 4),
            Collect(g_lin, 0.5, 13.0),
            Total(g_down, 0.7, 13.0),
        ],
        both,
        4,
    )
    d_hidden_norm, g_mlp_rows = rms_back(hidden, full_mlp_gain, 1e-6, d_mlp_in)
    d_hidden = out_cotangent.astype(f32) + d_hidden_norm

    (d_attn,) = exchange([Gather("shard", d_hidden.astype(bf16), 4)], group, 5)
    d_attn = d_attn.reshape(tokens, width)
    g_output = contract_rows(zed, d_attn).astype(bf16)
    out_terms, g_output = exchange(
        [Scatter("shard", project(product, w_down).astype(bf16), 4), Total(g_output, 0.5, 10.0)],
        both,
        6,
    )
    d_zed = times_t(d_attn, w_output).reshape(shards, rows, own)
    d_proj, g_taps, g_head = mixer_backward(
        projected, sums, mixed, d_zed, taps, head_row, low, off, rem, saves, heads
    )
    d_proj = d_proj.reshape(tokens, -1)
    g_proj = contract_rows(normed, d_proj).astype(bf16)
    d_normed, g_proj = exchange(
        [Scatter("shard", times_t(d_proj, attn_weights).astype(bf16), 4), Collect(g_proj, 0.5, 10.0)],
        both,
        7,
    )
    d_source, g_attn_rows = rms_back(source, full_attn_gain, 1e-6, d_normed)

    def dealt(values):
        return values.reshape(shards, -1)

    small = jnp.concatenate(
        [dealt(jnp.sum(g_attn_rows, axis=0)), dealt(jnp.sum(g_mlp_rows, axis=0)), dealt(g_head)], axis=1
    )
    small = jnp.pad(small, ((0, 0), (0, -small.shape[1] % HD)))
    small = jnp.broadcast_to(small[:, None, :], (shards, 8, small.shape[1]))
    small, g_taps = exchange(
        [Small(small, jnp.pad(g_taps, ((0, 16 - g_taps.shape[0]), (0, 0))))], both, 8
    )
    g_query, g_key, g_value, g_outgate = widen(g_proj, 4, width, col_window, col_first)
    g_gate, g_up = widen(g_lin, 2, ffn, ffn_window, ffn_first)
    g_beta = g_proj[..., 4 * own : 4 * own + heads].transpose(0, 2, 1, 3)
    g_down = lax.dynamic_slice_in_dim(g_down.reshape(-1, width), shift, hidden_own)
    gains = width // shards
    return (
        (hidden + out_terms).astype(bf16),
        (d_hidden + d_source).astype(bf16),
        g_query,
        g_key,
        g_value,
        g_beta.reshape(weight_rows, total_heads).astype(f32),
        g_outgate,
        g_output.reshape(own, width).astype(f32),
        g_taps[:TAPS],
        g_taps[TAPS : 2 * TAPS],
        g_taps[2 * TAPS : 3 * TAPS],
        small[0, :gains],
        small[0, 2 * gains : 2 * gains + head_gain.shape[0]],
        small[0, gains : 2 * gains],
        g_gate,
        g_up,
        g_down.astype(f32),
    )


def solution(mesh):
    tokens = P(("replica", "shard"), None)
    whole, columns, vector = P("shard", None), P(None, "shard"), P("shard")
    in_specs = (tokens, tokens, P("replica", None, None), P("replica", None)) + (whole,) * 6
    in_specs += (columns,) * 3 + (vector,) * 3 + (whole,) * 3
    out_specs = (tokens, tokens) + (whole,) * 6 + (columns,) * 3 + (vector,) * 3 + (whole,) * 3
    return jax.shard_map(body, mesh=mesh, in_specs=in_specs, out_specs=out_specs, check_vma=False)
```

time: 1990 us -> 1230 us (0.62)
  local copies, waits for them, and re-layouts: 393 us -> 20.7 us
  other arithmetic: 182 us -> 37.6 us
  Pallas kernels: 1130 us -> 1000 us
  blocking collectives: 107 us -> 0 us
    pallas_call x1, Pallas kernels: 109 us -> 30.3 us  [mixer_forward(): pl.pallas_call(functools.partial(delta_forward, lanes, heads, group), gri...]
    slice x51 -> x2, local copies, waits for them, and re-layouts: 76.6 us -> 2.66 us  [the longest x1 1.38 us: body(): g_taps[2 * TAPS:3 * TAPS]]
    unnamed x339 -> x87, local copies, waits for them, and re-layouts: 67.1 us -> 5.82 us
    psum x2 -> x0, blocking collectives: 55.9 us -> none  [the longest x1 44.6 us: small(): total = lax.psum(values.astype(f32), ('replica', 'shard'))]
    reduce_sum x9 -> x2, other arithmetic: 52.9 us -> 0.3 us  [the longest x1 0.18 us: segment_masks(): jnp.sum(jnp.where(order_row[:, None] == second, flat[None, :], 0), axis=1)]
    mul x15 -> x0, local copies, waits for them, and re-layouts: 50.6 us -> none  [the longest x6 25.4 us: unit_back(): split * (inverse * inverse * inverse) * inner]
    convert_element_type x13 -> x3, local copies, waits for them, and re-layouts: 48.5 us -> 1.16 us  [the longest x2 1.08 us: body(): g_beta.reshape(weight_rows, total_heads).astype(f32)]
    convert_element_type x15 -> x11, other arithmetic: 60.6 us -> 20.7 us  [the longest x1 4.15 us: body(): (d_hidden + d_source).astype(bf16)]
  transfers between devices with their start and end apart: 3 -> 0, of which waited for: 0 -> 0; matrix products, arithmetic and copies ran while one was open for 20% -> 0% of each run, Pallas kernels for 33% -> 0%
where the time goes in v2:
time: 1230 us; the launch traced here: 1220 us
  Pallas kernels  1000 us (81%)
  matrix products  159 us (13%)
  other arithmetic  37.6 us (3%)
  local copies, waits for them, and re-layouts  20.7 us (2%)
    pallas_call x9, Pallas kernels, exchange(): pl.pallas_call(kernel, in_specs=[ANY] * len(inputs), out_specs=[spec for...  930 us
    dot_general x4, matrix products, times_t(): lax.dot_general(left_side, right_side, (((1,), (1,)), ((), ())), preferre...  57.3 us
    dot_general x4, matrix products, contract_rows(): lax.dot_general(left_side, right_side, (((0,), (0,)), ((), ())), preferre...  52 us
    dot_general x4, matrix products, project(): return jnp.dot(left_side, right_side, preferred_element_type=jnp.float32)  49.7 us
    pallas_call x1, Pallas kernels, mixer_backward(): pl.pallas_call(functools.partial(delta_backward, lanes, heads, group), gr...  32.8 us
    pallas_call x1, Pallas kernels, mixer_forward(): pl.pallas_call(functools.partial(delta_forward, lanes, heads, group), gri...  30.3 us

profile of v2, /device:TPU:0, one launch (start us, length us, event | category | flops | bytes accessed | tf_op | source)
XLA Modules:
  0.0 1223.0 jit_solution(14933995500773744709)
XLA Ops:
  4.2 118.0 %shard_map.314 = (bf16[8,4,64,1024]{3,2,1,0:T(8,128)(2,1)}, bf16[8,256,2048]{2,1,0:T(8,128)(2,1)}, bf16[8,256,128]{2,1,0:T(8,128)(2,1)}) custom-call(bf16[256,2048]{1,0:T(8,128)(2,1)} %refs_0_.2, bf16[256,2048]{1,0:T(8,128)(2,1)} %refs_1_.2, bf16[256,2048]{1,0:T(8,128)(2,1)} %refs_2_.2, bf16[256,2048]{1,0:T(8,128)(2,1)} %refs_3_.1, ...), custom_call_target="tpu_custom_call" | custom-call | tf_op jit(solution)/shard_map/pallas_call | solution.py:771
  125.6 5.7 fusion
  132.0 16.0 %fusion.5.proj_ref = f32[8,256,1152]{2,1,0:T(8,128)} fusion(bf16[8,256,2048]{2,1,0:T(8,128)(2,1)S(1)} %copy-done.15, f32[2048]{0:T(1024)S(1)} %bitcast.87, f32[8,256]{1,0:T(8,128)S(1)} %add_rsqrt_fusion, bf16[2048,2]{1,0:T(8,128)(2,1)S(1)} %constant_dynamic-slice_fusion, bf16[2048,1024]{1,0:T(8,128)(2,1)} %bitcast.100), kind=kOutput, calls=%fused_computation.13 | convolution fusion | flops 9694609408 | bytes 22044672 | tf_op jit(solution)/shard_map/dot_general | solution.py:1231
  153.5 30.3 %shard_map.315 = (bf16[8,256,256]{2,1,0:T(8,128)(2,1)S(1)}, bf16[8,256,256]{2,1,0:T(8,128)(2,1)S(1)}, f32[8,256,768]{2,1,0:T(8,128)}, bf16[32,2,128,128]{3,2,1,0...) custom-call(f32[8,256,1152]{2,1,0:T(8,128)} %fusion.5.proj_ref, ...), custom_call_target="tpu_custom_call" | custom-call | tf_op jit(solution)/shard_map/pallas_call | solution.py:1146
  189.4 95.2 %shard_map.316 = f32[256,2048]{1,0:T(8,128)} custom-call(bf16[8,4,64,2048]{3,2,1,0:T(8,128)(2,1)} %bitcast.66), custom_call_target="tpu_custom_call" | custom-call | tf_op jit(solution)/shard_map/pallas_call | solution.py:771
  289.6 93.5 %shard_map.317 = bf16[8,256,2048]{2,1,0:T(8,128)(2,1)} custom-call(bf16[256,2048]{1,0:T(8,128)(2,1)} %multiply_convert_fusion.3.refs_0_), custom_call_target="tpu_custom_call" | custom-call | tf_op jit(solution)/shard_map/pallas_call | solution.py:771
  383.1 112.3 %shard_map.318 = (bf16[8,4,64,1536]{3,2,1,0:T(8,128)(2,1)}, bf16[8,256,2048]{2,1,0:T(8,128)(2,1)}) custom-call(bf16[256,5632]{1,0:T(8,128)(2,1)} %refs_0_.3, bf16[256,5632]{1,0:T(8,128)(2,1)} %refs_1_.3, bf16[256,2048]{1,0:T(8,128)(2,1)} %refs_2_.3), custom_call_target="tpu_custom_call" | custom-call | tf_op jit(solution)/shard_map/pallas_call | solution.py:771
  495.3 19.0 %fusion.34 = f32[2048,1536]{0,1:T(8,128)} fusion(bf16[2048,2048]{1,0:T(8,128)(2,1)} %bitcast.69, bf16[2048,1536]{1,0:T(8,128)(2,1)} %bitcast.97), kind=kOutput, calls=%fused_computation.93 | convolution fusion | flops 12884901888 | bytes 27262976 | tf_op jit(solution)/shard_map/dot_general | solution.py:1231
  516.6 17.9 %multiply_convert_fusion.1 = (bf16[2048,768]{0,1:T(8,128)(2,1)}, bf16[2048,768]{0,1:T(8,128)(2,1)}, bf16[2048,768]{0,1:T(8,128)(2,1)}) fusion(f32[2048,1536]{0,1:T(8,128)} %fusion.34, bf16[2048,2048]{1,0:T(8,128)(2,1)} %bitcast.95, bf16[768,2048]{1,0:T(8,128)(2,1)S(1)} %constant_dynamic-update-slice_fusion), kind=kOutput, calls=%fused_computation.16 | convolution fusion | flops 6467616768 | bytes 33554432 | tf_op jit(solution)/shard_map/dot_general | solution.py:1235
  534.6 17.3 %convolution_convert_fusion.4 = bf16[2048,1536]{1,0:T(8,128)(2,1)} fusion(bf16[2048,2048]{1,0:T(8,128)(2,1)S(1)} %bitcast.72, bf16[2048,768]{0,1:T(8,128)(2,1)} %get-tuple-element.92, bf16[2048,768]{0,1:T(8,128)(2,1)} %get-tuple-element.91), kind=kOutput, calls=%fused_computation.12 | convolution fusion | flops 12900630528 | bytes 20971520 | tf_op jit(solution)/shard_map/dot_general | solution.py:1241
  551.9 12.0 convolution_convert_fusion.5
  563.8 18.9 %convolution_convert_fusion.1 = bf16[2048,2048]{1,0:T(8,128)(2,1)} fusion(bf16[2048,1536]{1,0:T(8,128)(2,1)} %bitcast.98, bf16[2048,768]{0,1:T(8,128)(2,1)} %get-tuple-element.92, bf16[2048,768]{0,1:T(8,128)(2,1)S(1)} %copy-done.37), kind=kOutput, calls=%fused_computation.9 | convolution fusion | flops 12901679104 | bytes 20971520 | tf_op jit(solution)/shard_map/dot_general | solution.py:1235
  582.8 147.6 %shard_map.319 = (f32[256,2048]{1,0:T(8,128)}, bf16[4,8,64,1536]{3,2,1,0:T(8,128)(2,1)}, bf16[4,4,48,2048]{3,2,1,0:T(8,128)(2,1)}) custom-call(bf16[8,4,64,2048]{3,2,1,0:T(8,128)(2,1)} %bitcast.74, bf16[8,4,64,1536]{3,2,1,0:T(8,128)(2,1)} %bitcast.76, bf16[4,4,48,2048]{3,2,1,0:T(8,128)(2,1)} %bitcast.80), custom_call_target="tpu_custom_call" | custom-call | tf_op jit(solution)/shard_map/pallas_call | solution.py:771
  737.4 102.2 %shard_map.320 = bf16[8,256,2048]{2,1,0:T(8,128)(2,1)} custom-call(bf16[256,2048]{1,0:T(8,128)(2,1)} %get-tuple-element.87.refs_0_), custom_call_target="tpu_custom_call" | custom-call | tf_op jit(solution)/shard_map/pallas_call | solution.py:771
  839.7 7.2 fusion.21.dzed_ref
  847.0 32.8 %shard_map.322 = (bf16[8,256,1152]{2,1,0:T(8,128)(2,1)}, f32[12,256]{1,0:T(8,128)S(1)}, f32[1,128]{1,0:T(1,128)S(1)}) custom-call(f32[8,256,1152]{2,1,0:T(8,128)} %fusion.5.proj_ref, f32[8,256,768]{2,1,0:T(8,128)} %get-tuple-element.56.sums_ref, bf16[8,256,256]{2,1,0:T(8,128)(2,1)S(1)} %get-tuple-element.57.mixed_ref, f32[8,256,256]{2,1,0:T(8,128)} %fusion.21.dzed_ref, ...), custom_call_target="tpu_custom_call" | custom-call | tf_op jit(solution)/shard_map/pallas_call | solution.py:1175
  879.9 15.9 %bitcast_convert_fusion = bf16[2048,1152]{1,0:T(8,128)(2,1)} fusion(bf16[8,256,1152]{2,1,0:T(8,128)(2,1)} %get-tuple-element.63, bf16[8,256,2048]{2,1,0:T(8,128)(2,1)S(1)} %bitcast.68, f32[2048]{0:T(1024)S(1)} %bitcast.88, f32[8,256]{1,0:T(8,128)S(1)} %copy-done.27), kind=kOutput, calls=%fused_computation.6 | convolution fusion | flops 9682812928 | bytes 17842176 | tf_op jit(solution)/shard_map/dot_general | solution.py:1241
  895.8 13.2 %convolution_convert_fusion = bf16[2048,2048]{1,0:T(8,128)(2,1)} fusion(bf16[2048,1152]{1,0:T(8,128)(2,1)S(1)} %bitcast.99, bf16[2048,2]{1,0:T(8,128)(2,1)S(1)} %copy-done.22, bf16[2048,1024]{1,0:T(8,128)(2,1)S(1)} %bitcast.101), kind=kOutput, calls=%fused_computation.8 | convolution fusion | flops 9682026496 | bytes 17309696 | tf_op jit(solution)/shard_map/dot_general | solution.py:1235
  909.0 150.5 %shard_map.323 = (f32[256,2048]{1,0:T(8,128)}, bf16[4,8,64,1152]{3,2,1,0:T(8,128)(2,1)}) custom-call(bf16[8,4,64,2048]{3,2,1,0:T(8,128)(2,1)} %bitcast.75, bf16[8,4,64,1152]{3,2,1,0:T(8,128)(2,1)} %bitcast.78), custom_call_target="tpu_custom_call" | custom-call | tf_op jit(solution)/shard_map/pallas_call | solution.py:771
  1064.3 13.7 %shard_map.325 = (f32[8,640]{1,0:T(8,128)}, f32[16,256]{1,0:T(8,128)}) custom-call(f32[8,8,640]{2,1,0:T(8,128)} %broadcast_in_dim.82.refs_0_, f32[16,256]{1,0:T(8,128)} %pad.24.refs_1_), custom_call_target="tpu_custom_call" | custom-call | tf_op jit(solution)/shard_map/pallas_call | solution.py:771
  1093.1 6.8 fusion.9
  1099.9 9.1 convolution_convert_fusion.2
  1109.0 97.2 %shard_map.321 = (f32[256,2048]{1,0:T(8,128)}, bf16[4,4,16,2048]{3,2,1,0:T(8,128)(2,1)}) custom-call(bf16[8,4,64,2048]{3,2,1,0:T(8,128)(2,1)} %bitcast.73, bf16[4,4,16,2048]{3,2,1,0:T(8,128)(2,1)} %bitcast.79), custom_call_target="tpu_custom_call" | custom-call | tf_op jit(solution)/shard_map/pallas_call | solution.py:771
  1212.0 7.5 shard_map.326
  (152 shorter events, 61.6 us)
Async XLA Ops:
  0.7 183.2 %copy-start = (bf16[256,2048]{1,0:T(8,128)(2,1)S(1)}, bf16[256,2048]{1,0:T(8,128)(2,1)}, u32[]{:S(2)}) copy-start(bf16[256,2048]{1,0:T(8,128)(2,1)} %param.28) | copy-start | bytes 3145732
  123.5 7.9 copy-start.21
  123.5 8.5 copy-start.15
  132.0 16.0 %copy-start.32 = (s32[1,8,2]{1,2,0:T(2,128)S(1)}, s32[1,8,2]{1,2,0:T(2,128)}, u32[]{:S(2)}) copy-start(s32[1,8,2]{1,2,0:T(2,128)} %param.21) | copy-start | bytes 196
  132.0 16.2 %copy-start.35 = (s32[1,16]{1,0:T(1,128)S(1)}, s32[1,16]{1,0:T(1,128)}, u32[]{:S(2)}) copy-start(s32[1,16]{1,0:T(1,128)} %param.22) | copy-start | bytes 196
  132.0 21.5 %copy-start.29 = (bf16[4,256]{1,0:T(4,128)(2,1)S(1)}, bf16[4,256]{1,0:T(4,128)(2,1)}, u32[]{:S(2)}) copy-start(bf16[4,256]{1,0:T(4,128)(2,1)} %param.31) | copy-start | bytes 6148
  132.0 21.5 %copy-start.30 = (bf16[4,256]{1,0:T(4,128)(2,1)S(1)}, bf16[4,256]{1,0:T(4,128)(2,1)}, u32[]{:S(2)}) copy-start(bf16[4,256]{1,0:T(4,128)(2,1)} %param.30) | copy-start | bytes 6148
  132.0 21.5 %copy-start.31 = (bf16[4,256]{1,0:T(4,128)(2,1)S(1)}, bf16[4,256]{1,0:T(4,128)(2,1)}, u32[]{:S(2)}) copy-start(bf16[4,256]{1,0:T(4,128)(2,1)} %param.29) | copy-start | bytes 6148
  516.2 18.3 %slice-start.2 = ((s8[8388608]{0:T(1024)(128)(4,1)}), s8[4194304]{0:T(1024)(128)(4,1)S(1)}, s32[]{:S(2)}) async-start(s8[8388608]{0:T(1024)(128)(4,1)} %bitcast.70), calls=%async_computation.2 | async-start | bytes 8388608
  516.6 17.9 %copy-start.17 = (bf16[768,2048]{1,0:T(8,128)(2,1)}, bf16[768,2048]{1,0:T(8,128)(2,1)S(1)}, u32[]{:S(2)}) copy-start(bf16[768,2048]{1,0:T(8,128)(2,1)S(1)} %constant_dynamic-update-slice_fusion) | copy-start | bytes 9437188
  516.6 17.9 %slice-start.3 = ((s8[8388608]{0:T(1024)(128)(4,1)}), s8[4194304]{0:T(1024)(128)(4,1)S(1)}, s32[]{:S(2)}) async-start(s8[8388608]{0:T(1024)(128)(4,1)} %bitcast.70), calls=%async_computation.3 | async-start | bytes 8388608
  551.8 12.0 copy-start.37
  839.7 40.1 %slice-start = ((s8[8388608]{0:T(1024)(128)(4,1)}), s8[4194304]{0:T(1024)(128)(4,1)S(1)}, s32[]{:S(2)}) async-start(s8[8388608]{0:T(1024)(128)(4,1)} %bitcast.67), calls=%async_computation | async-start | bytes 8388608
  847.0 32.9 %slice-start.1 = ((s8[8388608]{0:T(1024)(128)(4,1)}), s8[4194304]{0:T(1024)(128)(4,1)S(1)}, s32[]{:S(2)}) async-start(s8[8388608]{0:T(1024)(128)(4,1)} %bitcast.67), calls=%async_computation.1 | async-start | bytes 8388608
  847.0 32.9 %copy-start.24 = (f32[1,2,8,128]{3,1,2,0:T(2,128)S(1)}, f32[1,2,8,128]{3,1,2,0:T(2,128)}, u32[]{:S(2)}) copy-start(f32[1,2,8,128]{3,1,2,0:T(2,128)} %copy-done.23) | copy-start | bytes 24580
  847.0 32.9 %copy-start.27 = (f32[8,256]{1,0:T(8,128)S(1)}, f32[8,256]{1,0:T(8,128)}, u32[]{:S(2)}) copy-start(f32[8,256]{1,0:T(8,128)} %copy-done.26) | copy-start | bytes 24580
  879.9 15.9 %copy-start.22 = (bf16[2048,2]{1,0:T(8,128)(2,1)S(1)}, bf16[2048,2]{1,0:T(8,128)(2,1)}, u32[]{:S(2)}) copy-start(bf16[2048,2]{1,0:T(8,128)(2,1)} %copy-done.21) | copy-start | bytes 24580
  879.9 15.9 %copy-start.33 = (bf16[8,256,1152]{2,1,0:T(8,128)(2,1)S(1)}, bf16[8,256,1152]{2,1,0:T(8,128)(2,1)}, u32[]{:S(2)}) copy-start(bf16[8,256,1152]{2,1,0:T(8,128)(2,1)} %get-tuple-element.63) | copy-start | bytes 14155780
  879.9 15.9 %copy-start.34 = (bf16[8,4,64,1024]{3,2,1,0:T(8,128)(2,1)S(1)}, bf16[8,4,64,1024]{3,2,1,0:T(8,128)(2,1)}, u32[]{:S(2)}) copy-start(bf16[8,4,64,1024]{3,2,1,0:T(8,128)(2,1)} %get-tuple-element.50) | copy-start | bytes 12582916
  909.0 150.5 %copy-start.14 = (bf16[256,2048]{1,0:T(8,128)(2,1)S(1)}, bf16[256,2048]{1,0:T(8,128)(2,1)}, u32[]{:S(2)}) copy-start(bf16[256,2048]{1,0:T(8,128)(2,1)} %refs_4_.1) | copy-start | bytes 3145732
  909.0 150.5 %copy-start.25 = (f32[256]{0:T(256)S(1)}, f32[256]{0:T(256)}, u32[]{:S(2)}) copy-start(f32[256]{0:T(256)} %get-tuple-element.101) | copy-start | bytes 3076
  1061.8 27.1 %copy-start.28 = (f32[256]{0:T(256)S(1)}, f32[256]{0:T(256)}, u32[]{:S(2)}) copy-start(f32[256]{0:T(256)} %get-tuple-element.100) | copy-start | bytes 3076
  1109.0 100.0 %copy-start.13 = (f32[256,2048]{1,0:T(8,128)S(1)}, f32[256,2048]{1,0:T(8,128)}, u32[]{:S(2)}) copy-start(f32[256,2048]{1,0:T(8,128)} %copy-done.11) | copy-start | bytes 6291460
  1209.0 10.5 copy-start.20
  (18 other events, 89.1 us)

commit v3 on v2

--- a/solution.py
+++ b/solution.py
@@ -39,6 +39,31 @@
 
     def other(self, k):
         return lax.rem(self.me + k, self.count)
+
+    def slot(self, zz, xx):
+        return zz * self.X + xx
+
+
+class Turned(Lines):
+    def __init__(self, line):
+        self.axis, self.count, self.me = line.axis, line.count, line.me
+        self.Z, self.X, self.z, self.x = line.X, line.Z, line.x, line.z
+        self.targets = line.targets[2:] + line.targets[:2]
+        self.exists = line.exists[2:] + line.exists[:2]
+
+    def slot(self, zz, xx):
+        return xx * self.Z + zz
+
+
+class Column(Lines):
+    def __init__(self, line):
+        self.axis, self.count, self.me = line.axis, line.Z, line.z
+        self.Z, self.X, self.z, self.x = line.Z, 1, line.z, jnp.int32(0)
+        self.targets = line.targets
+        self.exists = line.exists[:2] + (jnp.bool_(False),) * 2
+
+    def slot(self, zz, xx):
+        return zz
 
 
 def greet(lines, everyone):
@@ -110,7 +135,7 @@
 
             @pl.when(here)
             def _(way=way):
-                origin = (z - d if way == UP else z + d) * X + x
+                origin = line.slot(z - d if way == UP else z + d, x)
                 copy(way, origin, c).wait_recv()
                 for onward in (way, RIGHT, LEFT):
 
@@ -123,7 +148,7 @@
 
             @pl.when(here)
             def _(way=way):
-                origin = level * X + (x - e if way == RIGHT else x + e)
+                origin = line.slot(level, x - e if way == RIGHT else x + e)
                 copy(way, origin, c).wait_recv()
                 if X > 2:
 
@@ -138,21 +163,21 @@
 
                     @pl.when(exists[way] & here)
                     def _(way=way, zz=zz, c=c):
-                        copy(way, zz * X + x, c).wait_send()
+                        copy(way, line.slot(zz, x), c).wait_send()
 
                 for xx in range(X):
                     for way, here in ((RIGHT, xx <= x), (LEFT, xx >= x)):
 
                         @pl.when(exists[way] & here)
                         def _(way=way, zz=zz, xx=xx, c=c):
-                            copy(way, zz * X + xx, c).wait_send()
+                            copy(way, line.slot(zz, xx), c).wait_send()
 
     steps = []
     for c in range(chunks):
         steps.append((start + pace * c / chunks, functools.partial(first, c)))
     for d in range(1, Z):
         for c in range(chunks):
-            steps.append((start + pace * (d + (c + 1) / chunks), functools.partial(hop, d, c)))
+            steps.append((start + pace * (d - 1 + (c + 1) / chunks), functools.partial(hop, d, c)))
     for e in range(1, X):
         for dz in range(Z):
             level = lax.rem(z + dz, Z)
@@ -163,16 +188,18 @@
     return steps
 
 
-def scatter_slots(axis):
-    Z, X = grid_of(axis)
-    if X <= 2:
+def scatter_slots(dims):
+    Z, X = dims
+    if X == 1:
+        return Z, 1
+    if X == 2:
         return Z, Z
     return Z * X, Z * (X + 1)
 
 
-def scatter_scratch(axis, chunks, rows, width, kind):
-    Z, X = grid_of(axis)
-    held, across = scatter_slots(axis)
+def scatter_scratch(dims, chunks, rows, width, kind):
+    Z, X = dims
+    held, across = scatter_slots(dims)
     return [
         pltpu.VMEM((held, chunks, rows, width), kind),
         pltpu.VMEM((across, chunks, rows, width), kind),
@@ -188,18 +215,26 @@
 STEP = 16
 
 
+def stride(rows):
+    return max(n for n in (16, 32, 64) if rows % n == 0 and n <= BIG)
+
+
+BIG = 64
+
+
 def scatter_steps(line, chunks, block, piece, scratch, store, done, start, pace):
     mine, from_x, from_z, load_sem, xs_sem, xr_sem, zs_sem, zr_sem = scratch
     Z, X, z, x = line.Z, line.X, line.z, line.x
     exists = line.exists
     rows = mine.shape[2]
+    step = stride(rows)
 
     def spot(zz, xx):
         return zz if X <= 2 else zz * X + xx
 
     def load(zz, xx):
         at = spot(zz, xx)
-        return pltpu.make_async_copy(block(zz * X + xx), mine.at[at], load_sem.at[at])
+        return pltpu.make_async_copy(block(line.slot(zz, xx)), mine.at[at], load_sem.at[at])
 
     def x_landing(zz, xx, right, receiver):
         if X <= 2:
@@ -208,7 +243,7 @@
 
     def x_copy(right, zz, xx, c):
         landing = x_landing(zz, xx, right, x + 1 if right else x - 1)
-        src = piece(zz * X + xx, c) if X <= 2 else mine.at[spot(zz, xx), c]
+        src = piece(line.slot(zz, xx), c) if X <= 2 else mine.at[spot(zz, xx), c]
         return remote(
             src,
             from_x.at[landing, c],
@@ -232,13 +267,13 @@
 
     def add_in(at, buffer, landing, c):
         def body(i, carry):
-            part = pl.ds(pl.multiple_of(i * STEP, STEP), STEP)
+            part = pl.ds(pl.multiple_of(i * step, step), step)
             mine[at, c, part] = (
                 mine[at, c, part].astype(jnp.float32) + buffer[landing, c, part].astype(jnp.float32)
             ).astype(mine.dtype)
             return carry
 
-        lax.fori_loop(0, rows // STEP, body, 0)
+        lax.fori_loop(0, rows // step, body, 0)
 
     def x_line(zz):
         for k in range(X - 1):
@@ -322,7 +357,7 @@
             wait_in(from_z, zr_sem, Z, c)
 
         def body(i, carry):
-            part = pl.ds(pl.multiple_of(i * STEP, STEP), STEP)
+            part = pl.ds(pl.multiple_of(i * step, step), step)
             total = mine[spot(z, x), c, part].astype(jnp.float32)
             below = from_z[z, c, part].astype(jnp.float32)
             above = from_z[Z, c, part].astype(jnp.float32)
@@ -331,7 +366,7 @@
             store(c, part, total)
             return carry
 
-        lax.fori_loop(0, rows // STEP, body, 0)
+        lax.fori_loop(0, rows // step, body, 0)
         done(c)
 
     def finish():
@@ -351,73 +386,107 @@
     for k in range(Z - 1):
         for c in range(chunks):
             steps.append(
-                (start + pace * (1 + k + (c + 1) / chunks), functools.partial(pass_on, k, c))
+                (start + pace * (k + (c + 1) / chunks), functools.partial(pass_on, k, c))
             )
     for c in range(chunks):
-        steps.append((start + pace * (Z + (c + 1) / chunks), functools.partial(settle, c)))
+        steps.append((start + pace * (Z - 1 + (c + 1) / chunks), functools.partial(settle, c)))
     steps.append((start + pace * (Z + 2), finish))
     return steps
 
 
 class Gather:
-    def __init__(self, axis, block, chunks, start=0.0, pace=21.0):
+    def __init__(self, axis, block, chunks, start=0.0, pace=21.0, beside=False, turned=False):
         self.axis, self.chunks, self.start, self.pace = axis, chunks, start, pace
+        self.beside, self.turned = beside, turned
         self.inputs = [block]
         self.everyone = ()
         count = lax.axis_size(axis)
-        self.outputs = [(ANY, jax.ShapeDtypeStruct((count,) + block.shape, block.dtype))]
-        self.scratch = [DMA] + gather_sems(axis, chunks)
+        rows, width = block.shape
+        shape = (rows, count * width) if beside else (count, rows, width)
+        self.outputs = [(ANY, jax.ShapeDtypeStruct(shape, block.dtype))]
+        self.scratch = [DMA] + gather_sems(axis, chunks - turned)
+        if turned:
+            self.scratch += gather_sems(axis, 1)
 
     def steps(self, lines, ins, outs, scratch):
         line, (x_ref,), (out_ref,) = lines[self.axis], ins, outs
         own_sem, *sems = scratch
-        rows = x_ref.shape[0] // self.chunks
-        own = pltpu.make_async_copy(x_ref, out_ref.at[line.me], own_sem)
-
-        def part(c):
-            return pl.ds(c * rows, rows)
-
-        steps = gather_steps(
-            line,
-            self.chunks,
-            lambda origin, c: out_ref.at[origin, part(c)],
-            lambda c: x_ref.at[part(c)],
-            lambda c: None,
-            sems,
-            self.start,
-            self.pace,
-        )
+        rows, width = x_ref.shape[0] // self.chunks, x_ref.shape[1]
+
+        def view(origin, part):
+            if self.beside:
+                return out_ref.at[part, pl.ds(pl.multiple_of(origin * width, HD), width)]
+            return out_ref.at[origin, part]
+
+        own = pltpu.make_async_copy(x_ref, view(line.me, pl.ds(0, x_ref.shape[0])), own_sem)
+
+        def part_steps(line, first, count, sems, start):
+            def part(c):
+                return pl.ds((first + c) * rows, rows)
+
+            return gather_steps(
+                line,
+                count,
+                lambda origin, c: view(origin, part(c)),
+                lambda c: x_ref.at[part(c)],
+                lambda c: None,
+                sems,
+                start,
+                self.pace,
+            )
+
+        straight = self.chunks - self.turned
+        steps = part_steps(line, 0, straight, sems[:2], self.start)
+        if self.turned:
+            steps += part_steps(Turned(line), straight, 1, sems[2:], self.start + 0.9 * self.pace)
         return [(self.start, own.start)] + steps + [(steps[-1][0], own.wait)]
 
 
 class Scatter:
-    def __init__(self, axis, terms, chunks, start=0.0, pace=21.0):
+    def __init__(self, axis, terms, chunks, start=0.0, pace=21.0, turned=False, column=False):
         self.axis, self.chunks, self.start, self.pace = axis, chunks, start, pace
-        count = lax.axis_size(axis)
+        self.turned, self.column = turned, column
+        dims = grid_of(axis)
+        if column:
+            dims = (dims[0], 1)
+        count = dims[0] * dims[1]
         rows, width = terms.shape[0] // count // chunks, terms.shape[1]
         self.inputs = [terms.reshape(count, chunks, rows, width)]
         self.everyone = ()
         self.outputs = [(VMEM, jax.ShapeDtypeStruct((chunks * rows, width), jnp.float32))]
-        self.scratch = scatter_scratch(axis, chunks, rows, width, terms.dtype)
+        self.scratch = scatter_scratch(dims, chunks - turned, rows, width, terms.dtype)
+        self.half = len(self.scratch)
+        if turned:
+            self.scratch += scatter_scratch(dims[::-1], 1, rows, width, terms.dtype)
 
     def steps(self, lines, ins, outs, scratch):
         (p_ref,), (out_ref,) = ins, outs
         rows = p_ref.shape[2]
 
-        def store(c, part, total):
-            out_ref[pl.ds(pl.multiple_of(c * rows + part.start, STEP), STEP)] = total
-
-        return scatter_steps(
-            lines[self.axis],
-            self.chunks,
-            lambda slot: p_ref.at[slot],
-            lambda slot, c: p_ref.at[slot, c],
-            scratch,
-            store,
-            lambda c: None,
-            self.start,
-            self.pace,
-        )
+        def part_steps(line, first, count, scratch, start):
+            def store(c, part, total):
+                at = pl.multiple_of((first + c) * rows + part.start, STEP)
+                out_ref[pl.ds(at, part.size)] = total
+
+            return scatter_steps(
+                line,
+                count,
+                lambda slot: p_ref.at[slot, pl.ds(first, count)],
+                lambda slot, c: p_ref.at[slot, first + c],
+                scratch,
+                store,
+                lambda c: None,
+                start,
+                self.pace,
+            )
+
+        line, straight = lines[self.axis], self.chunks - self.turned
+        if self.column:
+            line = Column(line)
+        steps = part_steps(line, 0, straight, scratch[: self.half], self.start)
+        if self.turned:
+            steps += part_steps(Turned(line), straight, 1, scratch[self.half :], self.start + 0.01)
+        return steps
 
 
 class Spread:
@@ -500,94 +569,119 @@
         return [(self.start, begin)] + steps + [(steps[-1][0], finish)]
 
 
-class Collect:
+class Trade:
+    def __init__(self, block, start=0.0, pace=6.0):
+        self.inputs = [block]
+        self.start, self.pace = start, pace
+        self.everyone = ()
+        shards, part, width = block.shape
+        shape = (shards, lax.axis_size("replica"), part, width)
+        self.outputs = [(ANY, jax.ShapeDtypeStruct(shape, block.dtype))]
+        self.scratch = [DMA] + gather_sems("replica", shards)
+
+    def steps(self, lines, ins, outs, scratch):
+        own_sem, *sems = scratch
+        (x_ref,), (out_ref,) = ins, outs
+        copies = lines["replica"]
+        own = pltpu.make_async_copy(x_ref, out_ref.at[:, copies.me], own_sem)
+        steps = gather_steps(
+            copies,
+            x_ref.shape[0],
+            lambda origin, c: out_ref.at[c, origin],
+            lambda c: x_ref.at[c],
+            lambda c: None,
+            sems,
+            self.start,
+            self.pace,
+        )
+        return [(self.start, own.start)] + steps + [(steps[-1][0], own.wait)]
+
+
+class Sum:
     def __init__(self, terms, start=0.0, pace=6.0):
         shards, replicas = lax.axis_size("shard"), lax.axis_size("replica")
         part, wide = terms.shape[0] // shards // replicas, terms.shape[1]
         self.inputs = [terms.reshape(shards, replicas, part, wide)]
         self.start, self.pace = start, pace
-        self.everyone = ("shard",)
-        kind = terms.dtype
-        self.outputs = [(ANY, jax.ShapeDtypeStruct((replicas, shards, part, wide), kind))]
-        self.own_scratch = [
-            pltpu.VMEM((shards, part, wide), kind),
-            DMA,
-            DMA((shards,)),
-            DMA((shards,)),
-        ] + gather_sems("replica", shards)
-        self.scratch = self.own_scratch + scatter_scratch("replica", shards, part, wide, kind)
+        self.everyone = ()
+        self.outputs = [(VMEM, jax.ShapeDtypeStruct((shards, part, wide), terms.dtype))]
+        self.scratch = scatter_scratch(grid_of("replica"), shards, part, wide, terms.dtype)
 
     def steps(self, lines, ins, outs, scratch):
         (p_ref,), (out_ref,) = ins, outs
-        total_ref, own_sem, send_sem, recv_sem = scratch[:4]
-        sems = scratch[4:6]
+
+        def store(c, part, total):
+            out_ref[c, part] = total.astype(out_ref.dtype)
+
+        return scatter_steps(
+            lines["replica"],
+            out_ref.shape[0],
+            lambda slot: p_ref.at[:, slot],
+            lambda slot, c: p_ref.at[c, slot],
+            scratch,
+            store,
+            lambda c: None,
+            self.start,
+            self.pace,
+        )
+
+
+class Deliver:
+    def __init__(self, sums, start=0.0, again=30.0, pace=24.0):
+        self.inputs = [sums]
+        self.start, self.again, self.pace = start, again, pace
+        self.everyone = ("shard",)
+        shards, replicas = lax.axis_size("shard"), lax.axis_size("replica")
+        self.outputs = [(ANY, jax.ShapeDtypeStruct((replicas,) + sums.shape, sums.dtype))]
+        self.scratch = [DMA, DMA((shards,)), DMA((shards,))] + gather_sems("replica", shards)
+
+    def steps(self, lines, ins, outs, scratch):
+        own_sem, send_sem, recv_sem, *sems = scratch
+        (x_ref,), (out_ref,) = ins, outs
         group, copies = lines["shard"], lines["replica"]
-
-        def own():
-            return pltpu.make_async_copy(
-                total_ref.at[group.me], out_ref.at[copies.me, group.me], own_sem
+        own = pltpu.make_async_copy(
+            x_ref.at[group.me], out_ref.at[copies.me, group.me], own_sem
+        )
+
+        def deal(k):
+            target = group.other(k)
+            return remote(
+                x_ref.at[target],
+                out_ref.at[copies.me, group.me],
+                send_sem.at[k],
+                recv_sem.at[group.me],
+                {"shard": target},
             )
 
-        def deal(c):
-            return remote(
-                total_ref.at[c],
-                out_ref.at[copies.me, group.me],
-                send_sem.at[c],
-                recv_sem.at[group.me],
-                {"shard": jnp.int32(c)},
-            )
-
-        def store(c, part, total):
-            total_ref[c, part] = total.astype(total_ref.dtype)
-
-        def done(c):
-            @pl.when(c == group.me)
-            def _():
-                own().start()
-
-            @pl.when(c != group.me)
-            def _():
-                deal(c).start()
+        def begin():
+            own.start()
+            for k in range(1, group.count):
+                deal(k).start()
 
         def ready(c):
             @pl.when(c == group.me)
             def _():
-                own().wait()
+                own.wait()
 
             @pl.when(c != group.me)
             def _():
                 in_place(out_ref.at[copies.me, c], recv_sem.at[c]).wait()
 
         def finish():
-            for c in range(group.count):
-
-                @pl.when(c != group.me)
-                def _(c=c):
-                    deal(c).wait_send()
-
-        summing = scatter_steps(
-            copies,
-            group.count,
-            lambda slot: p_ref.at[:, slot],
-            lambda slot, c: p_ref.at[c, slot],
-            scratch[6:],
-            store,
-            done,
-            self.start,
-            self.pace,
-        )
-        again = self.start + self.pace * (copies.Z + 3)
-        sharing = gather_steps(
+            for k in range(1, group.count):
+                deal(k).wait_send()
+
+        steps = gather_steps(
             copies,
             group.count,
             lambda origin, c: out_ref.at[origin, c],
             lambda c: out_ref.at[copies.me, c],
             ready,
             sems,
-            again,
+            self.again,
             self.pace,
         )
-        return summing + sharing + [(sharing[-1][0], finish)]
+        return [(self.start, begin)] + steps + [(steps[-1][0], finish)]
 
 
 class Total:
@@ -603,7 +697,7 @@
         self.outputs = [(ANY, jax.ShapeDtypeStruct((replicas, chunks, rows, wide), kind))]
         self.scratch = [pltpu.VMEM((chunks, rows, wide), kind), DMA((chunks,))]
         self.scratch += gather_sems("replica", chunks)
-        self.scratch += scatter_scratch("replica", chunks, rows, wide, kind)
+        self.scratch += scatter_scratch(grid_of("replica"), chunks, rows, wide, kind)
 
     def steps(self, lines, ins, outs, scratch):
         (p_ref,), (out_ref,) = ins, outs
@@ -730,7 +824,7 @@
                 share(0, k).wait_send()
                 share(1, k).wait_send()
 
-        return [(self.start, begin), (self.start + 5.0, middle), (self.start + 10.0, end)]
+        return [(-0.5, begin), (self.start, middle), (self.start + 40.0, end)]
 
 
 def layout_of(tasks):
@@ -1162,6 +1256,7 @@
             pltpu.VMEM((lanes, 8 * group, KINDS * wide), jnp.float32),
         ],
         compiler_params=pltpu.CompilerParams(vmem_limit_bytes=48 * 1024 * 1024),
+        cost_estimate=pl.CostEstimate(flops=35 * 10**9, bytes_accessed=40 * 10**6, transcendentals=0),
     )(proj, taps, gain, low, off, rem)
 
 
@@ -1195,6 +1290,7 @@
             pltpu.VMEM((size, HD), jnp.float32),
         ],
         compiler_params=pltpu.CompilerParams(vmem_limit_bytes=48 * 1024 * 1024),
+        cost_estimate=pl.CostEstimate(flops=35 * 10**9, bytes_accessed=40 * 10**6, transcendentals=0),
     )(proj, sums, mixed, dzed, taps, gain, low, off, rem, *saves)
 
 
@@ -1251,6 +1347,15 @@
     r = lax.rsqrt(jnp.mean(values * values, axis=-1, keepdims=True) + eps)
     inner = jnp.mean(values * gain * grad, axis=-1, keepdims=True)
     return r * gain * grad - values * (r * r * r) * inner, grad * values * r
+
+
+def deal(stacked):
+    return lax.all_to_all(stacked, "shard", split_axis=0, concat_axis=0, tiled=True)
+
+
+def cross(blocks):
+    shards = lax.axis_size("shard")
+    return lax.ppermute(blocks, "shard", [(s, s ^ 1) for s in range(shards)])
 
 
 def column_windows(columns, shards):
@@ -1337,22 +1442,12 @@
     attn_weights, all_source, little = exchange(
         [
             Spread((w_query, w_key, w_value, w_outgate), col_window, col_first, -0.5, 12.0),
-            Gather("shard", layer_input, 4),
+            Gather("shard", layer_input, 8, turned=True),
             Gather("shard", little, 1, 0.0, 20.0),
         ],
         both,
         0,
     )
-    mlp_weights, dy = exchange(
-        [
-            Spread((w_gate, w_up), ffn_window, ffn_first, -0.5, 16.0),
-            Gather("shard", out_cotangent, 4),
-        ],
-        both,
-        1,
-    )
-    dy = dy.reshape(tokens, width)
-    mlp_weights = mlp_weights.reshape(width, 2 * ffn_window)
     full_attn_gain = little[:, :, total_heads].reshape(width).astype(f32)
     full_mlp_gain = little[:, :, total_heads + 1].reshape(width).astype(f32)
     head_row = little[:, : head_gain.shape[0], total_heads + 2].reshape(1, HD).astype(f32)
@@ -1360,6 +1455,28 @@
     attn_weights = jnp.concatenate(
         [attn_weights.reshape(width, 4 * own), jnp.pad(beta, ((0, 0), (0, HD - heads)))], axis=1
     )
+    replicas = lax.axis_size("replica")
+    part = weight_rows // replicas
+    at = lax.axis_index("replica") * part
+    windows = [
+        lax.slice_in_dim(w, ffn_first(s), ffn_first(s) + ffn_window, axis=1)
+        for s in range(shards)
+        for w in (
+            lax.dynamic_slice_in_dim(w_gate, at, part),
+            lax.dynamic_slice_in_dim(w_up, at, part),
+        )
+    ]
+    mlp_weights = jnp.stack(
+        [jnp.concatenate(windows[2 * s : 2 * s + 2], axis=1) for s in range(shards)]
+    )
+    full_output = jnp.broadcast_to(
+        lax.dynamic_slice_in_dim(w_output, at, part)[None], (shards, part, width)
+    )
+    later_weights = jnp.concatenate([mlp_weights, full_output], axis=2)
+    later_weights, all_source = lax.optimization_barrier((later_weights, all_source))
+    later_weights = deal(later_weights)
+    mlp_weights = later_weights[..., : 2 * ffn_window]
+    full_output = later_weights[..., 2 * ffn_window :]
     low, off, rem = segment_masks(seq_lengths[0], seq_order[0], shards, rows)
 
     source = layer_input.astype(f32)
@@ -1368,14 +1485,22 @@
     projected = project(normed, attn_weights).reshape(shards, rows, -1)
     taps = jnp.concatenate([conv_query, conv_key, conv_value], axis=0).astype(f32)
     zed, mixed, sums, *saves = mixer_forward(projected, taps, head_row, low, off, rem, heads)
+    all_zed, mlp_weights, full_output, dy = exchange(
+        [
+            Gather("shard", zed.reshape(tokens, own), 8, 0.0, 21.0, True, True),
+            Trade(mlp_weights, 0.2, 31.0),
+            Trade(full_output, 0.1, 42.0),
+            Gather("shard", out_cotangent, 8, 80.0, 21.0, turned=True),
+        ],
+        both,
+        2,
+    )
     zed = zed.reshape(tokens, own)
-    (hidden,) = exchange([Scatter("shard", project(zed, w_output).astype(bf16), 4)], group, 2)
-    hidden = source + hidden
-
-    (mlp_in,) = exchange(
-        [Gather("shard", rms(hidden, full_mlp_gain, 1e-6).astype(bf16), 4)], group, 3
-    )
-    mlp_in = mlp_in.reshape(tokens, width)
+    mlp_weights = mlp_weights.reshape(width, 2 * ffn_window)
+    dy = dy.reshape(tokens, width)
+    all_hidden = all_source + project(all_zed, full_output.reshape(width, width))
+    mlp_in = rms(all_hidden, full_mlp_gain, 1e-6).astype(bf16)
+    hidden = lax.dynamic_slice_in_dim(all_hidden, shard * rows, rows)
     w_down = lax.dynamic_update_slice(jnp.zeros((ffn_window, width), bf16), w_down, (shift, 0))
     lin = project(mlp_in, mlp_weights)
     gate_lin, up_lin = lin[:, :ffn_window], lin[:, ffn_window:]
@@ -1390,8 +1515,8 @@
     d_mlp_in, g_lin, g_down = exchange(
         [
             Scatter("shard", times_t(d_lin, mlp_weights).astype(bf16), 4),
-            Collect(g_lin, 0.5, 13.0),
-            Total(g_down, 0.7, 13.0),
+            Sum(g_lin, 0.5, 20.0),
+            Total(g_down, 0.7, 16.0),
         ],
         both,
         4,
@@ -1399,38 +1524,49 @@
     d_hidden_norm, g_mlp_rows = rms_back(hidden, full_mlp_gain, 1e-6, d_mlp_in)
     d_hidden = out_cotangent.astype(f32) + d_hidden_norm
 
-    (d_attn,) = exchange([Gather("shard", d_hidden.astype(bf16), 4)], group, 5)
+    (d_attn,) = exchange(
+        [Gather("shard", d_hidden.astype(bf16), 8, turned=True)], group, 5
+    )
+    g_lin, d_attn = lax.optimization_barrier((g_lin, d_attn))
+    g_lin = deal(g_lin)
     d_attn = d_attn.reshape(tokens, width)
     g_output = contract_rows(zed, d_attn).astype(bf16)
-    out_terms, g_output = exchange(
-        [Scatter("shard", project(product, w_down).astype(bf16), 4), Total(g_output, 0.5, 10.0)],
-        both,
-        6,
-    )
     d_zed = times_t(d_attn, w_output).reshape(shards, rows, own)
     d_proj, g_taps, g_head = mixer_backward(
         projected, sums, mixed, d_zed, taps, head_row, low, off, rem, saves, heads
     )
     d_proj = d_proj.reshape(tokens, -1)
     g_proj = contract_rows(normed, d_proj).astype(bf16)
-    d_normed, g_proj = exchange(
-        [Scatter("shard", times_t(d_proj, attn_weights).astype(bf16), 4), Collect(g_proj, 0.5, 10.0)],
+    d_normed, g_proj, g_output, g_lin = exchange(
+        [
+            Scatter("shard", times_t(d_proj, attn_weights).astype(bf16), 4),
+            Sum(g_proj, 0.5, 16.0),
+            Total(g_output, 0.7, 14.0),
+            Gather("replica", g_lin.reshape(-1, 2 * ffn_window), 4, 0.3, 31.0),
+        ],
+        both,
+        6,
+    )
+    d_source, g_attn_rows = rms_back(source, full_attn_gain, 1e-6, d_normed)
+
+    def dealt(values):
+        return values.reshape(shards, -1)
+
+    small = jnp.concatenate(
+        [dealt(jnp.sum(g_attn_rows, axis=0)), dealt(jnp.sum(g_mlp_rows, axis=0)), dealt(g_head)], axis=1
+    )
+    small = jnp.pad(small, ((0, 0), (0, -small.shape[1] % HD)))
+    small = jnp.broadcast_to(small[:, None, :], (shards, 8, small.shape[1]))
+    out_terms, g_proj, small, g_taps = exchange(
+        [
+            Scatter("shard", project(product, w_down).astype(bf16), 4),
+            Deliver(g_proj, -0.4, 30.0, 24.0),
+            Small(small, jnp.pad(g_taps, ((0, 16 - g_taps.shape[0]), (0, 0))), 50.0),
+        ],
         both,
         7,
     )
-    d_source, g_attn_rows = rms_back(source, full_attn_gain, 1e-6, d_normed)
-
-    def dealt(values):
-        return values.reshape(shards, -1)
-
-    small = jnp.concatenate(
-        [dealt(jnp.sum(g_attn_rows, axis=0)), dealt(jnp.sum(g_mlp_rows, axis=0)), dealt(g_head)], axis=1
-    )
-    small = jnp.pad(small, ((0, 0), (0, -small.shape[1] % HD)))
-    small = jnp.broadcast_to(small[:, None, :], (shards, 8, small.shape[1]))
-    small, g_taps = exchange(
-        [Small(small, jnp.pad(g_taps, ((0, 16 - g_taps.shape[0]), (0, 0))))], both, 8
-    )
+    g_lin = g_lin.reshape(replicas, shards, -1, 2 * ffn_window)
     g_query, g_key, g_value, g_outgate = widen(g_proj, 4, width, col_window, col_first)
     g_gate, g_up = widen(g_lin, 2, ffn, ffn_window, ffn_first)
     g_beta = g_proj[..., 4 * own : 4 * own + heads].transpose(0, 2, 1, 3)

time: 1230 us -> 1110 us (0.902); the launches traced: 1220 us -> 1090 us
  Pallas kernels: 1000 us -> 805 us
  matrix products: 159 us -> 187 us
  waiting for transfers between devices: 0 us -> 24 us
    pallas_call x9 -> x6, Pallas kernels: 930 us -> 731 us  [exchange(): pl.pallas_call(kernel, in_specs=[ANY] * len(inputs), out_specs=[spec for...]
    all_to_all x0 -> x2, waiting for transfers between devices: none -> 24 us  [deal(): lax.all_to_all(stacked, 'shard', split_axis=0, concat_axis=0, tiled=True)]
    dot_general x4, matrix products: 49.7 us -> 72.1 us  [project(): return jnp.dot(left_side, right_side, preferred_element_type=jnp.float32)]
  transfers between devices with their start and end apart: 0 -> 2, of which waited for: 0 -> 2; matrix products, arithmetic and copies ran while one was open for 0% -> 5% of each run, Pallas kernels for 0% -> 3%
where the time goes in v3:
time: 1110 us; the launch traced here: 1090 us
  Pallas kernels  805 us (73%)
  matrix products  187 us (17%)
  other arithmetic  34.7 us (3%)
  local copies, waits for them, and re-layouts  28.1 us (3%)
  waiting for transfers between devices  24 us (2%)
    pallas_call x6, Pallas kernels, exchange(): pl.pallas_call(kernel, in_specs=[ANY] * len(inputs), out_specs=[spec for...  731 us
    dot_general x4, matrix products, project(): return jnp.dot(left_side, right_side, preferred_element_type=jnp.float32)  72.1 us
    dot_general x4, matrix products, times_t(): lax.dot_general(left_side, right_side, (((1,), (1,)), ((), ())), preferre...  60.9 us
    dot_general x4, matrix products, contract_rows(): lax.dot_general(left_side, right_side, (((0,), (0,)), ((), ())), preferre...  54.1 us
    pallas_call x1, Pallas kernels, mixer_backward(): pl.pallas_call(functools.partial(delta_backward, lanes, heads, group), gr...  32.9 us
    pallas_call x1, Pallas kernels, mixer_forward(): pl.pallas_call(functools.partial(delta_forward, lanes, heads, group), gri...  30.2 us
    all_to_all x2, waiting for transfers between devices, deal(): lax.all_to_all(stacked, 'shard', split_axis=0, concat_axis=0, tiled=True)  24 us
  transfers between devices with their start and end apart: 2, of which 2 were waited for; matrix products, arithmetic and copies ran while one was open for 5% of the time, Pallas kernels for 3%

profile of v3, /device:TPU:0, one launch (start us, length us, event | category | flops | bytes accessed | tf_op | source)
XLA Modules:
  0.0 1090.4 jit_solution(12493639433342456276)
XLA Ops:
  8.5 123.0 %shard_map.314 = (bf16[8,4,64,1024]{3,2,1,0:T(8,128)(2,1)}, bf16[8,256,2048]{2,1,0:T(8,128)(2,1)}, bf16[8,256,128]{2,1,0:T(8,128)(2,1)}) custom-call(bf16[256,2048]{1,0:T(8,128)(2,1)} %refs_0_.1, bf16[256,2048]{1,0:T(8,128)(2,1)} %refs_1_.1, bf16[256,2048]{1,0:T(8,128)(2,1)} %refs_2_.1, bf16[256,2048]{1,0:T(8,128)(2,1)} %refs_3_.2, ...), custom_call_target="tpu_custom_call" | custom-call | tf_op jit(solution)/shard_map/pallas_call | solution.py:865
  148.3 15.8 %fusion.1.proj_ref = f32[8,256,1152]{2,1,0:T(8,128)} fusion(bf16[8,256,2048]{2,1,0:T(8,128)(2,1)} %get-tuple-element.57, f32[2048]{0:T(1024)S(1)} %bitcast.113, f32[8,256]{1,0:T(8,128)S(1)} %add_rsqrt_fusion.1, bf16[2048,2]{1,0:T(8,128)(2,1)S(1)} %constant_dynamic-slice_fusion.2, bf16[2048,1024]{1,0:T(8,128)(2,1)S(1)} %bitcast.130), kind=kOutput, calls=%fused_computation.12 | convolution fusion | flops 9694609408 | bytes 22044672 | tf_op jit(solution)/shard_map/dot_general | solution.py:1327
  166.7 30.2 %shard_map.315 = (bf16[8,256,256]{2,1,0:T(8,128)(2,1)S(1)}, bf16[8,256,256]{2,1,0:T(8,128)(2,1)S(1)}, f32[8,256,768]{2,1,0:T(8,128)}, bf16[32,2,128,128]{3,2,1,0...) custom-call(f32[8,256,1152]{2,1,0:T(8,128)} %fusion.1.proj_ref, ...), custom_call_target="tpu_custom_call" | custom-call | flops 35000000512 | bytes 40000000 | tf_op jit(solution)/shard_map/pallas_call | solution.py:1240
  200.0 16.3 %all-to-all-done = bf16[8,64,3584]{2,1,0:T(8,128)(2,1)} async-done(((bf16[8,64,3584]{2,1,0:T(8,128)(2,1)}), bf16[8,64,3584]{2,1,0:T(8,128)(2,1)}, u32[]{:S(2)}, u32[]{:S(2)}) %all-to-all-start) | async-done | bytes 3670048 | tf_op jit(solution)/shard_map/all_to_all | solution.py:1353
  222.1 195.1 %shard_map.316 = (bf16[2048,2048]{1,0:T(8,128)(2,1)}, bf16[8,4,64,1536]{3,2,1,0:T(8,128)(2,1)}, bf16[8,4,64,2048]{3,2,1,0:T(8,128)(2,1)}, bf16[8,256,2048]{2,1,0:T(8,128)(2,1)}) custom-call(bf16[2048,256]{1,0:T(8,128)(2,1)} %bitcast.98, bf16[8,64,1536]{2,1,0:T(8,128)(2,1)} %slice.120.refs_1_, bf16[8,64,2048]{2,1,0:T(8,128)(2,1)} %slice.121.refs_2_, ...), custom_call_target="tpu_custom_call" | custom-call | tf_op jit(solution)/shard_map/pallas_call | solution.py:865
  417.2 25.3 %multiply_reduce_fusion = (f32[2048]{0:T(1024)S(1)}, f32[2048,2048]{1,0:T(8,128)}) fusion(bf16[2048,2048]{1,0:T(8,128)(2,1)} %get-tuple-element.62, bf16[2048,2048]{1,0:T(8,128)(2,1)} %bitcast.127, bf16[8,256,2048]{2,1,0:T(8,128)(2,1)} %get-tuple-element.57), kind=kOutput, calls=%fused_computation.2 | convolution fusion | flops 17196644352 | bytes 41951232 | tf_op jit(solution)/shard_map/dot_general | solution.py:1327
  442.5 21.8 %fusion.34 = f32[2048,1536]{0,1:T(8,128)} fusion(bf16[2048,1536]{1,0:T(8,128)(2,1)} %bitcast.128, f32[2048,2048]{1,0:T(8,128)} %get-tuple-element.136, f32[2048]{0:T(1024)S(1)} %bitcast.117, f32[2048]{0:T(1024)S(1)} %add_rsqrt_fusion), kind=kOutput, calls=%fused_computation.108 | convolution fusion | flops 12897484800 | bytes 35667968 | tf_op jit(solution)/shard_map/dot_general | solution.py:1327
  464.2 18.7 %multiply_convert_fusion.5 = (bf16[2048,768]{0,1:T(8,128)(2,1)}, bf16[2048,768]{0,1:T(8,128)(2,1)}, bf16[2048,768]{0,1:T(8,128)(2,1)}) fusion(f32[2048,1536]{0,1:T(8,128)} %fusion.34, bf16[2048,2048]{1,0:T(8,128)(2,1)} %bitcast.125, bf16[768,2048]{1,0:T(8,128)(2,1)} %copy-done.22), kind=kOutput, calls=%fused_computation.15 | convolution fusion | flops 6467616768 | bytes 33554432 | tf_op jit(solution)/shard_map/dot_general | solution.py:1331
  482.9 21.2 %convolution_convert_fusion.3 = bf16[2048,1536]{1,0:T(8,128)(2,1)} fusion(bf16[2048,768]{0,1:T(8,128)(2,1)} %get-tuple-element.106, bf16[2048,768]{0,1:T(8,128)(2,1)} %get-tuple-element.105, f32[2048,2048]{1,0:T(8,128)} %get-tuple-element.136, f32[2048]{0:T(1024)S(1)} %bitcast.118, f32[2048]{0:T(1024)S(1)} %add_rsqrt_fusion), kind=kOutput, calls=%fused_computation.11 | convolution fusion | flops 12913213440 | bytes 29376512 | tf_op jit(solution)/shard_map/dot_general | solution.py:1337
  504.2 19.5 %convolution_convert_fusion.1 = bf16[2048,2048]{1,0:T(8,128)(2,1)} fusion(bf16[2048,1536]{1,0:T(8,128)(2,1)} %bitcast.129, bf16[2048,768]{0,1:T(8,128)(2,1)} %get-tuple-element.106, bf16[2048,768]{0,1:T(8,128)(2,1)} %get-tuple-element.105), kind=kOutput, calls=%fused_computation.9 | convolution fusion | flops 12901679104 | bytes 20971520 | tf_op jit(solution)/shard_map/dot_general | solution.py:1331
  523.6 10.4 convolution_convert_fusion.4
  534.0 9.3 convolution_convert_fusion.2
  545.1 96.4 %shard_map.317 = (f32[256,2048]{1,0:T(8,128)}, bf16[8,64,1536]{2,1,0:T(8,128)(2,1)}, bf16[4,4,48,2048]{3,2,1,0:T(8,128)(2,1)}) custom-call(bf16[8,4,64,2048]{3,2,1,0:T(8,128)(2,1)} %bitcast.102, bf16[8,4,64,1536]{3,2,1,0:T(8,128)(2,1)} %bitcast.105, bf16[4,4,48,2048]{3,2,1,0:T(8,128)(2,1)} %bitcast.109), custom_call_target="tpu_custom_call" | custom-call | tf_op jit(solution)/shard_map/pallas_call | solution.py:865
  648.6 91.6 %shard_map.318 = bf16[8,256,2048]{2,1,0:T(8,128)(2,1)} custom-call(bf16[256,2048]{1,0:T(8,128)(2,1)} %get-tuple-element.103.refs_0_), custom_call_target="tpu_custom_call" | custom-call | tf_op jit(solution)/shard_map/pallas_call | solution.py:865
  740.3 7.2 fusion.16.dzed_ref
  747.6 32.9 %shard_map.319 = (bf16[8,256,1152]{2,1,0:T(8,128)(2,1)}, f32[12,256]{1,0:T(8,128)S(1)}, f32[1,128]{1,0:T(1,128)S(1)}) custom-call(f32[8,256,1152]{2,1,0:T(8,128)} %fusion.1.proj_ref, f32[8,256,768]{2,1,0:T(8,128)} %get-tuple-element.65.sums_ref, bf16[8,256,256]{2,1,0:T(8,128)(2,1)S(1)} %get-tuple-element.66.mixed_ref, f32[8,256,256]{2,1,0:T(8,128)} %fusion.16.dzed_ref, ...), custom_call_target="tpu_custom_call" | custom-call | flops 35000000512 | bytes 40000000 | tf_op jit(solution)/shard_map/pallas_call | solution.py:1270
  780.6 15.7 %bitcast_convert_fusion = bf16[2048,1152]{1,0:T(8,128)(2,1)} fusion(bf16[8,256,1152]{2,1,0:T(8,128)(2,1)} %get-tuple-element.76, bf16[8,256,2048]{2,1,0:T(8,128)(2,1)S(1)} %bitcast.100, f32[2048]{0:T(1024)S(1)} %bitcast.114, f32[8,256]{1,0:T(8,128)S(1)} %copy-done.33), kind=kOutput, calls=%fused_computation.6 | convolution fusion | flops 9682812928 | bytes 17842176 | tf_op jit(solution)/shard_map/dot_general | solution.py:1337
  802.1 5.1 dynamic-slice_convert_fusion
  807.8 6.8 fusion.4
  814.7 15.5 %convolution_convert_fusion = bf16[2048,2048]{1,0:T(8,128)(2,1)} fusion(bf16[2048,1152]{1,0:T(8,128)(2,1)} %bitcast.133, bf16[2048,2]{1,0:T(8,128)(2,1)S(1)} %copy-done.27, bf16[2048,1024]{1,0:T(8,128)(2,1)S(1)} %bitcast.131), kind=kOutput, calls=%fused_computation.8 | convolution fusion | flops 9682026496 | bytes 17309696 | tf_op jit(solution)/shard_map/dot_general | solution.py:1331
  830.1 7.7 all-to-all-done.1
  837.8 110.8 %shard_map.320 = (f32[256,2048]{1,0:T(8,128)}, bf16[8,64,1152]{2,1,0:T(8,128)(2,1)}, bf16[4,4,16,2048]{3,2,1,0:T(8,128)(2,1)}, bf16[4,512,1536]{2,1,0:T(8,128)(2,1)}) custom-call(bf16[8,4,64,2048]{3,2,1,0:T(8,128)(2,1)} %bitcast.103, bf16[8,4,64,1152]{3,2,1,0:T(8,128)(2,1)} %bitcast.107, bf16[4,4,16,2048]{3,2,1,0:T(8,128)(2,1)} %bitcast.108, ...), custom_call_target="tpu_custom_call" | custom-call | tf_op jit(solution)/shard_map/pallas_call | solution.py:865
  951.6 113.8 %shard_map.321 = (f32[256,2048]{1,0:T(8,128)}, bf16[4,8,64,1152]{3,2,1,0:T(8,128)(2,1)}, f32[8,640]{1,0:T(8,128)}, f32[16,256]{1,0:T(8,128)}) custom-call(bf16[8,4,64,2048]{3,2,1,0:T(8,128)(2,1)} %bitcast.101, bf16[8,64,1152]{2,1,0:T(8,128)(2,1)} %get-tuple-element.78.refs_1_, f32[8,8,640]{2,1,0:T(8,128)} %broadcast_in_dim.89.refs_2_, f32[16,256]{1,0:T(8,128)} %pad.24.refs_3_), custom_call_target="tpu_custom_call" | custom-call | tf_op jit(solution)/shard_map/pallas_call | solution.py:865
  1073.8 7.5 shard_map.323
  (174 shorter events, 70.8 us)
Async XLA Ops:
  131.5 84.8 %all-to-all-start = ((bf16[8,64,3584]{2,1,0:T(8,128)(2,1)}), bf16[8,64,3584]{2,1,0:T(8,128)(2,1)}, u32[]{:S(2)}, u32[]{:S(2)}) async-start(bf16[8,64,3584]{2,1,0:T(8,128)(2,1)} %pad_maximum_fusion.3), calls=%async_computation | async-start | bytes 7340032 | tf_op jit(solution)/shard_map/all_to_all | solution.py:1353
  137.0 7.9 copy-start.35
  137.0 7.8 copy-start.36
  137.0 7.8 copy-start.37
  144.9 21.8 %copy-start.8 = (f32[12,256]{1,0:T(8,128)}, f32[12,256]{1,0:T(8,128)S(1)}, u32[]{:S(2)}) copy-start(f32[12,256]{1,0:T(8,128)S(1)} %maximum_convert_fusion.taps_ref) | copy-start | bytes 36868
  145.8 20.8 %copy-start.6 = (bf16[32,64,64]{2,1,0:T(8,128)(2,1)}, bf16[32,64,64]{2,1,0:T(8,128)(2,1)S(1)}, u32[]{:S(2)}) copy-start(bf16[32,64,64]{2,1,0:T(8,128)(2,1)S(1)} %and_convert_fusion.low_ref) | copy-start | bytes 786436
  147.4 16.7 %copy-start.22 = (bf16[768,2048]{1,0:T(8,128)(2,1)}, bf16[768,2048]{1,0:T(8,128)(2,1)S(1)}, u32[]{:S(2)}) copy-start(bf16[768,2048]{1,0:T(8,128)(2,1)S(1)} %constant_dynamic-update-slice_fusion) | copy-start | bytes 9437188
  200.0 217.2 %copy-start.10 = (bf16[32,2,64,64]{3,2,1,0:T(8,128)(2,1)}, bf16[32,2,64,64]{3,2,1,0:T(8,128)(2,1)S(1)}, u32[]{:S(2)}) copy-start(bf16[32,2,64,64]{3,2,1,0:T(8,128)(2,1)S(1)} %get-tuple-element.72.t_ref) | copy-start | bytes 1572868
  504.2 19.5 %copy-start.42 = (bf16[2048,768]{0,1:T(8,128)(2,1)S(1)}, bf16[2048,768]{0,1:T(8,128)(2,1)}, u32[]{:S(2)}) copy-start(bf16[2048,768]{0,1:T(8,128)(2,1)} %get-tuple-element.107) | copy-start | bytes 9437188
  523.6 10.4 copy-start.23
  740.2 7.3 copy-start.4
  740.2 7.3 copy-start.5
  740.3 7.3 copy-start.7
  740.3 7.3 copy-start.9
  740.3 7.3 copy-start.11
  740.3 7.3 copy-start.13
  740.3 40.2 %slice-start = ((s8[8388608]{0:T(1024)(128)(4,1)}), s8[4194304]{0:T(1024)(128)(4,1)S(1)}, s32[]{:S(2)}) async-start(s8[8388608]{0:T(1024)(128)(4,1)} %bitcast.99), calls=%async_computation.2 | async-start | bytes 8388608
  747.6 33.0 %slice-start.1 = ((s8[8388608]{0:T(1024)(128)(4,1)}), s8[4194304]{0:T(1024)(128)(4,1)S(1)}, s32[]{:S(2)}) async-start(s8[8388608]{0:T(1024)(128)(4,1)} %bitcast.99), calls=%async_computation.3 | async-start | bytes 8388608
  747.6 33.0 %copy-start.29 = (f32[1,2,8,128]{3,1,2,0:T(2,128)S(1)}, f32[1,2,8,128]{3,1,2,0:T(2,128)}, u32[]{:S(2)}) copy-start(f32[1,2,8,128]{3,1,2,0:T(2,128)} %copy-done.28) | copy-start | bytes 24580
  747.6 33.0 %copy-start.33 = (f32[8,256]{1,0:T(8,128)S(1)}, f32[8,256]{1,0:T(8,128)}, u32[]{:S(2)}) copy-start(f32[8,256]{1,0:T(8,128)} %copy-done.32) | copy-start | bytes 24580
  796.3 41.5 %all-to-all-start.1 = ((bf16[8,64,1536]{2,1,0:T(8,128)(2,1)}), bf16[8,64,1536]{2,1,0:T(8,128)(2,1)}, u32[]{:S(2)}, u32[]{:S(2)}) async-start(bf16[8,64,1536]{2,1,0:T(8,128)(2,1)} %get-tuple-element.77), calls=%async_computation.1 | async-start | bytes 3145728 | tf_op jit(solution)/shard_map/all_to_all | solution.py:1353
  800.8 7.0 copy-start.3
  837.8 110.9 %copy-start.16 = (bf16[256,2048]{1,0:T(8,128)(2,1)S(1)}, bf16[256,2048]{1,0:T(8,128)(2,1)}, u32[]{:S(2)}) copy-start(bf16[256,2048]{1,0:T(8,128)(2,1)} %refs_4_.1) | copy-start | bytes 3145732
  837.8 110.9 %copy-start.30 = (f32[256]{0:T(256)S(1)}, f32[256]{0:T(256)}, u32[]{:S(2)}) copy-start(f32[256]{0:T(256)} %get-tuple-element.130) | copy-start | bytes 3076
  (23 other events, 95.5 us)

commit v4 on v3

--- a/solution.py
+++ b/solution.py
@@ -100,6 +100,17 @@
 
 def in_place(view, sem):
     return pltpu.make_async_copy(view, view, sem)
+
+
+def staged(src, dst, held, sems):
+    load = pltpu.make_async_copy(src, held, sems.at[0])
+    save = pltpu.make_async_copy(held, dst, sems.at[1])
+
+    def turn():
+        load.wait()
+        save.start()
+
+    return load.start, turn, save.wait
 
 
 def gather_sems(axis, chunks):
@@ -404,13 +415,14 @@
         rows, width = block.shape
         shape = (rows, count * width) if beside else (count, rows, width)
         self.outputs = [(ANY, jax.ShapeDtypeStruct(shape, block.dtype))]
-        self.scratch = [DMA] + gather_sems(axis, chunks - turned)
+        self.scratch = [pltpu.VMEM(block.shape, block.dtype), DMA((2,))]
+        self.scratch += gather_sems(axis, chunks - turned)
         if turned:
             self.scratch += gather_sems(axis, 1)
 
     def steps(self, lines, ins, outs, scratch):
         line, (x_ref,), (out_ref,) = lines[self.axis], ins, outs
-        own_sem, *sems = scratch
+        held, own_sems, *sems = scratch
         rows, width = x_ref.shape[0] // self.chunks, x_ref.shape[1]
 
         def view(origin, part):
@@ -418,7 +430,7 @@
                 return out_ref.at[part, pl.ds(pl.multiple_of(origin * width, HD), width)]
             return out_ref.at[origin, part]
 
-        own = pltpu.make_async_copy(x_ref, view(line.me, pl.ds(0, x_ref.shape[0])), own_sem)
+        begin, turn, end = staged(x_ref, view(line.me, pl.ds(0, x_ref.shape[0])), held, own_sems)
 
         def part_steps(line, first, count, sems, start):
             def part(c):
@@ -439,7 +451,7 @@
         steps = part_steps(line, 0, straight, sems[:2], self.start)
         if self.turned:
             steps += part_steps(Turned(line), straight, 1, sems[2:], self.start + 0.9 * self.pace)
-        return [(self.start, own.start)] + steps + [(steps[-1][0], own.wait)]
+        return [(self.start, begin), (self.start + 0.95 * self.pace, turn)] + steps + [(steps[-1][0], end)]
 
 
 class Scatter:
@@ -577,13 +589,14 @@
         shards, part, width = block.shape
         shape = (shards, lax.axis_size("replica"), part, width)
         self.outputs = [(ANY, jax.ShapeDtypeStruct(shape, block.dtype))]
-        self.scratch = [DMA] + gather_sems("replica", shards)
+        self.scratch = [pltpu.VMEM(block.shape, block.dtype), DMA((2,))]
+        self.scratch += gather_sems("replica", shards)
 
     def steps(self, lines, ins, outs, scratch):
-        own_sem, *sems = scratch
+        held, own_sems, *sems = scratch
         (x_ref,), (out_ref,) = ins, outs
         copies = lines["replica"]
-        own = pltpu.make_async_copy(x_ref, out_ref.at[:, copies.me], own_sem)
+        begin, turn, end = staged(x_ref, out_ref.at[:, copies.me], held, own_sems)
         steps = gather_steps(
             copies,
             x_ref.shape[0],
@@ -594,7 +607,7 @@
             self.start,
             self.pace,
         )
-        return [(self.start, own.start)] + steps + [(steps[-1][0], own.wait)]
+        return [(self.start, begin), (self.start + 0.95 * self.pace, turn)] + steps + [(steps[-1][0], end)]
 
 
 class Sum:
@@ -1323,6 +1336,196 @@
     return low.astype(jnp.bfloat16), spread(place - start_at), spread(end_at - place)
 
 
+def exchange_beside(tasks, axes, ident, compute, grid, pace, operands, results, scratch, flops):
+    inputs, outputs, own_scratch, spans = layout_of(tasks)
+    counts = (len(inputs), len(operands), len(outputs), len(results), len(own_scratch), len(scratch))
+
+    def kernel(*refs):
+        groups, at = [], 0
+        for count in counts:
+            groups.append(refs[at : at + count])
+            at += count
+        task_ins, ins, task_outs, outs, task_scratch, rest = groups
+        steps = task_steps(tasks, spans, axes, task_ins, task_outs, task_scratch)
+        due = [min(max(int(when // pace), 0), grid) for when, _ in steps]
+        for i in range(grid):
+            if i in due:
+
+                @pl.when(pl.program_id(0) == i)
+                def _(i=i):
+                    for turn, (_, step) in zip(due, steps):
+                        if turn == i:
+                            step()
+
+        compute(*ins, *outs, *rest)
+
+        @pl.when(pl.program_id(0) == grid - 1)
+        def _():
+            for turn, (_, step) in zip(due, steps):
+                if turn == grid:
+                    step()
+
+    return pl.pallas_call(
+        kernel,
+        grid=(grid,),
+        in_specs=[ANY] * len(inputs) + [spec for _, spec in operands],
+        out_specs=[spec for spec, _ in outputs] + [spec for spec, _ in results],
+        out_shape=[shape for _, shape in outputs] + [shape for _, shape in results],
+        scratch_shapes=own_scratch + list(scratch),
+        compiler_params=pltpu.CompilerParams(
+            collective_id=ident, has_side_effects=True, vmem_limit_bytes=60 * 1024 * 1024
+        ),
+        cost_estimate=pl.CostEstimate(flops=flops, bytes_accessed=60 * 10**6, transcendentals=0),
+    )(*inputs, *[array for array, _ in operands])
+
+
+def feed_forward(
+    rows, window, zed_ref, source_ref, wo_ref, wi_ref, wd_ref, gain_ref,
+    hidden_ref, in_ref, product_ref, slopes_ref, out_ref, held,
+):
+    width = source_ref.shape[1]
+    wide = 512
+    squares = jnp.zeros((rows, 1), jnp.float32)
+    for n in range(0, width, wide):
+        cols = slice(n, n + wide)
+        part = source_ref[:, cols].astype(jnp.float32) + dot_nn(zed_ref[...], wo_ref[:, cols])
+        held[:, cols] = part
+        squares = squares + jnp.sum(part * part, axis=1, keepdims=True)
+    scale = lax.rsqrt(squares / width + 1e-6)
+    for n in range(0, width, wide):
+        cols = slice(n, n + wide)
+        in_ref[:, cols] = (held[:, cols] * scale * gain_ref[:, cols]).astype(in_ref.dtype)
+
+    @pl.when(pl.program_id(0) == lax.axis_index("shard"))
+    def _():
+        hidden_ref[...] = held[...]
+
+    wide = 256
+    for n in range(0, window, wide):
+        cols = slice(n, n + wide)
+        ups = slice(window + n, window + n + wide)
+        gate = dot_nn(in_ref[...], wi_ref[:, cols])
+        up = dot_nn(in_ref[...], wi_ref[:, ups])
+        s = sigmoid(gate)
+        silu = gate * s
+        product_ref[:, cols] = (silu * up).astype(product_ref.dtype)
+        slopes_ref[:, cols] = (up * s * (1.0 + gate * (1.0 - s))).astype(slopes_ref.dtype)
+        slopes_ref[:, ups] = silu.astype(slopes_ref.dtype)
+    wide = 512
+    for n in range(0, width, wide):
+        cols = slice(n, n + wide)
+        out_ref[:, cols] = dot_nn(product_ref[...], wd_ref[:, cols]).astype(out_ref.dtype)
+
+
+def feed_backward(window, dy_ref, slopes_ref, wi_ref, wd_ref, dlin_ref, dterm_ref):
+    width = dy_ref.shape[1]
+    wide = 256
+    for n in range(0, window, wide):
+        cols = slice(n, n + wide)
+        ups = slice(window + n, window + n + wide)
+        d_product = dot_nt(dy_ref[...], wd_ref[cols])
+        for part in (cols, ups):
+            slope = slopes_ref[:, part].astype(jnp.float32)
+            dlin_ref[:, part] = (d_product * slope).astype(dlin_ref.dtype)
+    wide = 512
+    for n in range(0, width, wide):
+        cols = slice(n, n + wide)
+        dterm_ref[:, cols] = dot_nt(dlin_ref[...], wi_ref[cols]).astype(dterm_ref.dtype)
+
+
+def whole(array):
+    return pl.BlockSpec(array.shape, lambda i: (0, 0), pipeline_mode=pl.Buffered(1))
+
+
+def run_feed_forward(tasks, axes, ident, zed, source, w_output, w_in, w_down, gain, rows):
+    tokens, width = source.shape
+    window = w_down.shape[0]
+
+    def token(columns):
+        return pl.BlockSpec((rows, columns), lambda i: (i, 0))
+
+    results = [(fixed((rows, width)), jax.ShapeDtypeStruct((rows, width), jnp.float32))]
+    for columns in (width, window, 2 * window, width):
+        results.append((token(columns), jax.ShapeDtypeStruct((tokens, columns), zed.dtype)))
+    return exchange_beside(
+        tasks,
+        axes,
+        ident,
+        functools.partial(feed_forward, rows, window),
+        tokens // rows,
+        6.0,
+        [(zed, token(width)), (source, token(width))]
+        + [(a, whole(a)) for a in (w_output, w_in, w_down, gain)],
+        results,
+        [pltpu.VMEM((rows, width), jnp.float32)],
+        90 * 10**9,
+    )
+
+
+def run_feed_backward(dy, slopes, w_in, w_down, rows):
+    tokens, width = dy.shape
+    window = w_down.shape[0]
+
+    def token(columns):
+        return pl.BlockSpec((rows, columns), lambda i: (i, 0))
+
+    columns = (2 * window, width)
+    return pl.pallas_call(
+        functools.partial(feed_backward, window),
+        grid=(tokens // rows,),
+        in_specs=[token(width), token(2 * window), whole(w_in), whole(w_down)],
+        out_specs=[token(c) for c in columns],
+        out_shape=[jax.ShapeDtypeStruct((tokens, c), dy.dtype) for c in columns],
+        compiler_params=pltpu.CompilerParams(vmem_limit_bytes=60 * 1024 * 1024),
+        cost_estimate=pl.CostEstimate(flops=30 * 10**9, bytes_accessed=40 * 10**6, transcendentals=0),
+    )(dy, slopes, w_in, w_down)
+
+
+def feed_gradients(in_ref, dlin_ref, product_ref, dy_ref, glin_ref, gdown_ref):
+    glin_ref[...] = dot_tn(in_ref[...], dlin_ref[...]).astype(glin_ref.dtype)
+    gdown_ref[...] = dot_tn(product_ref[...], dy_ref[...]).astype(gdown_ref.dtype)
+
+
+def run_feed_gradients(tasks, axes, ident, mlp_in, d_lin, product, dy):
+    tokens, width = mlp_in.shape
+    window = product.shape[1]
+    wide = 256
+    if tokens > 2048:
+        kind = mlp_in.dtype
+        return (
+            *exchange(tasks, axes, ident),
+            contract_rows(mlp_in, d_lin).astype(kind),
+            contract_rows(product, dy).astype(kind),
+        )
+
+    def columns(rows):
+        return pl.BlockSpec((rows, wide), lambda i: (0, i))
+
+    return exchange_beside(
+        tasks,
+        axes,
+        ident,
+        feed_gradients,
+        width // wide,
+        4.0,
+        [
+            (mlp_in, columns(tokens)),
+            (d_lin, whole(d_lin)),
+            (product, whole(product)),
+            (dy, columns(tokens)),
+        ],
+        [
+            (
+                pl.BlockSpec((wide, 2 * window), lambda i: (i, 0)),
+                jax.ShapeDtypeStruct((width, 2 * window), mlp_in.dtype),
+            ),
+            (columns(window), jax.ShapeDtypeStruct((window, width), mlp_in.dtype)),
+        ],
+        [],
+        90 * 10**9,
+    )
+
+
 def project(left_side, right_side):
     return jnp.dot(left_side, right_side, preferred_element_type=jnp.float32)
 
@@ -1480,52 +1683,51 @@
     low, off, rem = segment_masks(seq_lengths[0], seq_order[0], shards, rows)
 
     source = layer_input.astype(f32)
-    all_source = all_source.reshape(tokens, width).astype(f32)
-    normed = rms(all_source, full_attn_gain, 1e-6).astype(bf16)
+    all_source = all_source.reshape(tokens, width)
+    normed = rms(all_source.astype(f32), full_attn_gain, 1e-6).astype(bf16)
     projected = project(normed, attn_weights).reshape(shards, rows, -1)
     taps = jnp.concatenate([conv_query, conv_key, conv_value], axis=0).astype(f32)
     zed, mixed, sums, *saves = mixer_forward(projected, taps, head_row, low, off, rem, heads)
-    all_zed, mlp_weights, full_output, dy = exchange(
+    all_zed, mlp_weights, full_output = exchange(
         [
             Gather("shard", zed.reshape(tokens, own), 8, 0.0, 21.0, True, True),
             Trade(mlp_weights, 0.2, 31.0),
             Trade(full_output, 0.1, 42.0),
-            Gather("shard", out_cotangent, 8, 80.0, 21.0, turned=True),
         ],
         both,
         2,
     )
     zed = zed.reshape(tokens, own)
     mlp_weights = mlp_weights.reshape(width, 2 * ffn_window)
+    w_down = lax.dynamic_update_slice(jnp.zeros((ffn_window, width), bf16), w_down, (shift, 0))
+    dy, hidden, mlp_in, product, slopes, out_terms = run_feed_forward(
+        [Gather("shard", out_cotangent, 8, turned=True)],
+        group,
+        3,
+        all_zed,
+        all_source,
+        full_output.reshape(width, width),
+        mlp_weights,
+        w_down,
+        full_mlp_gain[None, :],
+        rows,
+    )
     dy = dy.reshape(tokens, width)
-    all_hidden = all_source + project(all_zed, full_output.reshape(width, width))
-    mlp_in = rms(all_hidden, full_mlp_gain, 1e-6).astype(bf16)
-    hidden = lax.dynamic_slice_in_dim(all_hidden, shard * rows, rows)
-    w_down = lax.dynamic_update_slice(jnp.zeros((ffn_window, width), bf16), w_down, (shift, 0))
-    lin = project(mlp_in, mlp_weights)
-    gate_lin, up_lin = lin[:, :ffn_window], lin[:, ffn_window:]
-    s = jax.nn.sigmoid(gate_lin)
-    product = (gate_lin * s * up_lin).astype(bf16)
-    d_product = times_t(dy, w_down)
-    d_gate = (d_product * up_lin * s * (1.0 + gate_lin * (1.0 - s))).astype(bf16)
-    d_up = (d_product * gate_lin * s).astype(bf16)
-    d_lin = jnp.concatenate([d_gate, d_up], axis=1)
-    g_down = contract_rows(product, dy).astype(bf16)
-    g_lin = contract_rows(mlp_in, d_lin).astype(bf16)
-    d_mlp_in, g_lin, g_down = exchange(
+    d_lin, d_terms = run_feed_backward(dy, slopes, mlp_weights, w_down, rows)
+    d_mlp_in, g_lin, g_down = run_feed_gradients(
+        [Scatter("shard", d_terms, 4)], group, 4, mlp_in, d_lin, product, dy
+    )
+    d_hidden_norm, g_mlp_rows = rms_back(hidden, full_mlp_gain, 1e-6, d_mlp_in)
+    d_hidden = out_cotangent.astype(f32) + d_hidden_norm
+
+    d_attn, g_lin, g_down = exchange(
         [
-            Scatter("shard", times_t(d_lin, mlp_weights).astype(bf16), 4),
+            Gather("shard", d_hidden.astype(bf16), 8, turned=True),
             Sum(g_lin, 0.5, 20.0),
             Total(g_down, 0.7, 16.0),
         ],
         both,
-        4,
-    )
-    d_hidden_norm, g_mlp_rows = rms_back(hidden, full_mlp_gain, 1e-6, d_mlp_in)
-    d_hidden = out_cotangent.astype(f32) + d_hidden_norm
-
-    (d_attn,) = exchange(
-        [Gather("shard", d_hidden.astype(bf16), 8, turned=True)], group, 5
+        5,
     )
     g_lin, d_attn = lax.optimization_barrier((g_lin, d_attn))
     g_lin = deal(g_lin)
@@ -1559,7 +1761,7 @@
     small = jnp.broadcast_to(small[:, None, :], (shards, 8, small.shape[1]))
     out_terms, g_proj, small, g_taps = exchange(
         [
-            Scatter("shard", project(product, w_down).astype(bf16), 4),
+            Scatter("shard", out_terms, 4),
             Deliver(g_proj, -0.4, 30.0, 24.0),
             Small(small, jnp.pad(g_taps, ((0, 16 - g_taps.shape[0]), (0, 0))), 50.0),
         ],

time: 1110 us -> 1040 us (0.937)
  matrix products: 187 us -> 61.7 us
  Pallas kernels: 805 us -> 863 us
    pallas_call x0 -> x3, Pallas kernels: none -> 226 us  [the longest x2 193 us: exchange_beside(): pl.pallas_call(kernel, grid=(grid,), in_specs=[ANY] * len(inputs) + [spec...]
    pallas_call x6 -> x5, Pallas kernels: 731 us -> 563 us  [exchange(): pl.pallas_call(kernel, in_specs=[ANY] * len(inputs), out_specs=[spec for...]
    dot_general x4 -> x1, matrix products: 72.1 us -> 15.6 us  [project(): return jnp.dot(left_side, right_side, preferred_element_type=jnp.float32)]
    dot_general x4 -> x2, matrix products: 60.9 us -> 22.8 us  [times_t(): lax.dot_general(left_side, right_side, (((1,), (1,)), ((), ())), preferre...]
    dot_general x4 -> x2, matrix products: 54.1 us -> 23.3 us  [contract_rows(): lax.dot_general(left_side, right_side, (((0,), (0,)), ((), ())), preferre...]
  transfers between devices with their start and end apart: 2 -> 2, of which waited for: 2 -> 2; matrix products, arithmetic and copies ran while one was open for 5% -> 6% of each run, Pallas kernels for 3% -> 3%
where the time goes in v4:
time: 1040 us; the launch traced here: 1020 us
  Pallas kernels  863 us (83%)
  matrix products  61.7 us (6%)
  other arithmetic  34.8 us (3%)
  local copies, waits for them, and re-layouts  34 us (3%)
  waiting for transfers between devices  20.5 us (2%)
    pallas_call x5, Pallas kernels, exchange(): pl.pallas_call(kernel, in_specs=[ANY] * len(inputs), out_specs=[spec for...  563 us
    pallas_call x2, Pallas kernels, exchange_beside(): pl.pallas_call(kernel, grid=(grid,), in_specs=[ANY] * len(inputs) + [spec...  193 us
    pallas_call x1, Pallas kernels, mixer_backward(): pl.pallas_call(functools.partial(delta_backward, lanes, heads, group), gr...  32.7 us
    pallas_call x1, Pallas kernels, run_feed_backward(): pl.pallas_call(functools.partial(feed_backward, window), grid=(tokens //...  32.5 us
    pallas_call x1, Pallas kernels, mixer_forward(): pl.pallas_call(functools.partial(delta_forward, lanes, heads, group), gri...  30.2 us
    dot_general x2, matrix products, contract_rows(): lax.dot_general(left_side, right_side, (((0,), (0,)), ((), ())), preferre...  23.3 us
    dot_general x2, matrix products, times_t(): lax.dot_general(left_side, right_side, (((1,), (1,)), ((), ())), preferre...  22.8 us
  transfers between devices with their start and end apart: 2, of which 2 were waited for; matrix products, arithmetic and copies ran while one was open for 6% of the time, Pallas kernels for 3%

profile of v4, /device:TPU:0, one launch (start us, length us, event | category | flops | bytes accessed | tf_op | source)
XLA Modules:
  0.0 1023.8 jit_solution(7363418394821328246)
XLA Ops:
  8.5 123.0 %shard_map.314 = (bf16[8,4,64,1024]{3,2,1,0:T(8,128)(2,1)}, bf16[8,256,2048]{2,1,0:T(8,128)(2,1)}, bf16[8,256,128]{2,1,0:T(8,128)(2,1)}) custom-call(bf16[256,2048]{1,0:T(8,128)(2,1)} %refs_0_.2, bf16[256,2048]{1,0:T(8,128)(2,1)} %refs_1_.1, bf16[256,2048]{1,0:T(8,128)(2,1)} %refs_2_.1, bf16[256,2048]{1,0:T(8,128)(2,1)} %refs_3_.1, ...), custom_call_target="tpu_custom_call" | custom-call | tf_op jit(solution)/shard_map/pallas_call | solution.py:878
  131.5 4.8 all-to-all-start
  136.7 5.1 fusion
  151.2 15.6 %fusion.5.proj_ref = f32[8,256,1152]{2,1,0:T(8,128)} fusion(bf16[8,256,2048]{2,1,0:T(8,128)(2,1)} %get-tuple-element.67, f32[2048]{0:T(1024)S(1)} %bitcast.106, f32[8,256]{1,0:T(8,128)S(1)} %add_rsqrt_fusion, bf16[2048,2]{1,0:T(8,128)(2,1)S(1)} %constant_dynamic-slice_fusion.2, bf16[2048,1024]{1,0:T(8,128)(2,1)S(1)} %bitcast.121), kind=kOutput, calls=%fused_computation.9 | convolution fusion | flops 9694609408 | bytes 22044672 | tf_op jit(solution)/shard_map/dot_general | solution.py:1530
  169.4 30.2 %shard_map.315 = (bf16[8,256,256]{2,1,0:T(8,128)(2,1)S(1)}, bf16[8,256,256]{2,1,0:T(8,128)(2,1)S(1)}, f32[8,256,768]{2,1,0:T(8,128)}, bf16[32,2,128,128]{3,2,1,0...) custom-call(f32[8,256,1152]{2,1,0:T(8,128)} %fusion.5.proj_ref, ...), custom_call_target="tpu_custom_call" | custom-call | flops 35000000512 | bytes 40000000 | tf_op jit(solution)/shard_map/pallas_call | solution.py:1253
  202.6 13.5 %all-to-all-done = bf16[8,64,3584]{2,1,0:T(8,128)(2,1)} async-done(((bf16[8,64,3584]{2,1,0:T(8,128)(2,1)}), bf16[8,64,3584]{2,1,0:T(8,128)(2,1)}, u32[]{:S(2)}, u32[]{:S(2)}) %all-to-all-start) | async-done | bytes 3670048 | tf_op jit(solution)/shard_map/all_to_all | solution.py:1556
  221.9 110.9 %shard_map.316 = (bf16[2048,2048]{1,0:T(8,128)(2,1)}, bf16[8,4,64,1536]{3,2,1,0:T(8,128)(2,1)}, bf16[8,4,64,2048]{3,2,1,0:T(8,128)(2,1)}) custom-call(bf16[2048,256]{1,0:T(8,128)(2,1)} %bitcast.90, bf16[8,64,1536]{2,1,0:T(8,128)(2,1)} %slice.112.refs_1_, bf16[8,64,2048]{2,1,0:T(8,128)(2,1)} %slice.113.refs_2_), custom_call_target="tpu_custom_call" | custom-call | tf_op jit(solution)/shard_map/pallas_call | solution.py:878
  332.8 95.5 %shard_map.317 = (bf16[8,256,2048]{2,1,0:T(8,128)(2,1)}, f32[256,2048]{1,0:T(8,128)}, bf16[2048,2048]{1,0:T(8,128)(2,1)}, bf16[2048,768]{1,0:T(8,128)(2,1)}, bf1...) custom-call(bf16[256,2048]{1,0:T(8,128)(2,1)} %refs_0_.3, bf16[2048,2048]{1,0:T(8,128)(2,1)} %get-tuple-element.72.refs_1_, ...), custom_call_target="tpu_custom_call" | custom-call | flops 89999998976 | bytes 60000000 | tf_op jit(solution)/shard_map/pallas_call | solution.py:1368
  430.1 32.5 %shard_map.318 = (bf16[2048,1536]{1,0:T(8,128)(2,1)}, bf16[2048,2048]{1,0:T(8,128)(2,1)}) custom-call(bf16[2048,2048]{1,0:T(8,128)(2,1)} %bitcast.124, bf16[2048,1536]{1,0:T(8,128)(2,1)} %get-tuple-element.80.slopes_ref, bf16[2048,1536]{1,0:T(8,128)(2,1)} %bitcast.120, bf16[768,2048]{1,0:T(8,128)(2,1)} %copy-done.25), custom_call_target="tpu_custom_call" | custom-call | flops 30000001024 | bytes 40000000 | tf_op jit(solution)/shard_map/pallas_call | solution.py:1473
  462.6 97.9 %shard_map.319 = (f32[256,2048]{1,0:T(8,128)}, bf16[2048,1536]{1,0:T(8,128)(2,1)}, bf16[768,2048]{1,0:T(8,128)(2,1)}) custom-call(bf16[8,4,64,2048]{3,2,1,0:T(8,128)(2,1)} %bitcast.126, bf16[2048,2048]{1,0:T(8,128)(2,1)} %get-tuple-element.82.refs_1_, bf16[2048,1536]{1,0:T(8,128)(2,1)} %get-tuple-element.83.refs_2_, ...), custom_call_target="tpu_custom_call" | custom-call | flops 89999998976 | bytes 60000000 | tf_op jit(solution)/shard_map/pallas_call | solution.py:1368
  563.9 3.5 fusion.37
  567.5 104.8 %shard_map.320 = (bf16[8,256,2048]{2,1,0:T(8,128)(2,1)}, bf16[8,64,1536]{2,1,0:T(8,128)(2,1)}, bf16[4,4,48,2048]{3,2,1,0:T(8,128)(2,1)}) custom-call(bf16[256,2048]{1,0:T(8,128)(2,1)} %get-tuple-element.123.refs_0_, bf16[8,4,64,1536]{3,2,1,0:T(8,128)(2,1)} %bitcast.97, bf16[4,4,48,2048]{3,2,1,0:T(8,128)(2,1)} %bitcast.102), custom_call_target="tpu_custom_call" | custom-call | tf_op jit(solution)/shard_map/pallas_call | solution.py:878
  672.4 7.2 fusion.21.dzed_ref
  679.7 32.7 %shard_map.321 = (bf16[8,256,1152]{2,1,0:T(8,128)(2,1)}, f32[12,256]{1,0:T(8,128)S(1)}, f32[1,128]{1,0:T(1,128)S(1)}) custom-call(f32[8,256,1152]{2,1,0:T(8,128)} %fusion.5.proj_ref, f32[8,256,768]{2,1,0:T(8,128)} %get-tuple-element.77.sums_ref, bf16[8,256,256]{2,1,0:T(8,128)(2,1)S(1)} %get-tuple-element.78.mixed_ref, f32[8,256,256]{2,1,0:T(8,128)} %fusion.21.dzed_ref, ...), custom_call_target="tpu_custom_call" | custom-call | flops 35000000512 | bytes 40000000 | tf_op jit(solution)/shard_map/pallas_call | solution.py:1283
  712.5 16.5 %bitcast_convert_fusion = bf16[2048,1152]{1,0:T(8,128)(2,1)} fusion(bf16[8,256,1152]{2,1,0:T(8,128)(2,1)} %get-tuple-element.96, bf16[8,256,2048]{2,1,0:T(8,128)(2,1)S(1)} %bitcast.93, f32[2048]{0:T(1024)S(1)} %bitcast.107, f32[8,256]{1,0:T(8,128)S(1)} %copy-done.36), kind=kOutput, calls=%fused_computation.6 | convolution fusion | flops 9682812928 | bytes 17842176 | tf_op jit(solution)/shard_map/dot_general | solution.py:1540
  729.0 3.6 all-to-all-start.1
  733.8 5.2 dynamic-slice_convert_fusion
  739.7 6.8 fusion.9
  746.5 15.5 %convolution_convert_fusion = bf16[2048,2048]{1,0:T(8,128)(2,1)} fusion(bf16[2048,1152]{1,0:T(8,128)(2,1)} %bitcast.127, bf16[2048,2]{1,0:T(8,128)(2,1)S(1)} %copy-done.29, bf16[2048,1024]{1,0:T(8,128)(2,1)S(1)} %bitcast.122), kind=kOutput, calls=%fused_computation.8 | convolution fusion | flops 9682026496 | bytes 17309696 | tf_op jit(solution)/shard_map/dot_general | solution.py:1534
  762.1 7.0 all-to-all-done.1
  770.2 111.1 %shard_map.322 = (f32[256,2048]{1,0:T(8,128)}, bf16[8,64,1152]{2,1,0:T(8,128)(2,1)}, bf16[4,4,16,2048]{3,2,1,0:T(8,128)(2,1)}, bf16[4,512,1536]{2,1,0:T(8,128)(2,1)}) custom-call(bf16[8,4,64,2048]{3,2,1,0:T(8,128)(2,1)} %bitcast.95, bf16[8,4,64,1152]{3,2,1,0:T(8,128)(2,1)} %bitcast.100, bf16[4,4,16,2048]{3,2,1,0:T(8,128)(2,1)} %bitcast.101, ...), custom_call_target="tpu_custom_call" | custom-call | tf_op jit(solution)/shard_map/pallas_call | solution.py:878
  884.3 113.1 %shard_map.323 = (f32[256,2048]{1,0:T(8,128)}, bf16[4,8,64,1152]{3,2,1,0:T(8,128)(2,1)}, f32[8,640]{1,0:T(8,128)}, f32[16,256]{1,0:T(8,128)}) custom-call(bf16[8,4,64,2048]{3,2,1,0:T(8,128)(2,1)} %bitcast.94, bf16[8,64,1152]{2,1,0:T(8,128)(2,1)} %get-tuple-element.98.refs_1_, f32[8,8,640]{2,1,0:T(8,128)} %broadcast_in_dim.88.refs_2_, f32[16,256]{1,0:T(8,128)} %pad.24.refs_3_), custom_call_target="tpu_custom_call" | custom-call | tf_op jit(solution)/shard_map/pallas_call | solution.py:878
  999.7 3.4 shard_map.324
  1006.7 7.7 shard_map.325
  (173 shorter events, 54.9 us)
Async XLA Ops:
  131.5 84.5 %all-to-all-start = ((bf16[8,64,3584]{2,1,0:T(8,128)(2,1)}), bf16[8,64,3584]{2,1,0:T(8,128)(2,1)}, u32[]{:S(2)}, u32[]{:S(2)}) async-start(bf16[8,64,3584]{2,1,0:T(8,128)(2,1)} %pad_maximum_fusion), calls=%async_computation | async-start | bytes 7340032 | tf_op jit(solution)/shard_map/all_to_all | solution.py:1556
  136.7 9.1 copy-start.38
  136.7 9.0 copy-start.39
  136.7 9.0 copy-start.40
  144.6 24.9 %copy-start.10 = (f32[1,128]{1,0:T(1,128)}, f32[1,128]{1,0:T(1,128)S(1)}, u32[]{:S(2)}) copy-start(f32[1,128]{1,0:T(1,128)S(1)} %reshape.313.gain_ref) | copy-start | bytes 1540
  145.8 23.6 %copy-start.8 = (f32[12,256]{1,0:T(8,128)}, f32[12,256]{1,0:T(8,128)S(1)}, u32[]{:S(2)}) copy-start(f32[12,256]{1,0:T(8,128)S(1)} %maximum_convert_fusion.taps_ref) | copy-start | bytes 36868
  146.8 22.7 %copy-start.6 = (bf16[32,64,64]{2,1,0:T(8,128)(2,1)}, bf16[32,64,64]{2,1,0:T(8,128)(2,1)S(1)}, u32[]{:S(2)}) copy-start(bf16[32,64,64]{2,1,0:T(8,128)(2,1)S(1)} %and_convert_fusion.low_ref) | copy-start | bytes 786436
  148.3 18.5 %copy-start.25 = (bf16[768,2048]{1,0:T(8,128)(2,1)}, bf16[768,2048]{1,0:T(8,128)(2,1)S(1)}, u32[]{:S(2)}) copy-start(bf16[768,2048]{1,0:T(8,128)(2,1)S(1)} %constant_dynamic-update-slice_fusion.refs_5_.wd_ref) | copy-start | bytes 9437188
  462.6 97.9 %copy-start.32 = (f32[1,2,8,128]{3,1,2,0:T(2,128)S(1)}, f32[1,2,8,128]{3,1,2,0:T(2,128)}, u32[]{:S(2)}) copy-start(f32[1,2,8,128]{3,1,2,0:T(2,128)} %copy.87) | copy-start | bytes 24580
  672.3 7.3 copy-start.4
  672.4 7.3 copy-start.5
  672.4 7.3 copy-start.7
  672.4 7.3 copy-start.9
  672.4 7.3 copy-start.11
  672.4 7.3 copy-start.13
  672.4 40.1 %slice-start = ((s8[8388608]{0:T(1024)(128)(4,1)}), s8[4194304]{0:T(1024)(128)(4,1)S(1)}, s32[]{:S(2)}) async-start(s8[8388608]{0:T(1024)(128)(4,1)} %bitcast.92), calls=%async_computation.2 | async-start | bytes 8388608
  679.7 32.8 %slice-start.1 = ((s8[8388608]{0:T(1024)(128)(4,1)}), s8[4194304]{0:T(1024)(128)(4,1)S(1)}, s32[]{:S(2)}) async-start(s8[8388608]{0:T(1024)(128)(4,1)} %bitcast.92), calls=%async_computation.3 | async-start | bytes 8388608
  679.7 32.8 %copy-start.31 = (f32[1,2,8,128]{3,1,2,0:T(2,128)S(1)}, f32[1,2,8,128]{3,1,2,0:T(2,128)}, u32[]{:S(2)}) copy-start(f32[1,2,8,128]{3,1,2,0:T(2,128)} %copy-done.30) | copy-start | bytes 24580
  679.7 32.8 %copy-start.36 = (f32[8,256]{1,0:T(8,128)S(1)}, f32[8,256]{1,0:T(8,128)}, u32[]{:S(2)}) copy-start(f32[8,256]{1,0:T(8,128)} %copy-done.35) | copy-start | bytes 24580
  729.0 40.1 %all-to-all-start.1 = ((bf16[8,64,1536]{2,1,0:T(8,128)(2,1)}), bf16[8,64,1536]{2,1,0:T(8,128)(2,1)S(1)}, u32[]{:S(2)}, u32[]{:S(2)}) async-start(bf16[8,64,1536]{2,1,0:T(8,128)(2,1)} %get-tuple-element.97), calls=%async_computation.1 | async-start | bytes 3145728 | tf_op jit(solution)/shard_map/all_to_all | solution.py:1556
  739.7 6.9 copy-start.43
  770.2 111.2 %copy-start.18 = (bf16[256,2048]{1,0:T(8,128)(2,1)S(1)}, bf16[256,2048]{1,0:T(8,128)(2,1)}, u32[]{:S(2)}) copy-start(bf16[256,2048]{1,0:T(8,128)(2,1)} %refs_4_.1) | copy-start | bytes 3145732
  770.2 111.2 %copy-start.33 = (f32[256]{0:T(256)S(1)}, f32[256]{0:T(256)}, u32[]{:S(2)}) copy-start(f32[256]{0:T(256)} %get-tuple-element.147) | copy-start | bytes 3076
  1006.7 10.0 copy-start.16
  (25 other events, 99.5 us)

commit v5 on v4

--- a/solution.py
+++ b/solution.py
@@ -233,7 +233,16 @@
 BIG = 64
 
 
-def scatter_steps(line, chunks, block, piece, scratch, store, done, start, pace):
+def far_first(count, at):
+    order = []
+    for k in range(count - 1):
+        order += [place for place, here in ((count - 1 - k, count - 1 - k > at), (k, k < at)) if here]
+    return order + [at]
+
+
+def scatter_steps(
+    line, chunks, block, piece, scratch, store, done, start, pace, launches=None, lag=0.0
+):
     mine, from_x, from_z, load_sem, xs_sem, xr_sem, zs_sem, zr_sem = scratch
     Z, X, z, x = line.Z, line.X, line.z, line.x
     exists = line.exists
@@ -393,15 +402,31 @@
                 def _(zz=zz, c=c):
                     z_copy(True, zz, c).wait_send()
 
-    steps = [(start, begin)]
+    tables = []
+    for at in range(Z):
+        tables.append(far_first(Z, at))
+
+    def visited(i):
+        return sum(jnp.where(z == at, tables[at][i], 0) for at in range(Z))
+
+    def launch(i):
+        if i < Z:
+            x_line(visited(i))
+        else:
+            load(visited(i - Z), x).start()
+
+    if launches is not None:
+        launches.append((visited, launch))
+    steps = [] if launches is not None else [(start, begin)]
     for k in range(Z - 1):
         for c in range(chunks):
             steps.append(
                 (start + pace * (k + (c + 1) / chunks), functools.partial(pass_on, k, c))
             )
     for c in range(chunks):
-        steps.append((start + pace * (Z - 1 + (c + 1) / chunks), functools.partial(settle, c)))
-    steps.append((start + pace * (Z + 2), finish))
+        when = start + lag + pace * (Z - 1 + (c + 1) / chunks)
+        steps.append((when, functools.partial(settle, c)))
+    steps.append((start + lag + pace * (Z + 2), finish))
     return steps
 
 
@@ -501,6 +526,48 @@
         return steps
 
 
+class Computed(Scatter):
+    def __init__(self, axis, rows, width, kind, chunks, start=0.0, pace=21.0):
+        self.axis, self.chunks, self.start, self.pace = axis, chunks, start, pace
+        self.everyone, self.inputs = (), []
+        dims = grid_of(axis)
+        count = dims[0] * dims[1]
+        self.outputs = [(VMEM, jax.ShapeDtypeStruct((rows, width), jnp.float32))]
+        self.scratch = [pltpu.VMEM((count, chunks, rows // chunks, width), kind)]
+        self.scratch += scatter_scratch(dims, chunks, rows // chunks, width, kind)
+
+    def steps(self, lines, ins, outs, scratch):
+        terms, *rest = scratch
+        (out_ref,) = outs
+        line = lines[self.axis]
+        rows = terms.shape[2]
+        launches = []
+
+        def store(c, part, total):
+            out_ref[pl.ds(pl.multiple_of(c * rows + part.start, STEP), part.size)] = total
+
+        steps = scatter_steps(
+            line,
+            self.chunks,
+            lambda slot: terms.at[slot],
+            lambda slot, c: terms.at[slot, c],
+            rest,
+            store,
+            lambda c: None,
+            self.start,
+            self.pace,
+            launches,
+        )
+        visited, self.launch = launches[0]
+
+        def slot(i):
+            other = i < line.Z
+            return line.slot(visited(i % line.Z), 1 - line.x if other else line.x)
+
+        self.slot, self.terms = slot, terms
+        return steps
+
+
 class Spread:
     def __init__(self, weights, window, first, start=0.0, pace=6.0):
         self.inputs = list(weights)
@@ -576,46 +643,49 @@
             ready,
             sems,
             self.start + 2 * self.pace,
-            self.pace,
+            2 * self.pace,
         )
         return [(self.start, begin)] + steps + [(steps[-1][0], finish)]
 
 
 class Trade:
-    def __init__(self, block, start=0.0, pace=6.0):
+    def __init__(self, block, first, width, start=0.0, pace=6.0):
         self.inputs = [block]
-        self.start, self.pace = start, pace
+        self.first, self.width, self.start, self.pace = first, width, start, pace
         self.everyone = ()
-        shards, part, width = block.shape
+        shards, part, _ = block.shape
         shape = (shards, lax.axis_size("replica"), part, width)
         self.outputs = [(ANY, jax.ShapeDtypeStruct(shape, block.dtype))]
-        self.scratch = [pltpu.VMEM(block.shape, block.dtype), DMA((2,))]
+        self.scratch = [pltpu.VMEM((shards, part, width), block.dtype), DMA((2,))]
         self.scratch += gather_sems("replica", shards)
 
     def steps(self, lines, ins, outs, scratch):
         held, own_sems, *sems = scratch
         (x_ref,), (out_ref,) = ins, outs
         copies = lines["replica"]
-        begin, turn, end = staged(x_ref, out_ref.at[:, copies.me], held, own_sems)
+        cols = pl.ds(self.first, self.width)
+        begin, turn, end = staged(
+            x_ref.at[:, :, cols], out_ref.at[:, copies.me], held, own_sems
+        )
         steps = gather_steps(
             copies,
             x_ref.shape[0],
             lambda origin, c: out_ref.at[c, origin],
-            lambda c: x_ref.at[c],
+            lambda c: x_ref.at[c, :, cols],
             lambda c: None,
             sems,
             self.start,
             self.pace,
         )
-        return [(self.start, begin), (self.start + 0.95 * self.pace, turn)] + steps + [(steps[-1][0], end)]
+        return [(self.start, begin), (self.start + 3.0, turn)] + steps + [(steps[-1][0], end)]
 
 
 class Sum:
-    def __init__(self, terms, start=0.0, pace=6.0):
+    def __init__(self, terms, start=0.0, pace=6.0, lag=0.0):
         shards, replicas = lax.axis_size("shard"), lax.axis_size("replica")
         part, wide = terms.shape[0] // shards // replicas, terms.shape[1]
         self.inputs = [terms.reshape(shards, replicas, part, wide)]
-        self.start, self.pace = start, pace
+        self.start, self.pace, self.lag = start, pace, lag
         self.everyone = ()
         self.outputs = [(VMEM, jax.ShapeDtypeStruct((shards, part, wide), terms.dtype))]
         self.scratch = scatter_scratch(grid_of("replica"), shards, part, wide, terms.dtype)
@@ -636,6 +706,7 @@
             lambda c: None,
             self.start,
             self.pace,
+            lag=self.lag,
         )
 
 
@@ -698,13 +769,14 @@
 
 
 class Total:
-    def __init__(self, terms, start=0.0, pace=6.0):
+    def __init__(self, terms, start=0.0, pace=6.0, again=60.0, lag=0.0):
         replicas = lax.axis_size("replica")
         share, wide = terms.shape[0] // replicas, terms.shape[1]
         chunks = max(n for n in (1, 2, 3, 4) if share % (n * STEP) == 0)
         rows = share // chunks
         self.inputs = [terms.reshape(replicas, chunks, rows, wide)]
-        self.start, self.pace, self.chunks = start, pace, chunks
+        self.start, self.pace, self.again, self.chunks = start, pace, again, chunks
+        self.lag = lag
         self.everyone = ()
         kind = terms.dtype
         self.outputs = [(ANY, jax.ShapeDtypeStruct((replicas, chunks, rows, wide), kind))]
@@ -739,6 +811,7 @@
             lambda c: own(c).start(),
             self.start,
             self.pace,
+            lag=self.lag,
         )
         sharing = gather_steps(
             copies,
@@ -747,7 +820,7 @@
             lambda c: total_ref.at[c],
             lambda c: None,
             scratch[2:4],
-            self.start + self.pace * (copies.Z + 2),
+            self.again,
             self.pace,
         )
         return summing + sharing + [(sharing[-1][0], finish)]
@@ -1379,6 +1452,63 @@
     )(*inputs, *[array for array, _ in operands])
 
 
+def exchange_computed(task, tasks, axes, ident, fill, compute, grid, pace, operands, results, flops):
+    slots = lax.axis_size(task.axis)
+    everything = [task] + tasks
+    inputs, outputs, own_scratch, spans = layout_of(everything)
+    counts = (len(inputs), len(operands), len(outputs), len(results), len(own_scratch))
+
+    def kernel(*refs):
+        groups, at = [], 0
+        for count in counts:
+            groups.append(refs[at : at + count])
+            at += count
+        task_ins, ins, task_outs, outs, task_scratch = groups
+        steps = task_steps(everything, spans, axes, task_ins, task_outs, task_scratch)
+        due = [min(max(int(when // pace), 0), grid + slots) for when, _ in steps]
+        now = pl.program_id(0)
+        for i in range(slots + grid):
+
+            @pl.when(now == i)
+            def _(i=i):
+                for turn, (_, step) in zip(due, steps):
+                    if turn == i:
+                        step()
+                if i < slots:
+                    fill(task.slot(i), task.terms, *ins, *outs)
+                    task.launch(i)
+                else:
+                    compute(*ins, *outs)
+
+        @pl.when(now == slots + grid - 1)
+        def _():
+            for turn, (_, step) in zip(due, steps):
+                if turn == slots + grid:
+                    step()
+
+    return pl.pallas_call(
+        kernel,
+        grid=(slots + grid,),
+        in_specs=[ANY] * len(inputs) + [spec for _, spec in operands],
+        out_specs=[spec for spec, _ in outputs] + [spec for spec, _ in results],
+        out_shape=[shape for _, shape in outputs] + [shape for _, shape in results],
+        scratch_shapes=own_scratch,
+        compiler_params=pltpu.CompilerParams(
+            collective_id=ident, has_side_effects=True, vmem_limit_bytes=60 * 1024 * 1024
+        ),
+        cost_estimate=pl.CostEstimate(flops=flops, bytes_accessed=60 * 10**6, transcendentals=0),
+    )(*inputs, *[array for array, _ in operands])
+
+
+def fill_input_terms(slot, terms, proj_ref, weights_ref):
+    chunks, rows, width = terms.shape[1:]
+    own = proj_ref[pl.ds(pl.multiple_of(slot * chunks * rows, chunks * rows), chunks * rows)]
+    wide = 512
+    for n in range(0, width, wide):
+        part = dot_nt(own, weights_ref[n : n + wide])
+        terms[slot, :, :, n : n + wide] = part.reshape(chunks, rows, wide).astype(terms.dtype)
+
+
 def feed_forward(
     rows, window, zed_ref, source_ref, wo_ref, wi_ref, wd_ref, gain_ref,
     hidden_ref, in_ref, product_ref, slopes_ref, out_ref, held,
@@ -1644,7 +1774,7 @@
     little = jnp.pad(little, ((0, 0), (0, HD - little.shape[1])))
     attn_weights, all_source, little = exchange(
         [
-            Spread((w_query, w_key, w_value, w_outgate), col_window, col_first, -0.5, 12.0),
+            Spread((w_query, w_key, w_value, w_outgate), col_window, col_first, -0.5, 13.0),
             Gather("shard", layer_input, 8, turned=True),
             Gather("shard", little, 1, 0.0, 20.0),
         ],
@@ -1678,8 +1808,6 @@
     later_weights = jnp.concatenate([mlp_weights, full_output], axis=2)
     later_weights, all_source = lax.optimization_barrier((later_weights, all_source))
     later_weights = deal(later_weights)
-    mlp_weights = later_weights[..., : 2 * ffn_window]
-    full_output = later_weights[..., 2 * ffn_window :]
     low, off, rem = segment_masks(seq_lengths[0], seq_order[0], shards, rows)
 
     source = layer_input.astype(f32)
@@ -1691,8 +1819,8 @@
     all_zed, mlp_weights, full_output = exchange(
         [
             Gather("shard", zed.reshape(tokens, own), 8, 0.0, 21.0, True, True),
-            Trade(mlp_weights, 0.2, 31.0),
-            Trade(full_output, 0.1, 42.0),
+            Trade(later_weights, 0, 2 * ffn_window, 0.2, 76.0),
+            Trade(later_weights, 2 * ffn_window, width, 0.1, 76.0),
         ],
         both,
         2,
@@ -1723,8 +1851,8 @@
     d_attn, g_lin, g_down = exchange(
         [
             Gather("shard", d_hidden.astype(bf16), 8, turned=True),
-            Sum(g_lin, 0.5, 20.0),
-            Total(g_down, 0.7, 16.0),
+            Sum(g_lin, 0.5, 26.0),
+            Total(g_down, 0.1, 10.0, 62.0),
         ],
         both,
         5,
@@ -1739,16 +1867,30 @@
     )
     d_proj = d_proj.reshape(tokens, -1)
     g_proj = contract_rows(normed, d_proj).astype(bf16)
-    d_normed, g_proj, g_output, g_lin = exchange(
-        [
-            Scatter("shard", times_t(d_proj, attn_weights).astype(bf16), 4),
-            Sum(g_proj, 0.5, 16.0),
-            Total(g_output, 0.7, 14.0),
-            Gather("replica", g_lin.reshape(-1, 2 * ffn_window), 4, 0.3, 31.0),
-        ],
-        both,
-        6,
-    )
+    beside = [
+        Sum(g_proj, 0.1, 10.0, 20.0),
+        Total(g_output, 0.05, 6.0, 70.0, 12.0),
+        Gather("replica", g_lin.reshape(-1, 2 * ffn_window), 4, 20.0, 46.0),
+    ]
+    if grid_of("shard")[1] == 2:
+        d_normed, g_proj, g_output, g_lin = exchange_computed(
+            Computed("shard", rows, width, bf16, 4, 12.0),
+            beside,
+            both,
+            6,
+            fill_input_terms,
+            None,
+            0,
+            2.0,
+            [(d_proj, whole(d_proj)), (attn_weights, whole(attn_weights))],
+            [],
+            90 * 10**9,
+        )
+    else:
+        d_terms = times_t(d_proj, attn_weights).astype(bf16)
+        d_normed, g_proj, g_output, g_lin = exchange(
+            [Scatter("shard", d_terms, 4)] + beside, both, 6
+        )
     d_source, g_attn_rows = rms_back(source, full_attn_gain, 1e-6, d_normed)
 
     def dealt(values):
@@ -1762,7 +1904,7 @@
     out_terms, g_proj, small, g_taps = exchange(
         [
             Scatter("shard", out_terms, 4),
-            Deliver(g_proj, -0.4, 30.0, 24.0),
+            Deliver(g_proj, -0.4, 60.0, 24.0),
             Small(small, jnp.pad(g_taps, ((0, 16 - g_taps.shape[0]), (0, 0))), 50.0),
         ],
         both,

time: 1040 us -> 1010 us (0.971)
  matrix products: 61.7 us -> 40.7 us
  waiting for transfers between devices: 20.5 us -> 6.37 us
    pallas_call x0 -> x1, Pallas kernels: none -> 108 us  [exchange_computed(): pl.pallas_call(kernel, grid=(slots + grid,), in_specs=[ANY] * len(inputs)...]
    pallas_call x5 -> x4, Pallas kernels: 563 us -> 462 us  [exchange(): pl.pallas_call(kernel, in_specs=[ANY] * len(inputs), out_specs=[spec for...]
    dot_general x2 -> x1, matrix products: 22.8 us -> 7.09 us  [times_t(): lax.dot_general(left_side, right_side, (((1,), (1,)), ((), ())), preferre...]
    all_to_all x2, waiting for transfers between devices: 20.5 us -> 6.37 us  [deal(): lax.all_to_all(stacked, 'shard', split_axis=0, concat_axis=0, tiled=True)]
  transfers between devices with their start and end apart: 2 -> 2, of which waited for: 2 -> 1; matrix products, arithmetic and copies ran while one was open for 6% -> 6% of each run, Pallas kernels for 3% -> 6%
where the time goes in v5:
time: 1010 us; the launch traced here: 1000 us
  Pallas kernels  870 us (86%)
  matrix products  40.7 us (4%)
  other arithmetic  35.9 us (4%)
  local copies, waits for them, and re-layouts  35.3 us (3%)
  starting transfers between devices  12.4 us (1%)
    pallas_call x4, Pallas kernels, exchange(): pl.pallas_call(kernel, in_specs=[ANY] * len(inputs), out_specs=[spec for...  462 us
    pallas_call x2, Pallas kernels, exchange_beside(): pl.pallas_call(kernel, grid=(grid,), in_specs=[ANY] * len(inputs) + [spec...  194 us
    pallas_call x1, Pallas kernels, exchange_computed(): pl.pallas_call(kernel, grid=(slots + grid,), in_specs=[ANY] * len(inputs)...  108 us
    pallas_call x1, Pallas kernels, mixer_backward(): pl.pallas_call(functools.partial(delta_backward, lanes, heads, group), gr...  32.6 us
    pallas_call x1, Pallas kernels, run_feed_backward(): pl.pallas_call(functools.partial(feed_backward, window), grid=(tokens //...  32.5 us
    pallas_call x1, Pallas kernels, mixer_forward(): pl.pallas_call(functools.partial(delta_forward, lanes, heads, group), gri...  30.2 us
    dot_general x2, matrix products, contract_rows(): lax.dot_general(left_side, right_side, (((0,), (0,)), ((), ())), preferre...  20.2 us
  transfers between devices with their start and end apart: 2, of which 1 were waited for; matrix products, arithmetic and copies ran while one was open for 6% of the time, Pallas kernels for 6%

profile of v5, /device:TPU:0, one launch (start us, length us, event | category | flops | bytes accessed | tf_op | source)
XLA Modules:
  0.0 1002.0 jit_solution(13536640384938595754)
XLA Ops:
  8.5 118.8 %shard_map.314 = (bf16[8,4,64,1024]{3,2,1,0:T(8,128)(2,1)}, bf16[8,256,2048]{2,1,0:T(8,128)(2,1)}, bf16[8,256,128]{2,1,0:T(8,128)(2,1)}) custom-call(bf16[256,2048]{1,0:T(8,128)(2,1)} %refs_0_.2, bf16[256,2048]{1,0:T(8,128)(2,1)} %refs_1_.1, bf16[256,2048]{1,0:T(8,128)(2,1)} %refs_2_.1, bf16[256,2048]{1,0:T(8,128)(2,1)} %refs_3_.1, ...), custom_call_target="tpu_custom_call" | custom-call | tf_op jit(solution)/shard_map/pallas_call | solution.py:951
  127.3 7.5 all-to-all-start
  135.2 5.1 fusion
  149.9 2.9 fusion.7.refs_4_
  154.6 13.4 %fusion.5.proj_ref = f32[8,256,1152]{2,1,0:T(8,128)} fusion(bf16[8,256,2048]{2,1,0:T(8,128)(2,1)S(1)} %bitcast.91, f32[2048]{0:T(1024)S(1)} %bitcast.105, f32[8,256]{1,0:T(8,128)S(1)} %add_rsqrt_fusion, bf16[2048,2]{1,0:T(8,128)(2,1)S(1)} %constant_dynamic-slice_fusion.2, bf16[2048,1024]{1,0:T(8,128)(2,1)S(1)} %bitcast.99), kind=kOutput, calls=%fused_computation.8 | convolution fusion | flops 9694609408 | bytes 22044672 | tf_op jit(solution)/shard_map/dot_general | solution.py:1660
  170.6 30.2 %shard_map.315 = (bf16[8,256,256]{2,1,0:T(8,128)(2,1)S(1)}, bf16[8,256,256]{2,1,0:T(8,128)(2,1)S(1)}, f32[8,256,768]{2,1,0:T(8,128)}, bf16[32,2,128,128]{3,2,1,0...) custom-call(f32[8,256,1152]{2,1,0:T(8,128)} %fusion.5.proj_ref, ...), custom_call_target="tpu_custom_call" | custom-call | flops 35000000512 | bytes 40000000 | tf_op jit(solution)/shard_map/pallas_call | solution.py:1326
  205.8 6.4 all-to-all-done.refs_1_.refs_2_
  212.1 105.9 %shard_map.316 = (bf16[2048,2048]{1,0:T(8,128)(2,1)}, bf16[8,4,64,1536]{3,2,1,0:T(8,128)(2,1)}, bf16[8,4,64,2048]{3,2,1,0:T(8,128)(2,1)}) custom-call(bf16[2048,256]{1,0:T(8,128)(2,1)} %bitcast.88, bf16[8,64,3584]{2,1,0:T(8,128)(2,1)} %all-to-all-done.refs_1_.refs_2_, bf16[8,64,3584]{2,1,0:T(8,128)(2,1)} %all-to-all-done.refs_1_.refs_2_), custom_call_target="tpu_custom_call" | custom-call | tf_op jit(solution)/shard_map/pallas_call | solution.py:951
  318.1 97.2 %shard_map.317 = (bf16[8,256,2048]{2,1,0:T(8,128)(2,1)}, f32[256,2048]{1,0:T(8,128)}, bf16[2048,2048]{1,0:T(8,128)(2,1)}, bf16[2048,768]{1,0:T(8,128)(2,1)}, bf1...) custom-call(bf16[256,2048]{1,0:T(8,128)(2,1)} %refs_0_.3, bf16[2048,2048]{1,0:T(8,128)(2,1)} %get-tuple-element.72.refs_1_, ...), custom_call_target="tpu_custom_call" | custom-call | flops 89999998976 | bytes 60000000 | tf_op jit(solution)/shard_map/pallas_call | solution.py:1441
  417.1 32.5 %shard_map.318 = (bf16[2048,1536]{1,0:T(8,128)(2,1)}, bf16[2048,2048]{1,0:T(8,128)(2,1)}) custom-call(bf16[2048,2048]{1,0:T(8,128)(2,1)} %bitcast.121, bf16[2048,1536]{1,0:T(8,128)(2,1)} %get-tuple-element.80.slopes_ref, bf16[2048,1536]{1,0:T(8,128)(2,1)} %bitcast.119, bf16[768,2048]{1,0:T(8,128)(2,1)} %constant_dynamic-update-slice_fusion.refs_5_.wd_ref), custom_call_target="tpu_custom_call" | custom-call | flops 30000001024 | bytes 40000000 | tf_op jit(solution)/shard_map/pallas_call | solution.py:1603
  449.6 96.5 %shard_map.319 = (f32[256,2048]{1,0:T(8,128)}, bf16[2048,1536]{1,0:T(8,128)(2,1)}, bf16[768,2048]{1,0:T(8,128)(2,1)}) custom-call(bf16[8,4,64,2048]{3,2,1,0:T(8,128)(2,1)} %bitcast.123, bf16[2048,2048]{1,0:T(8,128)(2,1)} %get-tuple-element.82.refs_1_, bf16[2048,1536]{1,0:T(8,128)(2,1)} %get-tuple-element.83.refs_2_, ...), custom_call_target="tpu_custom_call" | custom-call | flops 89999998976 | bytes 60000000 | tf_op jit(solution)/shard_map/pallas_call | solution.py:1441
  550.9 109.7 %shard_map.320 = (bf16[8,256,2048]{2,1,0:T(8,128)(2,1)}, bf16[8,64,1536]{2,1,0:T(8,128)(2,1)}, bf16[4,4,48,2048]{3,2,1,0:T(8,128)(2,1)}) custom-call(bf16[256,2048]{1,0:T(8,128)(2,1)} %get-tuple-element.123.refs_0_, bf16[8,4,64,1536]{3,2,1,0:T(8,128)(2,1)} %bitcast.96, bf16[4,4,48,2048]{3,2,1,0:T(8,128)(2,1)} %bitcast.100), custom_call_target="tpu_custom_call" | custom-call | tf_op jit(solution)/shard_map/pallas_call | solution.py:951
  660.7 7.1 fusion.19.dzed_ref
  667.8 4.9 all-to-all-start.1
  677.4 32.6 %shard_map.321 = (bf16[8,256,1152]{2,1,0:T(8,128)(2,1)}, f32[12,256]{1,0:T(8,128)S(1)}, f32[1,128]{1,0:T(1,128)S(1)}) custom-call(f32[8,256,1152]{2,1,0:T(8,128)} %fusion.5.proj_ref, f32[8,256,768]{2,1,0:T(8,128)} %get-tuple-element.77.sums_ref, bf16[8,256,256]{2,1,0:T(8,128)(2,1)S(1)} %copy-done.13, f32[8,256,256]{2,1,0:T(8,128)} %fusion.19.dzed_ref, ...), custom_call_target="tpu_custom_call" | custom-call | flops 35000000512 | bytes 40000000 | tf_op jit(solution)/shard_map/pallas_call | solution.py:1356
  711.2 5.3 dynamic-slice_convert_fusion
  717.1 6.8 fusion.9
  724.0 13.4 %bitcast_convert_fusion = bf16[2048,1152]{1,0:T(8,128)(2,1)} fusion(bf16[8,256,1152]{2,1,0:T(8,128)(2,1)S(1)} %copy-done.45, bf16[8,256,2048]{2,1,0:T(8,128)(2,1)S(1)} %bitcast.93, f32[2048]{0:T(1024)S(1)} %bitcast.106, f32[8,256]{1,0:T(8,128)S(1)} %copy-done.38), kind=kOutput, calls=%fused_computation.6 | convolution fusion | flops 9682812928 | bytes 17842176 | tf_op jit(solution)/shard_map/dot_general | solution.py:1670
  737.4 108.0 %shard_map.322 = (f32[256,2048]{1,0:T(8,128)}, bf16[8,64,1152]{2,1,0:T(8,128)(2,1)}, bf16[4,4,16,2048]{3,2,1,0:T(8,128)(2,1)}, bf16[4,512,1536]{2,1,0:T(8,128)(2,1)}) custom-call(bf16[8,4,64,1152]{3,2,1,0:T(8,128)(2,1)} %bitcast.125, bf16[4,4,16,2048]{3,2,1,0:T(8,128)(2,1)} %bitcast.102, bf16[512,1536]{1,0:T(8,128)(2,1)} %bitcast.29.refs_2_, ...), custom_call_target="tpu_custom_call" | custom-call | flops 89999998976 | bytes 60000000 | tf_op jit(solution)/shard_map/pallas_call | solution.py:1489
  848.3 127.2 %shard_map.323 = (f32[256,2048]{1,0:T(8,128)}, bf16[4,8,64,1152]{3,2,1,0:T(8,128)(2,1)}, f32[8,640]{1,0:T(8,128)}, f32[16,256]{1,0:T(8,128)}) custom-call(bf16[8,4,64,2048]{3,2,1,0:T(8,128)(2,1)} %bitcast.94, bf16[8,64,1152]{2,1,0:T(8,128)(2,1)} %get-tuple-element.98.refs_1_, f32[8,8,640]{2,1,0:T(8,128)} %broadcast_in_dim.88.refs_2_, f32[16,256]{1,0:T(8,128)} %pad.24.refs_3_), custom_call_target="tpu_custom_call" | custom-call | tf_op jit(solution)/shard_map/pallas_call | solution.py:951
  975.6 2.3 copy-done.1
  977.9 3.4 shard_map.324
  984.9 7.7 shard_map.325
  994.9 2.9 add_convert_fusion
  (178 shorter events, 52.6 us)
Async XLA Ops:
  127.3 7.6 copy-start.21
  127.3 84.8 %all-to-all-start = ((bf16[8,64,3584]{2,1,0:T(8,128)(2,1)}), bf16[8,64,3584]{2,1,0:T(8,128)(2,1)}, u32[]{:S(2)}, u32[]{:S(2)}) async-start(bf16[8,64,3584]{2,1,0:T(8,128)(2,1)} %pad_maximum_fusion), calls=%async_computation | async-start | bytes 7340032 | tf_op jit(solution)/shard_map/all_to_all | solution.py:1686
  135.2 5.2 copy-start.27
  135.2 5.9 copy-start.43
  135.2 6.1 copy-start.44
  140.4 12.4 %copy-start.37 = (f32[8,256]{1,0:T(8,128)}, f32[8,256]{1,0:T(8,128)S(1)}, u32[]{:S(2)}) copy-start(f32[8,256]{1,0:T(8,128)S(1)} %add_rsqrt_fusion) | copy-start | bytes 24580
  143.7 26.9 %copy-start.6 = (bf16[32,64,64]{2,1,0:T(8,128)(2,1)}, bf16[32,64,64]{2,1,0:T(8,128)(2,1)S(1)}, u32[]{:S(2)}) copy-start(bf16[32,64,64]{2,1,0:T(8,128)(2,1)S(1)} %and_convert_fusion.low_ref) | copy-start | bytes 786436
  143.9 8.9 copy-start.32
  144.0 26.6 %copy-start.10 = (f32[1,128]{1,0:T(1,128)}, f32[1,128]{1,0:T(1,128)S(1)}, u32[]{:S(2)}) copy-start(f32[1,128]{1,0:T(1,128)S(1)} %reshape.309.gain_ref) | copy-start | bytes 1540
  145.2 25.4 %copy-start.8 = (f32[12,256]{1,0:T(8,128)}, f32[12,256]{1,0:T(8,128)S(1)}, u32[]{:S(2)}) copy-start(f32[12,256]{1,0:T(8,128)S(1)} %maximum_convert_fusion.taps_ref) | copy-start | bytes 36868
  449.6 96.6 %copy-start.19 = (f32[256,2048]{1,0:T(8,128)S(1)}, f32[256,2048]{1,0:T(8,128)}, u32[]{:S(2)}) copy-start(f32[256,2048]{1,0:T(8,128)} %get-tuple-element.75) | copy-start | bytes 6291460
  449.6 96.6 %copy-start.34 = (f32[1,2,8,128]{3,1,2,0:T(2,128)S(1)}, f32[1,2,8,128]{3,1,2,0:T(2,128)}, u32[]{:S(2)}) copy-start(f32[1,2,8,128]{3,1,2,0:T(2,128)} %copy.87) | copy-start | bytes 24580
  667.8 4.9 copy-start.11
  667.8 69.7 %all-to-all-start.1 = ((bf16[8,64,1536]{2,1,0:T(8,128)(2,1)}), bf16[8,64,1536]{2,1,0:T(8,128)(2,1)}, u32[]{:S(2)}, u32[]{:S(2)}) async-start(bf16[8,64,1536]{2,1,0:T(8,128)(2,1)} %get-tuple-element.97), calls=%async_computation.1 | async-start | bytes 3145728 | tf_op jit(solution)/shard_map/all_to_all | solution.py:1686
  711.2 5.9 copy-start.3
  711.2 12.8 %slice-start.2 = ((s8[8388608]{0:T(1024)(128)(4,1)}), s8[4194304]{0:T(1024)(128)(4,1)S(1)}, s32[]{:S(2)}) async-start(s8[8388608]{0:T(1024)(128)(4,1)} %bitcast.92), calls=%async_computation.4 | async-start | bytes 8388608
  717.1 6.9 slice-start.3
  717.1 6.9 copy-start.33
  717.1 6.9 copy-start.38
  717.1 6.9 copy-start.45
  737.4 108.0 %copy-start.22 = (bf16[256,2048]{1,0:T(8,128)(2,1)S(1)}, bf16[256,2048]{1,0:T(8,128)(2,1)}, u32[]{:S(2)}) copy-start(bf16[256,2048]{1,0:T(8,128)(2,1)} %refs_4_.1) | copy-start | bytes 3145732
  737.4 108.0 %copy-start.35 = (f32[256]{0:T(256)S(1)}, f32[256]{0:T(256)}, u32[]{:S(2)}) copy-start(f32[256]{0:T(256)} %get-tuple-element.147) | copy-start | bytes 3076
  984.9 10.0 copy-start.20
  994.9 5.2 copy-start.25
  (28 other events, 80.5 us)

commit v6 on v5

--- a/solution.py
+++ b/solution.py
@@ -1860,7 +1860,6 @@
     g_lin, d_attn = lax.optimization_barrier((g_lin, d_attn))
     g_lin = deal(g_lin)
     d_attn = d_attn.reshape(tokens, width)
-    g_output = contract_rows(zed, d_attn).astype(bf16)
     d_zed = times_t(d_attn, w_output).reshape(shards, rows, own)
     d_proj, g_taps, g_head = mixer_backward(
         projected, sums, mixed, d_zed, taps, head_row, low, off, rem, saves, heads
@@ -1869,11 +1868,10 @@
     g_proj = contract_rows(normed, d_proj).astype(bf16)
     beside = [
         Sum(g_proj, 0.1, 10.0, 20.0),
-        Total(g_output, 0.05, 6.0, 70.0, 12.0),
         Gather("replica", g_lin.reshape(-1, 2 * ffn_window), 4, 20.0, 46.0),
     ]
     if grid_of("shard")[1] == 2:
-        d_normed, g_proj, g_output, g_lin = exchange_computed(
+        d_normed, g_proj, g_lin = exchange_computed(
             Computed("shard", rows, width, bf16, 4, 12.0),
             beside,
             both,
@@ -1888,9 +1886,13 @@
         )
     else:
         d_terms = times_t(d_proj, attn_weights).astype(bf16)
-        d_normed, g_proj, g_output, g_lin = exchange(
+        d_normed, g_proj, g_lin = exchange(
             [Scatter("shard", d_terms, 4)] + beside, both, 6
         )
+
+    g_proj = deal(g_proj)
+    d_attn, d_normed = lax.optimization_barrier((d_attn, d_normed))
+    g_output = contract_rows(zed, d_attn).astype(bf16)
     d_source, g_attn_rows = rms_back(source, full_attn_gain, 1e-6, d_normed)
 
     def dealt(values):
@@ -1901,15 +1903,17 @@
     )
     small = jnp.pad(small, ((0, 0), (0, -small.shape[1] % HD)))
     small = jnp.broadcast_to(small[:, None, :], (shards, 8, small.shape[1]))
-    out_terms, g_proj, small, g_taps = exchange(
+    out_terms, g_proj, g_output, small, g_taps = exchange(
         [
             Scatter("shard", out_terms, 4),
-            Deliver(g_proj, -0.4, 60.0, 24.0),
+            Gather("replica", g_proj.reshape(-1, 4 * own + HD), 4, 0.3, 34.0),
+            Total(g_output, 0.1, 8.0, 70.0, 25.0),
             Small(small, jnp.pad(g_taps, ((0, 16 - g_taps.shape[0]), (0, 0))), 50.0),
         ],
         both,
         7,
     )
+    g_proj = g_proj.reshape(replicas, shards, -1, 4 * own + HD)
     g_lin = g_lin.reshape(replicas, shards, -1, 2 * ffn_window)
     g_query, g_key, g_value, g_outgate = widen(g_proj, 4, width, col_window, col_first)
     g_gate, g_up = widen(g_lin, 2, ffn, ffn_window, ffn_first)

time: 1010 us -> 989 us (0.979)
  Pallas kernels: 870 us -> 841 us
    pallas_call x4, Pallas kernels: 462 us -> 434 us  [exchange(): pl.pallas_call(kernel, in_specs=[ANY] * len(inputs), out_specs=[spec for...]
  transfers between devices with their start and end apart: 2 -> 3, of which waited for: 1 -> 2; matrix products, arithmetic and copies ran while one was open for 6% -> 7% of each run, Pallas kernels for 6% -> 7%
where the time goes in v6:
time: 989 us; the launch traced here: 984 us
  Pallas kernels  841 us (85%)
  matrix products  44.2 us (4%)
  other arithmetic  36.2 us (4%)
  local copies, waits for them, and re-layouts  35.6 us (4%)
  starting transfers between devices  16.5 us (2%)
    pallas_call x4, Pallas kernels, exchange(): pl.pallas_call(kernel, in_specs=[ANY] * len(inputs), out_specs=[spec for...  434 us
    pallas_call x2, Pallas kernels, exchange_beside(): pl.pallas_call(kernel, grid=(grid,), in_specs=[ANY] * len(inputs) + [spec...  194 us
    pallas_call x1, Pallas kernels, exchange_computed(): pl.pallas_call(kernel, grid=(slots + grid,), in_specs=[ANY] * len(inputs)...  106 us
    pallas_call x1, Pallas kernels, mixer_backward(): pl.pallas_call(functools.partial(delta_backward, lanes, heads, group), gr...  32.7 us
    pallas_call x1, Pallas kernels, run_feed_backward(): pl.pallas_call(functools.partial(feed_backward, window), grid=(tokens //...  32.5 us
    pallas_call x1, Pallas kernels, mixer_forward(): pl.pallas_call(functools.partial(delta_forward, lanes, heads, group), gri...  30.2 us
    dot_general x2, matrix products, contract_rows(): lax.dot_general(left_side, right_side, (((0,), (0,)), ((), ())), preferre...  23.7 us
  transfers between devices with their start and end apart: 3, of which 2 were waited for; matrix products, arithmetic and copies ran while one was open for 7% of the time, Pallas kernels for 7%

profile of v6, /device:TPU:0, one launch (start us, length us, event | category | flops | bytes accessed | tf_op | source)
XLA Modules:
  0.0 983.7 jit_solution(7104526449161068593)
XLA Ops:
  8.5 118.8 %shard_map.314 = (bf16[8,4,64,1024]{3,2,1,0:T(8,128)(2,1)}, bf16[8,256,2048]{2,1,0:T(8,128)(2,1)}, bf16[8,256,128]{2,1,0:T(8,128)(2,1)}) custom-call(bf16[256,2048]{1,0:T(8,128)(2,1)} %refs_0_.2, bf16[256,2048]{1,0:T(8,128)(2,1)} %refs_1_.1, bf16[256,2048]{1,0:T(8,128)(2,1)} %refs_2_.1, bf16[256,2048]{1,0:T(8,128)(2,1)} %refs_3_.1, ...), custom_call_target="tpu_custom_call" | custom-call | tf_op jit(solution)/shard_map/pallas_call | solution.py:951
  127.3 7.5 all-to-all-start
  135.2 5.1 fusion
  149.9 2.9 fusion.7.refs_3_
  154.6 13.4 %fusion.5.proj_ref = f32[8,256,1152]{2,1,0:T(8,128)} fusion(bf16[8,256,2048]{2,1,0:T(8,128)(2,1)S(1)} %bitcast.94, f32[2048]{0:T(1024)S(1)} %bitcast.107, f32[8,256]{1,0:T(8,128)S(1)} %add_rsqrt_fusion, bf16[2048,2]{1,0:T(8,128)(2,1)S(1)} %constant_dynamic-slice_fusion.2, bf16[2048,1024]{1,0:T(8,128)(2,1)S(1)} %bitcast.101), kind=kOutput, calls=%fused_computation.8 | convolution fusion | flops 9694609408 | bytes 22044672 | tf_op jit(solution)/shard_map/dot_general | solution.py:1660
  170.6 30.2 %shard_map.315 = (bf16[8,256,256]{2,1,0:T(8,128)(2,1)S(1)}, bf16[8,256,256]{2,1,0:T(8,128)(2,1)S(1)}, f32[8,256,768]{2,1,0:T(8,128)}, bf16[32,2,128,128]{3,2,1,0...) custom-call(f32[8,256,1152]{2,1,0:T(8,128)} %fusion.5.proj_ref, ...), custom_call_target="tpu_custom_call" | custom-call | flops 35000000512 | bytes 40000000 | tf_op jit(solution)/shard_map/pallas_call | solution.py:1326
  205.7 6.4 all-to-all-done.refs_1_.refs_2_
  212.1 105.9 %shard_map.316 = (bf16[2048,2048]{1,0:T(8,128)(2,1)}, bf16[8,4,64,1536]{3,2,1,0:T(8,128)(2,1)}, bf16[8,4,64,2048]{3,2,1,0:T(8,128)(2,1)}) custom-call(bf16[2048,256]{1,0:T(8,128)(2,1)} %bitcast.87, bf16[8,64,3584]{2,1,0:T(8,128)(2,1)} %all-to-all-done.refs_1_.refs_2_, bf16[8,64,3584]{2,1,0:T(8,128)(2,1)} %all-to-all-done.refs_1_.refs_2_), custom_call_target="tpu_custom_call" | custom-call | tf_op jit(solution)/shard_map/pallas_call | solution.py:951
  318.1 97.1 %shard_map.317 = (bf16[8,256,2048]{2,1,0:T(8,128)(2,1)}, f32[256,2048]{1,0:T(8,128)}, bf16[2048,2048]{1,0:T(8,128)(2,1)}, bf16[2048,768]{1,0:T(8,128)(2,1)}, bf1...) custom-call(bf16[256,2048]{1,0:T(8,128)(2,1)} %refs_0_.3, bf16[2048,2048]{1,0:T(8,128)(2,1)} %get-tuple-element.74.refs_1_, ...), custom_call_target="tpu_custom_call" | custom-call | flops 89999998976 | bytes 60000000 | tf_op jit(solution)/shard_map/pallas_call | solution.py:1441
  417.0 32.5 %shard_map.318 = (bf16[2048,1536]{1,0:T(8,128)(2,1)}, bf16[2048,2048]{1,0:T(8,128)(2,1)}) custom-call(bf16[2048,2048]{1,0:T(8,128)(2,1)} %bitcast.123, bf16[2048,1536]{1,0:T(8,128)(2,1)} %get-tuple-element.82.slopes_ref, bf16[2048,1536]{1,0:T(8,128)(2,1)} %bitcast.121, bf16[768,2048]{1,0:T(8,128)(2,1)} %constant_dynamic-update-slice_fusion.refs_5_.wd_ref), custom_call_target="tpu_custom_call" | custom-call | flops 30000001024 | bytes 40000000 | tf_op jit(solution)/shard_map/pallas_call | solution.py:1603
  449.5 96.6 %shard_map.319 = (f32[256,2048]{1,0:T(8,128)}, bf16[2048,1536]{1,0:T(8,128)(2,1)}, bf16[768,2048]{1,0:T(8,128)(2,1)}) custom-call(bf16[8,4,64,2048]{3,2,1,0:T(8,128)(2,1)} %bitcast.125, bf16[2048,2048]{1,0:T(8,128)(2,1)} %get-tuple-element.84.refs_1_, bf16[2048,1536]{1,0:T(8,128)(2,1)} %get-tuple-element.85.refs_2_, ...), custom_call_target="tpu_custom_call" | custom-call | flops 89999998976 | bytes 60000000 | tf_op jit(solution)/shard_map/pallas_call | solution.py:1441
  546.2 2.9 multiply_reduce_fusion
  551.4 109.7 %shard_map.320 = (bf16[8,256,2048]{2,1,0:T(8,128)(2,1)}, bf16[8,64,1536]{2,1,0:T(8,128)(2,1)}, bf16[4,4,48,2048]{3,2,1,0:T(8,128)(2,1)}) custom-call(bf16[256,2048]{1,0:T(8,128)(2,1)} %get-tuple-element.127.refs_0_, bf16[8,4,64,1536]{3,2,1,0:T(8,128)(2,1)} %bitcast.97, bf16[4,4,48,2048]{3,2,1,0:T(8,128)(2,1)} %bitcast.103), custom_call_target="tpu_custom_call" | custom-call | tf_op jit(solution)/shard_map/pallas_call | solution.py:951
  661.1 7.1 fusion.18.dzed_ref
  668.2 4.4 all-to-all-start.1
  677.4 32.7 %shard_map.321 = (bf16[8,256,1152]{2,1,0:T(8,128)(2,1)}, f32[12,256]{1,0:T(8,128)S(1)}, f32[1,128]{1,0:T(1,128)S(1)}) custom-call(f32[8,256,1152]{2,1,0:T(8,128)} %fusion.5.proj_ref, f32[8,256,768]{2,1,0:T(8,128)} %get-tuple-element.79.sums_ref, bf16[8,256,256]{2,1,0:T(8,128)(2,1)S(1)} %copy-done.13, f32[8,256,256]{2,1,0:T(8,128)} %fusion.18.dzed_ref, ...), custom_call_target="tpu_custom_call" | custom-call | flops 35000000512 | bytes 40000000 | tf_op jit(solution)/shard_map/pallas_call | solution.py:1356
  710.0 17.0 %bitcast_convert_fusion = bf16[2048,1152]{1,0:T(8,128)(2,1)} fusion(bf16[8,256,1152]{2,1,0:T(8,128)(2,1)} %get-tuple-element.98, bf16[8,256,2048]{2,1,0:T(8,128)(2,1)} %get-tuple-element.69, f32[2048]{0:T(1024)S(1)} %bitcast.108, f32[8,256]{1,0:T(8,128)S(1)} %copy-done.39), kind=kOutput, calls=%fused_computation.6 | convolution fusion | flops 9682812928 | bytes 17842176 | tf_op jit(solution)/shard_map/dot_general | solution.py:1670
  727.1 105.8 %shard_map.322 = (f32[256,2048]{1,0:T(8,128)}, bf16[8,64,1152]{2,1,0:T(8,128)(2,1)}, bf16[4,512,1536]{2,1,0:T(8,128)(2,1)}) custom-call(bf16[8,4,64,1152]{3,2,1,0:T(8,128)(2,1)} %bitcast.127, bf16[512,1536]{1,0:T(8,128)(2,1)} %bitcast.27.refs_1_, bf16[2048,1152]{1,0:T(8,128)(2,1)} %bitcast.126, bf16[2048,1152]{1,0:T(8,128)(2,1)} %fusion.7.refs_3_), custom_call_target="tpu_custom_call" | custom-call | flops 89999998976 | bytes 60000000 | tf_op jit(solution)/shard_map/pallas_call | solution.py:1489
  832.9 4.6 all-to-all-start.2
  837.5 5.2 dynamic-slice_convert_fusion
  846.8 8.3 shard_map.325
  856.8 6.7 convolution_convert_fusion
  866.8 100.0 %shard_map.323 = (f32[256,2048]{1,0:T(8,128)}, bf16[4,512,1152]{2,1,0:T(8,128)(2,1)}, bf16[4,4,16,2048]{3,2,1,0:T(8,128)(2,1)}, f32[8,640]{1,0:T(8,128)}, f32[16,256]{1,0:T(8,128)}) custom-call(bf16[8,4,64,2048]{3,2,1,0:T(8,128)(2,1)} %bitcast.95, bf16[512,1152]{1,0:T(8,128)(2,1)} %bitcast.99, bf16[4,4,16,2048]{3,2,1,0:T(8,128)(2,1)} %bitcast.102, ...), custom_call_target="tpu_custom_call" | custom-call | tf_op jit(solution)/shard_map/pallas_call | solution.py:951
  969.1 3.4 shard_map.324
  (175 shorter events, 57.8 us)
Async XLA Ops:
  127.3 7.6 copy-start.21
  127.3 84.8 %all-to-all-start = ((bf16[8,64,3584]{2,1,0:T(8,128)(2,1)}), bf16[8,64,3584]{2,1,0:T(8,128)(2,1)}, u32[]{:S(2)}, u32[]{:S(2)}) async-start(bf16[8,64,3584]{2,1,0:T(8,128)(2,1)} %pad_maximum_fusion), calls=%async_computation | async-start | bytes 7340032 | tf_op jit(solution)/shard_map/all_to_all | solution.py:1686
  135.2 5.2 copy-start.26
  135.2 5.9 copy-start.44
  135.2 6.1 copy-start.45
  140.4 12.4 %copy-start.38 = (f32[8,256]{1,0:T(8,128)}, f32[8,256]{1,0:T(8,128)S(1)}, u32[]{:S(2)}) copy-start(f32[8,256]{1,0:T(8,128)S(1)} %add_rsqrt_fusion) | copy-start | bytes 24580
  143.7 26.9 %copy-start.6 = (bf16[32,64,64]{2,1,0:T(8,128)(2,1)}, bf16[32,64,64]{2,1,0:T(8,128)(2,1)S(1)}, u32[]{:S(2)}) copy-start(bf16[32,64,64]{2,1,0:T(8,128)(2,1)S(1)} %and_convert_fusion.low_ref) | copy-start | bytes 786436
  143.9 8.9 copy-start.32
  144.0 26.6 %copy-start.10 = (f32[1,128]{1,0:T(1,128)}, f32[1,128]{1,0:T(1,128)S(1)}, u32[]{:S(2)}) copy-start(f32[1,128]{1,0:T(1,128)S(1)} %reshape.320.gain_ref) | copy-start | bytes 1540
  145.2 25.4 %copy-start.8 = (f32[12,256]{1,0:T(8,128)}, f32[12,256]{1,0:T(8,128)S(1)}, u32[]{:S(2)}) copy-start(f32[12,256]{1,0:T(8,128)S(1)} %maximum_convert_fusion.taps_ref) | copy-start | bytes 36868
  449.5 96.6 %copy-start.19 = (f32[256,2048]{1,0:T(8,128)S(1)}, f32[256,2048]{1,0:T(8,128)}, u32[]{:S(2)}) copy-start(f32[256,2048]{1,0:T(8,128)} %get-tuple-element.77) | copy-start | bytes 6291460
  449.5 96.6 %copy-start.34 = (f32[1,2,8,128]{3,1,2,0:T(2,128)S(1)}, f32[1,2,8,128]{3,1,2,0:T(2,128)}, u32[]{:S(2)}) copy-start(f32[1,2,8,128]{3,1,2,0:T(2,128)} %copy.81) | copy-start | bytes 24580
  668.2 58.9 %all-to-all-start.1 = ((bf16[8,64,1536]{2,1,0:T(8,128)(2,1)}), bf16[8,64,1536]{2,1,0:T(8,128)(2,1)}, u32[]{:S(2)}, u32[]{:S(2)}) async-start(bf16[8,64,1536]{2,1,0:T(8,128)(2,1)} %get-tuple-element.99), calls=%async_computation.1 | async-start | bytes 3145728 | tf_op jit(solution)/shard_map/all_to_all | solution.py:1686
  677.4 32.7 %copy-start.33 = (f32[1,2,8,128]{3,1,2,0:T(2,128)S(1)}, f32[1,2,8,128]{3,1,2,0:T(2,128)}, u32[]{:S(2)}) copy-start(f32[1,2,8,128]{3,1,2,0:T(2,128)} %copy-done.32) | copy-start | bytes 24580
  677.4 32.7 %copy-start.39 = (f32[8,256]{1,0:T(8,128)S(1)}, f32[8,256]{1,0:T(8,128)}, u32[]{:S(2)}) copy-start(f32[8,256]{1,0:T(8,128)} %copy-done.38) | copy-start | bytes 24580
  832.9 32.8 %all-to-all-start.2 = ((bf16[8,64,1152]{2,1,0:T(8,128)(2,1)}), bf16[8,64,1152]{2,1,0:T(8,128)(2,1)S(1)}, u32[]{:S(2)}, u32[]{:S(2)}) async-start(bf16[8,64,1152]{2,1,0:T(8,128)(2,1)} %get-tuple-element.100), calls=%async_computation.2 | async-start | bytes 2359296 | tf_op jit(solution)/shard_map/all_to_all | solution.py:1686
  837.4 6.5 copy-start.35
  837.4 7.1 copy-start.22
  837.5 7.1 copy-start.36
  846.8 8.4 copy-start.23
  846.8 8.4 copy-start.24
  846.8 8.4 copy-start.40
  969.1 7.0 copy-start.30
  972.6 7.5 copy-start.20
  (27 other events, 76.9 us)
